TPU v7x, 512 devices: a whole 4x8x8 slice. The times are simulated.
512 devices in a mesh: gx: 16 (over z, core), gy: 4 (over x), gz: 8 (over y).
Axes of the slice: x: 4, y: 8, z: 8, core: 2. Of those that a mesh axis runs over, the one named last changes fastest.
Arguments:
- velocity: float32 [3, 128, 64, 1024], P(None, 'gx', 'gy', 'gz'), may hold values from -6 to 6
- displacement: float32 [3, 128, 64, 1024], P(None, 'gx', 'gy', 'gz'), may hold values from -1.25 to 1.25
- mass: float32 [128, 64, 1024], P('gx', 'gy', 'gz'), may hold values from 0.5 to 2
- stress: float32 [6, 128, 64, 1024], P(None, 'gx', 'gy', 'gz'), may hold values from -3 to 3
- plastic: float32 [128, 64, 1024], P('gx', 'gy', 'gz'), may hold values from 0 to 0.5
- yield_stress: float32 [128, 64, 1024], P('gx', 'gy', 'gz'), may hold values from 0.5 to 3
- facet_anchor: float32 [16, 4, 8, 8, 3, 128], P('gx', 'gy', 'gz'), may hold values from 0 to 4
- facet_nodes: int32 [16, 4, 8, 8, 4, 128], P('gx', 'gy', 'gz'), may hold values from 0 to 16383
- pair_source: int32 [16, 4, 8, 256], P('gx', 'gy', 'gz'), may hold values from 0 to 7
- pair_dest: int32 [16, 4, 8, 256, 1], P('gx', 'gy', 'gz'), may hold values from 0 to 127; in each aligned block of 256 rows (0 to 255, 256 to 511, ..., all dimensions but the last counted through in order) at most 4 rows name the same one
- pair_target: int32 [16, 4, 8, 256], P('gx', 'gy', 'gz'), may hold values from 0 to 7
Outputs:
- velocity_new: float32 [3, 128, 64, 1024], P(None, 'gx', 'gy', 'gz')
- displacement_new: float32 [3, 128, 64, 1024], P(None, 'gx', 'gy', 'gz')
- stress_new: float32 [6, 128, 64, 1024], P(None, 'gx', 'gy', 'gz')
- plastic_new: float32 [128, 64, 1024], P('gx', 'gy', 'gz')
Inputs may be any that keep to these rules, and one draw needn't show every extreme that they name: `pair_dest`: within the pairs of one device, no partner index appears more than 4 times.
All inputs are finite; a program needn't handle non-finite values.
Results may differ from a plain program's by a relative error of at most 0.00022.
Values sent between devices are 32-bit elements; how exact they have to be, the bound alone decides.
No kernel may reach another device: no remote copies, remote signals or barrier semaphores. Data moves between devices by JAX's collectives and lax.ppermute only.
A program may use at most 64 MiB of HBM per device.

v0:
```python
import jax
import jax.numpy as jnp
from jax import lax
from jax.sharding import PartitionSpec as P

FACETS = 128


TIME_STEP = 0.25
SHEAR_MODULUS = 1.0
BULK_MODULUS = 2.0
HARDENING = 1.0
PENALTY = 1.0
REACH_SQUARED = 1.0
SLOT_GROUP = 32
CORNERS = ((0, 0, 0), (0, 0, 1), (0, 1, 0), (0, 1, 1), (1, 0, 0), (1, 0, 1), (1, 1, 0), (1, 1, 1))
VOIGT = ((0, 3, 5), (3, 1, 4), (5, 4, 2))


def padded_2(block, sides, width):
    for axis, dim in sides:
        count = lax.axis_size(axis)
        forward = [(i, i + 1) for i in range(count - 1)]
        backward = [(target, source) for source, target in forward]
        low = lax.ppermute(
            lax.slice_in_dim(block, block.shape[dim] - width, None, axis=dim), axis, forward
        )
        high = lax.ppermute(lax.slice_in_dim(block, 0, width, axis=dim), axis, backward)
        block = jnp.concatenate([low, block, high], axis=dim)
    return block


def passed_along(value, axis, steps):
    count = lax.axis_size(axis)
    initial, last = (max(0, -steps), min(count, count - steps))
    return lax.ppermute(value, axis, [(source, source + steps) for source in range(initial, last)])


def velocity_gradient(corner_velocity):
    grad_rows = []
    for component in range(3):
        grad_row = []
        for direction in range(3):
            summed = 0.0
            for corner, corner_values in zip(CORNERS, corner_velocity):
                summed = summed + (2.0 * corner[direction] - 1.0) * corner_values[component]
            grad_row.append(0.25 * summed)
        grad_rows.append(grad_row)
    return grad_rows


def radial_return(grad, stress, plastic, yield_stress):
    inc_normal = [TIME_STEP * grad[axis_id][axis_id] for axis_id in range(3)]
    inc_shear = [
        TIME_STEP * 0.5 * (grad[0][1] + grad[1][0]),
        TIME_STEP * 0.5 * (grad[1][2] + grad[2][1]),
        TIME_STEP * 0.5 * (grad[0][2] + grad[2][0]),
    ]
    volume_inc = inc_normal[0] + inc_normal[1] + inc_normal[2]
    trial_normal = [
        stress[axis_id]
        + 2.0 * SHEAR_MODULUS * (inc_normal[axis_id] - volume_inc / 3.0)
        + BULK_MODULUS * volume_inc
        for axis_id in range(3)
    ]
    trial_shear = [
        stress[3 + axis_id] + 2.0 * SHEAR_MODULUS * inc_shear[axis_id] for axis_id in range(3)
    ]
    mean_stress = (trial_normal[0] + trial_normal[1] + trial_normal[2]) / 3.0
    dev_normal = [trial_normal[axis_id] - mean_stress for axis_id in range(3)]
    square_sum = (
        dev_normal[0] * dev_normal[0]
        + dev_normal[1] * dev_normal[1]
        + dev_normal[2] * dev_normal[2]
    )
    square_sum = square_sum + 2.0 * (
        trial_shear[0] * trial_shear[0]
        + trial_shear[1] * trial_shear[1]
        + trial_shear[2] * trial_shear[2]
    )
    equivalent = jnp.sqrt(1.5 * square_sum)
    limit = yield_stress + HARDENING * plastic
    gamma = jnp.maximum(equivalent - limit, 0.0) / (3.0 * SHEAR_MODULUS + HARDENING)
    factor = 1.0 - 3.0 * SHEAR_MODULUS * gamma / jnp.maximum(equivalent, limit)
    components = [dev_normal[axis_id] * factor + mean_stress for axis_id in range(3)]
    components = components + [trial_shear[axis_id] * factor for axis_id in range(3)]
    return (jnp.stack(components), plastic + gamma)


def corner_force(stress_new, corner):
    forces = []
    for component in range(3):
        summed = 0.0
        for direction in range(3):
            summed = summed + stress_new[VOIGT[component][direction]] * (
                2.0 * corner[direction] - 1.0
            )
        forces.append(0.25 * summed)
    return jnp.stack(forces)


def contact_force(own_centroids, source_centroids):
    offset_vec = own_centroids[:, :, :, None] - source_centroids[:, :, None, :]
    distance_sq = jnp.sum(offset_vec * offset_vec, axis=1)
    weight = PENALTY * jnp.maximum(REACH_SQUARED - distance_sq, 0.0)
    return jnp.sum(weight[:, None, :, :] * offset_vec, axis=3)


def on_device(
    velocity,
    displacement,
    mass,
    stress,
    plastic,
    yield_stress,
    facet_anchor,
    facet_nodes,
    pair_source,
    pair_dest,
    pair_target,
):
    size_x, size_y, size_z = (velocity.shape[1], velocity.shape[2], velocity.shape[3])
    velocity_halo = padded_2(velocity, (("gx", 1), ("gy", 2), ("gz", 3)), 1)
    element_state = jnp.concatenate((stress, plastic[None], yield_stress[None]), axis=0)
    lower_x = passed_along(element_state[:, -1:], "gx", 1)
    element_state = jnp.concatenate((lower_x, element_state), axis=1)
    lower_y = passed_along(element_state[:, :, -1:], "gy", 1)
    element_state = jnp.concatenate((lower_y, element_state), axis=2)
    lower_z = passed_along(element_state[:, :, :, -1:], "gz", 1)
    element_state = jnp.concatenate((lower_z, element_state), axis=3)
    valid_x = (jnp.arange(size_x + 1, dtype=jnp.int32) > 0) | (lax.axis_index("gx") > 0)
    valid_y = (jnp.arange(size_y + 1, dtype=jnp.int32) > 0) | (lax.axis_index("gy") > 0)
    valid_z = (jnp.arange(size_z + 1, dtype=jnp.int32) > 0) | (lax.axis_index("gz") > 0)
    valid_mask = valid_x[:, None, None] & valid_y[None, :, None] & valid_z[None, None, :]
    yield_ext = jnp.where(valid_mask, element_state[7], 1.0)
    corner_velocity = [
        velocity_halo[
            :,
            corner[0] : corner[0] + size_x + 1,
            corner[1] : corner[1] + size_y + 1,
            corner[2] : corner[2] + size_z + 1,
        ]
        for corner in CORNERS
    ]
    grad = velocity_gradient(corner_velocity)
    stress_ext, plastic_ext = radial_return(grad, element_state[:6], element_state[6], yield_ext)
    internal = jnp.zeros((3, size_x, size_y, size_z), jnp.float32)
    for corner in CORNERS:
        element_force = jnp.where(valid_mask[None], corner_force(stress_ext, corner), 0.0)
        internal = (
            internal
            + element_force[
                :,
                1 - corner[0] : 1 - corner[0] + size_x,
                1 - corner[1] : 1 - corner[1] + size_y,
                1 - corner[2] : 1 - corner[2] + size_z,
            ]
        )
    stress_new = stress_ext[:, 1:, 1:, 1:]
    plastic_new = plastic_ext[1:, 1:, 1:]
    size_gx = lax.axis_size("gx")
    size_gz = lax.axis_size("gz")
    peer_count = size_gx * size_gz
    block_count = facet_anchor.shape[3]
    pair_count = pair_source.shape[3]
    capacity = max(2, 2 * pair_count // peer_count)
    node_total = size_x * size_y * size_z
    flat_disp = displacement.reshape(3, node_total)
    node_ids = facet_nodes.reshape(block_count, 4, FACETS)
    anchors = facet_anchor.reshape(block_count, 3, FACETS)
    picked = flat_disp[:, node_ids]
    centroids = anchors + 0.25 * jnp.transpose(jnp.sum(picked, axis=2), (1, 0, 2))
    source_ids = pair_source.reshape(pair_count)
    dest_ids = pair_dest.reshape(pair_count)
    target_ids = pair_target.reshape(pair_count)
    onehot = (dest_ids[:, None] == jnp.arange(peer_count, dtype=jnp.int32)[None, :]).astype(
        jnp.int32
    )
    slot_rank = jnp.sum((jnp.cumsum(onehot, axis=0) - onehot) * onehot, axis=1)
    slot_index = dest_ids * capacity + slot_rank
    send_data = (
        jnp.zeros((peer_count * capacity, 3, FACETS), jnp.float32)
        .at[slot_index]
        .set(centroids[source_ids])
    )
    send_target = jnp.full((peer_count * capacity,), -1, jnp.int32).at[slot_index].set(target_ids)
    send_data = send_data.reshape(peer_count, capacity, 3, FACETS)
    send_target = send_target.reshape(peer_count, capacity)
    received = lax.all_to_all(send_data, ("gx", "gz"), split_axis=0, concat_axis=0, tiled=True)
    targets = lax.all_to_all(send_target, ("gx", "gz"), split_axis=0, concat_axis=0, tiled=True)
    item_shape = targets.shape
    slot_count = item_shape[0] * item_shape[1]
    padded = -(-slot_count // SLOT_GROUP) * SLOT_GROUP
    flat_data = received.reshape(slot_count, 3, FACETS)
    flat_target = targets.reshape(slot_count)

    def one_group(group_items):
        group_data, group_target = group_items
        own_centroids = centroids[jnp.maximum(group_target, 0)]
        pushed_force = contact_force(own_centroids, group_data)
        return pushed_force * (group_target >= 0).astype(jnp.float32)[:, None, None]

    forces = lax.map(
        one_group,
        (flat_data.reshape(-1, SLOT_GROUP, 3, FACETS), flat_target.reshape(-1, SLOT_GROUP)),
    )
    forces = forces.reshape(padded, 3, FACETS)[:slot_count].reshape(
        item_shape[0], item_shape[1], 3, FACETS
    )
    pushed, targets = (forces, targets)
    flat_targets = targets.reshape(-1)
    selector = (flat_targets[:, None] == jnp.arange(block_count, dtype=jnp.int32)[None, :]).astype(
        jnp.float32
    )
    facet_force = jnp.dot(
        selector.T,
        pushed.reshape(-1, 3 * FACETS),
        precision=lax.Precision.HIGHEST,
        preferred_element_type=jnp.float32,
    )
    facet_force = facet_force.reshape(block_count, 3, FACETS)
    quarter_force = 0.25 * jnp.transpose(facet_force, (1, 0, 2))
    node_force = jnp.zeros((3, node_total), jnp.float32)
    for corner_slot in range(4):
        node_force = node_force.at[:, node_ids[:, corner_slot, :]].add(quarter_force)
    contact = node_force.reshape(3, size_x, size_y, size_z)
    velocity_new = velocity + TIME_STEP * (contact - internal) / mass
    displacement_new = displacement + TIME_STEP * velocity_new
    return (velocity_new, displacement_new, stress_new, plastic_new)


def solution(mesh):
    return jax.shard_map(
        on_device,
        mesh=mesh,
        in_specs=(
            P(None, "gx", "gy", "gz"),
            P(None, "gx", "gy", "gz"),
            P("gx", "gy", "gz"),
            P(None, "gx", "gy", "gz"),
            P("gx", "gy", "gz"),
            P("gx", "gy", "gz"),
            P("gx", "gy", "gz", None, None, None),
            P("gx", "gy", "gz", None, None, None),
            P("gx", "gy", "gz", None),
            P("gx", "gy", "gz", None, None),
            P("gx", "gy", "gz", None),
        ),
        out_specs=(
            P(None, "gx", "gy", "gz"),
            P(None, "gx", "gy", "gz"),
            P(None, "gx", "gy", "gz"),
            P("gx", "gy", "gz"),
        ),
        check_vma=False,
    )
```

profile of v0, /device:TPU:56, one launch (start us, length us, event | category | flops | bytes accessed | tf_op | source)
XLA Modules:
  0.0 341.4 jit_solution(2541700096581975904)
XLA Ops:
  5.6 16.7 %all-to-all-start = ((s32[128,1,4]{2,1,0:T(1,128)}), s32[128,1,4]{2,1,0:T(1,128)S(1)}, u32[]{:S(2)}, u32[]{:S(2)}) async-start(s32[128,1,4]{2,1,0:T(1,128)} %bitcast.16), calls=%async_computation | async-start | bytes 131072 | tf_op jit(solution)/shard_map/all_to_all | solution.py:190
  34.4 4.7 %copy.116 = f32[3,8,16,128]{0,3,2,1:T(8,128)} copy(f32[3,8,16,128]{3,2,1,0:T(8,128)S(1)} %copy-done.25) | data formatting | bytes 393216 | tf_op args[1]
  41.9 14.1 %gather_fusion.1 = f32[4096,3]{1,0:T(8,128)S(1)} fusion(f32[3,16384]{0,1:T(8,128)} %bitcast.440, s32[4096]{0:T(1024)S(1)} %broadcast_clamp_fusion), kind=kCustom, calls=%fused_computation.1 | custom fusion | bytes 114688 | tf_op jit(solution)/shard_map/gather | solution.py:171
  58.4 4.5 %collective-permute-start.5 = (f32[3,10,1,128]{3,2,1,0:T(1,128)S(1)}, f32[3,10,1,128]{3,2,1,0:T(1,128)S(1)}, u32[]{:S(2)}, u32[]{:S(2)}) collective-permute-start(f32[3,10,1,128]{3,2,1,0:T(1,128)S(1)} %get-tuple-element.114), channel_id=1, source_target_pairs={{0,8},{8,16},{16,24},{1,9},{9,17},{17,25},{2,10},{10,18},{18,26},{... | collective-permute-start | bytes 46088 | tf_op jit(solution)/shard_map/ppermute | solution.py:25
  63.2 7.4 %gather_fusion.2 = f32[256,3,128]{1,2,0:T(8,128)} fusion(f32[8,3,128]{1,2,0:T(8,128)S(1)} %bitcast_add_fusion, s32[1024]{0:T(1024)S(1)} %pad_clamp_fusion.1), kind=kCustom, calls=%fused_computation.2 | custom fusion | bytes 787456 | tf_op jit(solution)/shard_map/gather | solution.py:184
  70.6 9.4 %copy.117 = f32[256,3,128]{2,1,0:T(4,128)S(1)} copy(f32[256,3,128]{1,2,0:T(8,128)} %gather_fusion.2) | data formatting | bytes 786432 | tf_op jit(solution)/shard_map/gather | solution.py:184
  80.1 7.0 %scatter_fusion = f32[512,3,128]{2,1,0:T(4,128)S(1)} fusion(f32[512,3,128]{2,1,0:T(4,128)S(1)} %broadcast_in_dim.92, s32[256]{0:T(256)S(1)} %bitcast.474, f32[256,3,128]{2,1,0:T(4,128)S(1)} %copy.117), kind=kCustom, calls=%fused_computation.4 | custom fusion | bytes 1180672 | tf_op jit(solution)/shard_map/scatter | solution.py:184
  88.8 15.8 %all-to-all-start.1 = ((f32[128,4,3,128]{3,1,2,0:T(4,128)}), f32[128,4,3,128]{3,1,2,0:T(4,128)S(1)}, u32[]{:S(2)}, u32[]{:S(2)}) async-start(f32[128,4,3,128]{3,1,2,0:T(4,128)} %copy.119), calls=%async_computation.1 | async-start | bytes 1572864 | tf_op jit(solution)/shard_map/all_to_all | solution.py:189
  110.6 4.6 %collective-permute-start.8 = (f32[3,10,18,1]{3,2,1,0:T(8,128)S(1)}, f32[3,10,18,1]{3,2,1,0:T(8,128)S(1)}, u32[]{:S(2)}, u32[]{:S(2)}) collective-permute-start(f32[3,10,18,1]{3,2,1,0:T(8,128)S(1)} %get-tuple-element.111), channel_id=1, source_target_pairs={{1,0},{2,1},{3,2},{4,3},{5,4},{6,5},{7,6},{9,8},{10,9},{11,10},{12... | collective-permute-start | bytes 6488 | tf_op jit(solution)/shard_map/ppermute | solution.py:28
  119.5 11.8 %collective-permute-done.7 = f32[3,10,18,1]{3,2,1,0:T(8,128)S(1)} collective-permute-done((f32[3,10,18,1]{3,2,1,0:T(8,128)S(1)}, f32[3,10,18,1]{3,2,1,0:T(8,128)S(1)}, u32[]{:S(2)}, u32[]{:S(2)}) %collective-permute-start.7) | collective-permute-done | bytes 2192 | tf_op jit(solution)/shard_map/ppermute | solution.py:25
  151.4 133.3 %while.10 = (s32[]{:T(128)}, f32[16,32,3,128]{3,2,1,0:T(4,128)S(1)}, s32[16,32]{1,0:T(8,128)}, f32[8,3,128]{2,1,0:T(4,128)S(1)}, f32[16,32,3,128]{3,1,0,2:T(8,128)S(1)}, /*index=5*/s32[]{:T(128)}) while((s32[]{:T(128)}, f32[16,32,3,128]{3,2,1,0:T(4,128)S(1)}, s32[16,32]{1,0:T(8,128)}, f32[8,3,128]{2,1,0:T(4,128)S(1)}, ...), condition=%wide.region_9.10_spmd, body=%wide.region_6.9_spmd.sunk | while | flops 9962594 | bytes 9065821 | solution.py:203
  155.2 3.7 %fusion.99 = f32[32,3,128]{2,1,0:T(4,128)S(1)} fusion(f32[32,128,128]{2,1,0:T(8,128)S(1)} %subtract_maximum_fusion.2, f32[32,3,128]{2,1,0:T(4,128)S(1)} %bitcast.439, f32[32,3,128]{2,1,0:T(4,128)S(1)} %gather_fusion), kind=kLoop, calls=%fused_computation.12.clone.1 | loop fusion | flops 4706304 | bytes 2244608 | tf_op jit(solution)/shard_map/while/body/eval_jaxpr/reduce_sum | solution.py:106
  163.5 3.7 %fusion.99 = f32[32,3,128]{2,1,0:T(4,128)S(1)} fusion(f32[32,128,128]{2,1,0:T(8,128)S(1)} %subtract_maximum_fusion.2, f32[32,3,128]{2,1,0:T(4,128)S(1)} %bitcast.439, f32[32,3,128]{2,1,0:T(4,128)S(1)} %gather_fusion), kind=kLoop, calls=%fused_computation.12.clone.1 | loop fusion | flops 4706304 | bytes 2244608 | tf_op jit(solution)/shard_map/while/body/eval_jaxpr/reduce_sum | solution.py:106
  171.8 3.7 %fusion.99 = f32[32,3,128]{2,1,0:T(4,128)S(1)} fusion(f32[32,128,128]{2,1,0:T(8,128)S(1)} %subtract_maximum_fusion.2, f32[32,3,128]{2,1,0:T(4,128)S(1)} %bitcast.439, f32[32,3,128]{2,1,0:T(4,128)S(1)} %gather_fusion), kind=kLoop, calls=%fused_computation.12.clone.1 | loop fusion | flops 4706304 | bytes 2244608 | tf_op jit(solution)/shard_map/while/body/eval_jaxpr/reduce_sum | solution.py:106
  180.2 3.7 %fusion.99 = f32[32,3,128]{2,1,0:T(4,128)S(1)} fusion(f32[32,128,128]{2,1,0:T(8,128)S(1)} %subtract_maximum_fusion.2, f32[32,3,128]{2,1,0:T(4,128)S(1)} %bitcast.439, f32[32,3,128]{2,1,0:T(4,128)S(1)} %gather_fusion), kind=kLoop, calls=%fused_computation.12.clone.1 | loop fusion | flops 4706304 | bytes 2244608 | tf_op jit(solution)/shard_map/while/body/eval_jaxpr/reduce_sum | solution.py:106
  188.5 3.7 %fusion.99 = f32[32,3,128]{2,1,0:T(4,128)S(1)} fusion(f32[32,128,128]{2,1,0:T(8,128)S(1)} %subtract_maximum_fusion.2, f32[32,3,128]{2,1,0:T(4,128)S(1)} %bitcast.439, f32[32,3,128]{2,1,0:T(4,128)S(1)} %gather_fusion), kind=kLoop, calls=%fused_computation.12.clone.1 | loop fusion | flops 4706304 | bytes 2244608 | tf_op jit(solution)/shard_map/while/body/eval_jaxpr/reduce_sum | solution.py:106
  196.8 3.7 %fusion.99 = f32[32,3,128]{2,1,0:T(4,128)S(1)} fusion(f32[32,128,128]{2,1,0:T(8,128)S(1)} %subtract_maximum_fusion.2, f32[32,3,128]{2,1,0:T(4,128)S(1)} %bitcast.439, f32[32,3,128]{2,1,0:T(4,128)S(1)} %gather_fusion), kind=kLoop, calls=%fused_computation.12.clone.1 | loop fusion | flops 4706304 | bytes 2244608 | tf_op jit(solution)/shard_map/while/body/eval_jaxpr/reduce_sum | solution.py:106
  205.1 3.7 %fusion.99 = f32[32,3,128]{2,1,0:T(4,128)S(1)} fusion(f32[32,128,128]{2,1,0:T(8,128)S(1)} %subtract_maximum_fusion.2, f32[32,3,128]{2,1,0:T(4,128)S(1)} %bitcast.439, f32[32,3,128]{2,1,0:T(4,128)S(1)} %gather_fusion), kind=kLoop, calls=%fused_computation.12.clone.1 | loop fusion | flops 4706304 | bytes 2244608 | tf_op jit(solution)/shard_map/while/body/eval_jaxpr/reduce_sum | solution.py:106
  213.4 3.7 %fusion.99 = f32[32,3,128]{2,1,0:T(4,128)S(1)} fusion(f32[32,128,128]{2,1,0:T(8,128)S(1)} %subtract_maximum_fusion.2, f32[32,3,128]{2,1,0:T(4,128)S(1)} %bitcast.439, f32[32,3,128]{2,1,0:T(4,128)S(1)} %gather_fusion), kind=kLoop, calls=%fused_computation.12.clone.1 | loop fusion | flops 4706304 | bytes 2244608 | tf_op jit(solution)/shard_map/while/body/eval_jaxpr/reduce_sum | solution.py:106
  286.2 9.9 %scatter_custom_fusion.2 = f32[3,16384]{0,1:T(8,128)} fusion(s32[1024]{0:T(1024)} %fusion.81, f32[1024,3]{1,0:T(8,128)S(1)} %bitcast.455, f32[]{:T(128)} %constant.33.clone.1), kind=kCustom, calls=%fused_computation.23 | custom fusion | flops 3072 | bytes 197120 | tf_op jit(solution)/shard_map/scatter-add | solution.py:225
  296.1 12.1 %scatter_fusion.1 = f32[3,16384]{0,1:T(8,128)} fusion(f32[3,16384]{0,1:T(8,128)} %scatter_custom_fusion.2, s32[1024]{0:T(1024)S(1)} %copy-done.35, f32[1024,3]{1,0:T(8,128)S(1)} %bitcast.456), kind=kCustom, calls=%fused_computation.6 | custom fusion | flops 3072 | bytes 40960 | tf_op jit(solution)/shard_map/scatter-add | solution.py:225
  308.1 12.1 %scatter_fusion.2 = f32[3,16384]{0,1:T(8,128)} fusion(f32[3,16384]{0,1:T(8,128)} %scatter_fusion.1, s32[1024]{0:T(1024)S(1)} %copy-done.33, f32[1024,3]{1,0:T(8,128)S(1)} %bitcast.457), kind=kCustom, calls=%fused_computation.7 | custom fusion | flops 3072 | bytes 40960 | tf_op jit(solution)/shard_map/scatter-add | solution.py:225
  320.2 12.1 %scatter_fusion.3 = f32[3,16384]{0,1:T(8,128)} fusion(f32[3,16384]{0,1:T(8,128)} %scatter_fusion.2, s32[1024]{0:T(1024)S(1)} %copy-done.34, f32[1024,3]{1,0:T(8,128)S(1)} %bitcast.458), kind=kCustom, calls=%fused_computation.8 | custom fusion | flops 3072 | bytes 40960 | tf_op jit(solution)/shard_map/scatter-add | solution.py:225
  332.4 6.1 %copy.132 = f32[3,8,16,128]{3,2,1,0:T(8,128)} copy(f32[3,8,16,128]{0,3,2,1:T(8,128)} %bitcast.437) | data formatting | bytes 393216 | tf_op jit(solution)/shard_map/reshape | solution.py:226
  (319 shorter events, 160.9 us)
Async XLA Ops:
  0.6 33.8 %copy-start.25 = (f32[3,8,16,128]{3,2,1,0:T(8,128)S(1)}, f32[3,8,16,128]{3,2,1,0:T(8,128)}, u32[]{:S(2)}) copy-start(f32[3,8,16,128]{3,2,1,0:T(8,128)} %param.14) | copy-start | bytes 589828
  5.6 82.6 %all-to-all-start = ((s32[128,1,4]{2,1,0:T(1,128)}), s32[128,1,4]{2,1,0:T(1,128)S(1)}, u32[]{:S(2)}, u32[]{:S(2)}) async-start(s32[128,1,4]{2,1,0:T(1,128)} %bitcast.16), calls=%async_computation | async-start | bytes 131072 | tf_op jit(solution)/shard_map/all_to_all | solution.py:190
  23.8 91.4 %collective-permute-start = (f32[8,1,16,128]{3,2,1,0:T(8,128)}, f32[8,1,16,128]{3,2,1,0:T(8,128)}, u32[]{:S(2)}, u32[]{:S(2)}) collective-permute-start(f32[8,1,16,128]{3,2,1,0:T(8,128)} %pad_maximum_fusion.22), channel_id=1, source_target_pairs={{0,32},{32,64},{64,96},{96,128},{128,160},{160,192},{192,224},{224... | collective-permute-start | bytes 196616 | tf_op jit(solution)/shard_map/ppermute | solution.py:36
  27.2 29.6 %collective-permute-start.3 = (f32[3,1,16,128]{3,2,1,0:T(8,128)S(1)}, f32[3,1,16,128]{3,2,1,0:T(8,128)S(1)}, u32[]{:S(2)}, u32[]{:S(2)}) collective-permute-start(f32[3,1,16,128]{3,2,1,0:T(8,128)S(1)} %get-tuple-element.133), channel_id=1, source_target_pairs={{0,32},{32,64},{64,96},{96,128},{128,160},{160,192},{192,224},{224... | collective-permute-start | bytes 73736 | tf_op jit(solution)/shard_map/ppermute | solution.py:25
  30.0 27.1 %collective-permute-start.4 = (f32[3,1,16,128]{3,2,1,0:T(8,128)S(1)}, f32[3,1,16,128]{3,2,1,0:T(8,128)S(1)}, u32[]{:S(2)}, u32[]{:S(2)}) collective-permute-start(f32[3,1,16,128]{3,2,1,0:T(8,128)S(1)} %get-tuple-element.132), channel_id=1, source_target_pairs={{32,0},{64,32},{96,64},{128,96},{160,128},{192,160},{224,192},{256... | collective-permute-start | bytes 73736 | tf_op jit(solution)/shard_map/ppermute | solution.py:28
  40.9 15.2 %copy-start.37 = (pred[129]{0:T(512)(128)(4,1)}, pred[129]{0:T(512)(128)(4,1)S(1)}, u32[]{:S(2)}) copy-start(pred[129]{0:T(512)(128)(4,1)S(1)} %compare_or_fusion) | copy-start | bytes 391
  41.0 15.1 %copy-start.31 = (pred[9,17]{1,0:T(8,128)(4,1)}, pred[9,17]{1,0:T(8,128)(4,1)S(1)}, u32[]{:S(2)}) copy-start(pred[9,17]{1,0:T(8,128)(4,1)S(1)} %broadcast_and_fusion.1) | copy-start | bytes 463
  57.1 52.0 %collective-permute-start.6 = (f32[3,10,1,128]{3,2,1,0:T(1,128)S(1)}, f32[3,10,1,128]{3,2,1,0:T(1,128)S(1)}, u32[]{:S(2)}, u32[]{:S(2)}) collective-permute-start(f32[3,10,1,128]{3,2,1,0:T(1,128)S(1)} %get-tuple-element.115), channel_id=1, source_target_pairs={{8,0},{16,8},{24,16},{9,1},{17,9},{25,17},{10,2},{18,10},{26,18},{... | collective-permute-start | bytes 46088 | tf_op jit(solution)/shard_map/ppermute | solution.py:28
  58.4 50.7 %collective-permute-start.5 = (f32[3,10,1,128]{3,2,1,0:T(1,128)S(1)}, f32[3,10,1,128]{3,2,1,0:T(1,128)S(1)}, u32[]{:S(2)}, u32[]{:S(2)}) collective-permute-start(f32[3,10,1,128]{3,2,1,0:T(1,128)S(1)} %get-tuple-element.114), channel_id=1, source_target_pairs={{0,8},{8,16},{16,24},{1,9},{9,17},{17,25},{2,10},{10,18},{18,26},{... | collective-permute-start | bytes 46088 | tf_op jit(solution)/shard_map/ppermute | solution.py:25
  88.2 27.0 %copy-start = (f32[6,8,16,128]{3,2,1,0:T(8,128)S(1)}, f32[6,8,16,128]{3,2,1,0:T(8,128)}, u32[]{:S(2)}) copy-start(f32[6,8,16,128]{3,2,1,0:T(8,128)} %param.16) | copy-start | bytes 1179652
  88.2 27.0 %copy-start.1 = (f32[8,16,128]{2,1,0:T(8,128)S(1)}, f32[8,16,128]{2,1,0:T(8,128)}, u32[]{:S(2)}) copy-start(f32[8,16,128]{2,1,0:T(8,128)} %param.18) | copy-start | bytes 196612
  88.2 27.0 %copy-start.3 = (f32[8,16,128]{2,1,0:T(8,128)S(1)}, f32[8,16,128]{2,1,0:T(8,128)}, u32[]{:S(2)}) copy-start(f32[8,16,128]{2,1,0:T(8,128)} %param.17) | copy-start | bytes 196612
  88.8 62.4 %all-to-all-start.1 = ((f32[128,4,3,128]{3,1,2,0:T(4,128)}), f32[128,4,3,128]{3,1,2,0:T(4,128)S(1)}, u32[]{:S(2)}, u32[]{:S(2)}) async-start(f32[128,4,3,128]{3,1,2,0:T(4,128)} %copy.119), calls=%async_computation.1 | async-start | bytes 1572864 | tf_op jit(solution)/shard_map/all_to_all | solution.py:189
  109.1 23.2 %copy-start.2 = (f32[8,16,128]{2,1,0:T(8,128)S(1)}, f32[8,16,128]{2,1,0:T(8,128)}, u32[]{:S(2)}) copy-start(f32[8,16,128]{2,1,0:T(8,128)} %param.18) | copy-start | bytes 196612
  109.1 23.1 %copy-start.4 = (f32[8,16,128]{2,1,0:T(8,128)S(1)}, f32[8,16,128]{2,1,0:T(8,128)}, u32[]{:S(2)}) copy-start(f32[8,16,128]{2,1,0:T(8,128)} %param.17) | copy-start | bytes 196612
  109.3 21.9 %collective-permute-start.7 = (f32[3,10,18,1]{3,2,1,0:T(8,128)S(1)}, f32[3,10,18,1]{3,2,1,0:T(8,128)S(1)}, u32[]{:S(2)}, u32[]{:S(2)}) collective-permute-start(f32[3,10,18,1]{3,2,1,0:T(8,128)S(1)} %get-tuple-element.110), channel_id=1, source_target_pairs={{0,1},{1,2},{2,3},{3,4},{4,5},{5,6},{6,7},{8,9},{9,10},{10,11},{11... | collective-permute-start | bytes 6488 | tf_op jit(solution)/shard_map/ppermute | solution.py:25
  110.6 20.6 %collective-permute-start.8 = (f32[3,10,18,1]{3,2,1,0:T(8,128)S(1)}, f32[3,10,18,1]{3,2,1,0:T(8,128)S(1)}, u32[]{:S(2)}, u32[]{:S(2)}) collective-permute-start(f32[3,10,18,1]{3,2,1,0:T(8,128)S(1)} %get-tuple-element.111), channel_id=1, source_target_pairs={{1,0},{2,1},{3,2},{4,3},{5,4},{6,5},{7,6},{9,8},{10,9},{11,10},{12... | collective-permute-start | bytes 6488 | tf_op jit(solution)/shard_map/ppermute | solution.py:28
  116.0 15.6 %collective-permute-start.1 = (f32[8,9,1,128]{3,2,1,0:T(1,128)S(1)}, f32[8,9,1,128]{3,2,1,0:T(1,128)S(1)}, u32[]{:S(2)}, u32[]{:S(2)}) collective-permute-start(f32[8,9,1,128]{3,2,1,0:T(1,128)S(1)} %pad_maximum_fusion.24), channel_id=1, source_target_pairs={{0,8},{8,16},{16,24},{1,9},{9,17},{17,25},{2,10},{10,18},{18,26},{... | collective-permute-start | bytes 110600 | tf_op jit(solution)/shard_map/ppermute | solution.py:36
  134.6 6.2 %collective-permute-start.2 = (f32[8,9,17,1]{2,0,3,1:T(8,128)}, f32[8,9,17,1]{2,0,3,1:T(8,128)}, u32[]{:S(2)}, u32[]{:S(2)}) collective-permute-start(f32[8,9,17,1]{2,0,3,1:T(8,128)} %copy.130), channel_id=1, source_target_pairs={{0,1},{1,2},{2,3},{3,4},{4,5},{5,6},{6,7},{8,9},{9,10},{10,11},{11... | collective-permute-start | bytes 14696 | tf_op jit(solution)/shard_map/ppermute | solution.py:36
  286.1 9.9 %copy-start.35 = (s32[1024]{0:T(1024)S(1)}, s32[1024]{0:T(1024)}, u32[]{:S(2)}) copy-start(s32[1024]{0:T(1024)} %fusion.82) | copy-start | bytes 12292
  286.1 22.0 %copy-start.33 = (s32[1024]{0:T(1024)S(1)}, s32[1024]{0:T(1024)}, u32[]{:S(2)}) copy-start(s32[1024]{0:T(1024)} %fusion.83) | copy-start | bytes 12292
  286.1 34.1 %copy-start.34 = (s32[1024]{0:T(1024)S(1)}, s32[1024]{0:T(1024)}, u32[]{:S(2)}) copy-start(s32[1024]{0:T(1024)} %fusion.84) | copy-start | bytes 12292
  332.3 6.2 %copy-start.13 = (f32[1,9,17,129]{3,2,1,0:T(8,128)S(1)}, f32[1,9,17,129]{3,2,1,0:T(8,128)}, u32[]{:S(2)}) copy-start(f32[1,9,17,129]{3,2,1,0:T(8,128)} %get-tuple-element.89) | copy-start | bytes 236848
  332.3 6.2 %copy-start.14 = (f32[1,9,17,129]{3,2,1,0:T(8,128)S(1)}, f32[1,9,17,129]{3,2,1,0:T(8,128)}, u32[]{:S(2)}) copy-start(f32[1,9,17,129]{3,2,1,0:T(8,128)} %get-tuple-element.90) | copy-start | bytes 236848
  (27 other events, 113.4 us)
where the time goes:
time: 346 us; the launch traced here: 341 us
  other arithmetic  191 us (55%)
  local copies, waits for them, and re-layouts  76.4 us (22%)
  starting transfers between devices  55.8 us (16%)
  waiting for transfers between devices  15.5 us (4%)
    reduce_sum x16, other arithmetic, contact_force(): return jnp.sum(weight[:, None, :, :] * offset_vec, axis=3)  59.6 us
    scatter-add x4, other arithmetic, on_device(): node_force.at[:, node_ids[:, corner_slot, :]].add(quarter_force)  46.1 us
    reduce_sum x16, other arithmetic, contact_force(): distance_sq = jnp.sum(offset_vec * offset_vec, axis=1)  33.2 us
    gather x2, local copies, waits for them, and re-layouts, on_device(): centroids[source_ids]  16.8 us
    all_to_all x1, starting transfers between devices, on_device(): lax.all_to_all(send_target, ('gx', 'gz'), split_axis=0, concat_axis=0, ti...  16.7 us
    all_to_all x1, starting transfers between devices, on_device(): lax.all_to_all(send_data, ('gx', 'gz'), split_axis=0, concat_axis=0, tile...  15.8 us
    gather x1, local copies, waits for them, and re-layouts, on_device(): picked = flat_disp[:, node_ids]  14.1 us
    ppermute x3, waiting for transfers between devices, padded_2(): lax.ppermute(lax.slice_in_dim(block, block.shape[dim] - width, None, axis...  11.8 us
  transfers between devices with their start and end apart: 11, of which 2 were waited for; matrix products, arithmetic and copies ran while one was open for 21% of the time, Pallas kernels for 0%

commit v1 on v0

v1 whole, which is shorter than its diff:
```python
import jax
import jax.numpy as jnp
from jax import lax
from jax.experimental import pallas as pl
from jax.experimental.pallas import tpu as pltpu
from jax.sharding import PartitionSpec as P

FACETS = 128
SLOTS = 4
ROWS = 13
TIME_STEP = 0.25
SHEAR_MODULUS = 1.0
BULK_MODULUS = 2.0
HARDENING = 1.0
PENALTY = 1.0
REACH_SQUARED = 1.0
VOIGT = ((0, 3, 5), (3, 1, 4), (5, 4, 2))
NT = (((1,), (1,)), ((), ()))
VMEM = pl.BlockSpec(memory_space=pltpu.VMEM)
SMEM = pl.BlockSpec(memory_space=pltpu.SMEM)


def params(mib):
    return pltpu.CompilerParams(vmem_limit_bytes=mib * 1024 * 1024)


def split_2(value):
    high = value.astype(jnp.bfloat16)
    rest = (value - high.astype(jnp.float32)).astype(jnp.bfloat16)
    return high, rest


def lane_pick(value, lane):
    pick = (lax.broadcasted_iota(jnp.int32, (8, 128), 1) == lane).astype(jnp.float32)
    return lax.dot_general(
        pick, value, NT, precision=lax.Precision.HIGHEST, preferred_element_type=jnp.float32
    )[0:1]


def columns_of(rows):
    count = rows.shape[0]
    padded = jnp.concatenate([rows, jnp.zeros((128 - count, 128), jnp.float32)], axis=0)
    return padded.T


def low_z_kernel(velocity_ref, face_ref):
    face_ref[...] = lane_pick(velocity_ref[...], 0)


def pack_kernel(
    disp_ref, anchor_ref, nodes_ref, source_ref, dest_ref, target_ref, cent_ref, send_ref, count, slot_target
):
    peers = send_ref.shape[0] // ROWS
    pairs = source_ref.shape[0]
    high, rest = split_2(disp_ref[...])
    table = jnp.concatenate([high, rest], axis=1)
    iota = lax.broadcasted_iota(jnp.int32, (128, 4 * FACETS), 0)
    for block in range(anchor_ref.shape[0] // 3):
        ids = jnp.concatenate([nodes_ref[block * 4 + m : block * 4 + m + 1, :] for m in range(4)], axis=1)
        here = jnp.where(iota == (ids & 127), 1.0, 0.0).astype(jnp.bfloat16)
        picked = jnp.dot(table, jnp.concatenate([here, here], axis=0), preferred_element_type=jnp.float32)
        in_row = iota == (ids >> 7)
        for c in range(3):
            kept = jnp.where(in_row, picked[c * 128 : (c + 1) * 128], 0.0)
            total = kept[:, :128] + kept[:, 128:256] + kept[:, 256:384] + kept[:, 384:]
            total = jnp.sum(total, axis=0, keepdims=True)
            cent_ref[block * 3 + c] = anchor_ref[block * 3 + c] + 0.25 * total
    send_ref[...] = jnp.zeros(send_ref.shape, jnp.float32)

    def clear(peer, carry):
        count[peer] = 0
        for k in range(SLOTS):
            slot_target[peer * SLOTS + k] = -1
        return carry

    lax.fori_loop(0, peers, clear, 0)

    def place(pair, carry):
        dest = dest_ref[pair]
        slot = count[dest]
        count[dest] = slot + 1
        slot_target[dest * SLOTS + slot] = target_ref[pair]
        send_ref[pl.ds(dest * ROWS + 3 * slot, 3)] = cent_ref[pl.ds(source_ref[pair] * 3, 3)]
        return carry

    lax.fori_loop(0, pairs, place, 0, unroll=8)
    lane = lax.broadcasted_iota(jnp.int32, (1, 128), 1)

    def write_targets(peer, carry):
        row = jnp.full((1, 128), -1, jnp.int32)
        for k in range(SLOTS):
            row = jnp.where(lane == k, slot_target[peer * SLOTS + k], row)
        send_ref[peer * ROWS + ROWS - 1] = row.astype(jnp.float32)
        return carry

    lax.fori_loop(0, peers, write_targets, 0, unroll=4)


def spread_kernel(cent_ref, wide_ref):
    for r in range(wide_ref.shape[0]):
        wide_ref[r] = jnp.broadcast_to(cent_ref[r], (FACETS, FACETS)).T


def stress_kernel(
    velocity_ref, face_z_ref, face_x_ref, face_y_ref, stress_ref, plastic_ref, yield_ref,
    stress_out, plastic_out, upper_out, lower_out, edge_y_out, edge_x_out,
):
    nx = velocity_ref.shape[1]
    columns = columns_of(
        jnp.concatenate([face_z_ref[...], face_x_ref[48:51, :], face_y_ref[27:33, :]], axis=0)
    )
    lane = lax.broadcasted_iota(jnp.int32, (16, 128), 1)
    row = lax.broadcasted_iota(jnp.int32, (16, 128), 0)
    grad_x, grad_y, grad_z = ([], [], [])
    for c in range(3):
        sum_yz, dif_y, dif_z = ([], [], [])
        for x in range(nx + 1):
            if x < nx:
                plane = velocity_ref[c, x]
                beyond = columns[x * 16 : x * 16 + 16, c : c + 1]
                edge = face_y_ref[c * 8 + x : c * 8 + x + 1, :]
                edge_beyond = columns[x * 16 : x * 16 + 1, 6 + c : 7 + c]
            else:
                plane = face_x_ref[c * 16 : c * 16 + 16, :]
                beyond = columns[0:16, 3 + c : 4 + c]
                edge = face_y_ref[24 + c : 25 + c, :]
                edge_beyond = columns[0:1, 9 + c : 10 + c]
            edge = jnp.broadcast_to(edge, (16, 128))
            after = jnp.where(lane == 127, beyond, pltpu.roll(plane, 127, 1))
            edge_after = jnp.where(lane == 127, edge_beyond, pltpu.roll(edge, 127, 1))
            sum_z, dif = plane + after, after - plane
            sum_z_next = jnp.where(row == 15, edge + edge_after, pltpu.roll(sum_z, 15, 0))
            dif_next = jnp.where(row == 15, edge_after - edge, pltpu.roll(dif, 15, 0))
            sum_yz.append(sum_z + sum_z_next)
            dif_y.append(sum_z_next - sum_z)
            dif_z.append(dif + dif_next)
        grad_x.append([0.25 * (sum_yz[x + 1] - sum_yz[x]) for x in range(nx)])
        grad_y.append([0.25 * (dif_y[x + 1] + dif_y[x]) for x in range(nx)])
        grad_z.append([0.25 * (dif_z[x + 1] + dif_z[x]) for x in range(nx)])
    stresses = []
    for x in range(nx):
        inc = [TIME_STEP * grad_x[0][x], TIME_STEP * grad_y[1][x], TIME_STEP * grad_z[2][x]]
        shear = [
            TIME_STEP * 0.5 * (grad_y[0][x] + grad_x[1][x]),
            TIME_STEP * 0.5 * (grad_z[1][x] + grad_y[2][x]),
            TIME_STEP * 0.5 * (grad_z[0][x] + grad_x[2][x]),
        ]
        volume = inc[0] + inc[1] + inc[2]
        trial = [
            stress_ref[d, x] + 2.0 * SHEAR_MODULUS * (inc[d] - volume / 3.0) + BULK_MODULUS * volume
            for d in range(3)
        ]
        trial_shear = [stress_ref[3 + d, x] + 2.0 * SHEAR_MODULUS * shear[d] for d in range(3)]
        mean = (trial[0] + trial[1] + trial[2]) / 3.0
        dev = [trial[d] - mean for d in range(3)]
        square = dev[0] * dev[0] + dev[1] * dev[1] + dev[2] * dev[2]
        square = square + 2.0 * (
            trial_shear[0] * trial_shear[0] + trial_shear[1] * trial_shear[1] + trial_shear[2] * trial_shear[2]
        )
        equivalent = jnp.sqrt(1.5 * square)
        plastic = plastic_ref[x]
        limit = yield_ref[x] + HARDENING * plastic
        gamma = jnp.maximum(equivalent - limit, 0.0) / (3.0 * SHEAR_MODULUS + HARDENING)
        factor = 1.0 - 3.0 * SHEAR_MODULUS * gamma / jnp.maximum(equivalent, limit)
        new = [dev[d] * factor + mean for d in range(3)] + [trial_shear[d] * factor for d in range(3)]
        for d in range(6):
            stress_out[d, x] = new[d]
        plastic_out[x] = plastic + gamma
        stresses.append(new)
    for c in range(3):
        before = None
        edge_before = None
        for x in range(nx + 1):
            if x < nx:
                s = [0.25 * stresses[x][VOIGT[c][d]] for d in range(3)]
                down = [jnp.where(row == 0, 0.0, pltpu.roll(v, 1, 0)) for v in s]
                here = [down[0] + s[0], down[1] - s[1], down[2] + s[2]]
                edge_here = [v[15:16] for v in s]
            if x == 0:
                x0, x1, x2 = -here[0], here[1], here[2]
                e0, e1, e2 = -edge_here[0], edge_here[1], edge_here[2]
            elif x < nx:
                x0, x1, x2 = before[0] - here[0], before[1] + here[1], before[2] + here[2]
                e0, e1, e2 = (
                    edge_before[0] - edge_here[0], edge_before[1] + edge_here[1], edge_before[2] + edge_here[2]
                )
            else:
                x0, x1, x2 = before
                e0, e1, e2 = edge_before
            both = x0 + x1
            edge_both = e0 + e1
            if x < nx:
                upper_out[c, x] = both + x2
                lower_out[c, x] = both - x2
            else:
                edge_x_out[c] = both + x2
                edge_x_out[3 + c] = both - x2
            edge_y_out[c, x : x + 1, :] = edge_both + e2
            edge_y_out[3 + c, x : x + 1, :] = edge_both - e2
            before, edge_before = here, edge_here


def force_kernel(upper_ref, lower_ref, from_y_ref, from_x_ref, internal_out, face_out):
    nx = upper_ref.shape[1]
    lane = lax.broadcasted_iota(jnp.int32, (16, 128), 1)
    row = lax.broadcasted_iota(jnp.int32, (16, 128), 0)
    for c in range(3):
        planes = []
        for x in range(nx):
            upper = upper_ref[c, x] + jnp.where(row == 0, from_y_ref[c, x : x + 1, :], 0.0)
            lower = lower_ref[c, x] + jnp.where(row == 0, from_y_ref[3 + c, x : x + 1, :], 0.0)
            if x == 0:
                upper = upper + from_x_ref[c]
                lower = lower + from_x_ref[3 + c]
            planes.append(upper)
            internal_out[c, x] = lower + jnp.where(lane == 0, 0.0, pltpu.roll(upper, 1, 1))
        face_out[:, c * 128 : (c + 1) * 128] = lane_pick(jnp.concatenate(planes, axis=0), 127)


def pair_kernel(
    got_ref, got_rows_ref, wide_ref, nodes_ref, internal_ref, from_z_ref, velocity_ref, disp_ref, mass_ref,
    velocity_out, disp_out, targets, target_vec, sums, slots, count, semaphore,
):
    blocks = wide_ref.shape[0] // 3
    peers = got_ref.shape[0] // ROWS
    target_rows = got_rows_ref[pl.ds(ROWS - 1, peers, stride=ROWS), :]
    if peers < 128:
        target_rows = jnp.concatenate([target_rows, jnp.full((128 - peers, 128), -1.0)], axis=0)
    target_vec[...] = target_rows.T[0:8, :].astype(jnp.int32)
    copy = pltpu.make_async_copy(target_vec, targets, semaphore)
    copy.start()
    copy.wait()
    for block in range(blocks + 1):
        count[block] = 0
    room = SLOTS * peers

    def sort_peer(peer, carry):
        for k in range(SLOTS):
            target = targets[k, peer]
            block = jnp.where(target < 0, blocks, target)
            place = count[block]
            count[block] = place + 1
            slots[block * room + place] = peer * ROWS + 3 * k
        return carry

    lax.fori_loop(0, peers, sort_peer, 0, unroll=2)

    def one_block(block, carry):
        number = count[block]
        for start in range(0, FACETS, 32):
            own = [wide_ref[block * 3 + c, start : start + 32, :] for c in range(3)]

            def group(step, total):
                total = list(total)
                for k in range(4):
                    place = step * 4 + k
                    inside = place < number
                    base = slots[block * room + jnp.where(inside, place, 0)]
                    away = jnp.where(inside, 0.0, 1.0e4)
                    offset = [
                        own[0] - (got_ref[base] + away), own[1] - got_ref[base + 1], own[2] - got_ref[base + 2]
                    ]
                    distance = offset[0] * offset[0] + offset[1] * offset[1] + offset[2] * offset[2]
                    weight = PENALTY * jnp.maximum(REACH_SQUARED - distance, 0.0)
                    total = [total[c] + weight * offset[c] for c in range(3)]
                return tuple(total)

            zero = jnp.zeros((32, FACETS), jnp.float32)
            total = lax.fori_loop(0, (number + 3) >> 2, group, (zero, zero, zero))
            for c in range(3):
                sums[block * 3 + c, start : start + 32, :] = total[c]
        return carry

    lax.fori_loop(0, blocks, one_block, 0)
    ones = jnp.ones((8, FACETS), jnp.float32)
    iota = lax.broadcasted_iota(jnp.int32, (128, FACETS), 0)
    contact = jnp.zeros((384, 128), jnp.float32)
    for block in range(blocks):
        left, right = ([], [])
        parts = []
        for c in range(3):
            force = lax.dot_general(
                ones, sums[block * 3 + c], NT, precision=lax.Precision.HIGHEST, preferred_element_type=jnp.float32
            )[0:1]
            high, rest = split_2(0.25 * force)
            parts.append((high.astype(jnp.float32), rest.astype(jnp.float32)))
        for m in range(4):
            ids = nodes_ref[block * 4 + m : block * 4 + m + 1, :]
            here = jnp.where(iota == (ids & 127), 1.0, 0.0).astype(jnp.bfloat16)
            in_row = iota == (ids >> 7)
            for part in range(2):
                left.append(
                    jnp.concatenate(
                        [jnp.where(in_row, parts[c][part], 0.0).astype(jnp.bfloat16) for c in range(3)], axis=0
                    )
                )
                right.append(here)
        contact = contact + lax.dot_general(
            jnp.concatenate(left, axis=1), jnp.concatenate(right, axis=1), NT, preferred_element_type=jnp.float32
        )
    columns = columns_of(from_z_ref[...])
    lane = lax.broadcasted_iota(jnp.int32, (128, 128), 1)
    for c in range(3):
        rows = slice(c * 128, c * 128 + 128)
        internal = internal_ref[rows, :] + jnp.where(lane == 0, columns[:, c : c + 1], 0.0)
        velocity = velocity_ref[rows, :] + TIME_STEP * (contact[rows] - internal) / mass_ref[...]
        velocity_out[rows, :] = velocity
        disp_out[rows, :] = disp_ref[rows, :] + TIME_STEP * velocity


def shifted(value, axis, step):
    count = lax.axis_size(axis)
    return lax.ppermute(value, axis, [(i, i + step) for i in range(count) if 0 <= i + step < count])


def f32(*shape):
    return jax.ShapeDtypeStruct(shape, jnp.float32)


def on_device(
    velocity,
    displacement,
    mass,
    stress,
    plastic,
    yield_stress,
    facet_anchor,
    facet_nodes,
    pair_source,
    pair_dest,
    pair_target,
):
    size_x, size_y, size_z = velocity.shape[1:]
    blocks = facet_anchor.shape[3]
    pairs = pair_source.shape[3]
    peers = lax.axis_size("gx") * lax.axis_size("gz")
    flat_velocity = velocity.reshape(-1, size_z)
    flat_disp = displacement.reshape(-1, size_z)
    nodes = facet_nodes.reshape(blocks * 4, FACETS)
    anchors = facet_anchor.reshape(blocks * 3, 1, FACETS)

    low_z = pl.pallas_call(
        low_z_kernel, out_shape=f32(1, flat_velocity.shape[0]), compiler_params=params(8), name="low_z"
    )(flat_velocity)
    face_z = shifted(low_z, "gz", -1).reshape(3, 128)
    face_x = shifted(
        jnp.concatenate([velocity[:, 0].reshape(48, size_z), face_z], axis=0), "gx", -1
    )
    centroids, send = pl.pallas_call(
        pack_kernel,
        out_shape=(f32(blocks * 3, 1, FACETS), f32(peers * ROWS, 1, FACETS)),
        in_specs=[VMEM, VMEM, VMEM, SMEM, SMEM, SMEM],
        out_specs=(VMEM, VMEM),
        scratch_shapes=[pltpu.SMEM((peers,), jnp.int32), pltpu.SMEM((peers * SLOTS,), jnp.int32)],
        compiler_params=params(16),
        name="pack",
    )(
        flat_disp,
        anchors,
        nodes,
        pair_source.reshape(pairs),
        pair_dest.reshape(pairs),
        pair_target.reshape(pairs),
    )
    got = lax.all_to_all(send, ("gx", "gz"), split_axis=0, concat_axis=0, tiled=True)
    wide = pl.pallas_call(
        spread_kernel, out_shape=f32(blocks * 3, FACETS, FACETS), compiler_params=params(8), name="spread"
    )(centroids)
    face_y = shifted(
        jnp.concatenate(
            [
                velocity[:, :, 0].reshape(24, size_z),
                face_x[:48].reshape(3, 16, size_z)[:, 0],
                face_z,
                face_x[48:],
            ],
            axis=0,
        ),
        "gy",
        -1,
    )
    stress_new, plastic_new, upper, lower, edge_y, edge_x = pl.pallas_call(
        stress_kernel,
        out_shape=(
            f32(*stress.shape),
            f32(*plastic.shape),
            f32(*velocity.shape),
            f32(*velocity.shape),
            f32(6, size_x + 1, size_z),
            f32(6, size_y, size_z),
        ),
        compiler_params=params(16),
        name="stress",
    )(velocity, face_z, face_x, face_y, stress, plastic, yield_stress)
    from_y = shifted(edge_y, "gy", 1)
    from_x = shifted(edge_x.at[:, 0].add(from_y[:, size_x]), "gx", 1)
    internal, high_z = pl.pallas_call(
        force_kernel,
        out_shape=(f32(*velocity.shape), f32(1, flat_velocity.shape[0])),
        compiler_params=params(8),
        name="force",
    )(upper, lower, from_y, from_x)
    from_z = shifted(high_z, "gz", 1).reshape(3, 128)
    velocity_new, displacement_new = pl.pallas_call(
        pair_kernel,
        out_shape=(f32(*flat_velocity.shape), f32(*flat_velocity.shape)),
        scratch_shapes=[
            pltpu.SMEM((8, 128), jnp.int32),
            pltpu.VMEM((8, 128), jnp.int32),
            pltpu.VMEM((blocks * 3, FACETS, FACETS), jnp.float32),
            pltpu.SMEM(((blocks + 1) * SLOTS * peers,), jnp.int32),
            pltpu.SMEM((blocks + 1,), jnp.int32),
            pltpu.SemaphoreType.DMA,
        ],
        compiler_params=params(24),
        name="pairs",
    )(
        got,
        got.reshape(peers * ROWS, FACETS),
        wide,
        nodes,
        internal.reshape(-1, size_z),
        from_z,
        flat_velocity,
        flat_disp,
        mass.reshape(-1, size_z),
    )
    return (
        velocity_new.reshape(velocity.shape),
        displacement_new.reshape(velocity.shape),
        stress_new,
        plastic_new,
    )


def solution(mesh):
    return jax.shard_map(
        on_device,
        mesh=mesh,
        in_specs=(
            P(None, "gx", "gy", "gz"),
            P(None, "gx", "gy", "gz"),
            P("gx", "gy", "gz"),
            P(None, "gx", "gy", "gz"),
            P("gx", "gy", "gz"),
            P("gx", "gy", "gz"),
            P("gx", "gy", "gz", None, None, None),
            P("gx", "gy", "gz", None, None, None),
            P("gx", "gy", "gz", None),
            P("gx", "gy", "gz", None, None),
            P("gx", "gy", "gz", None),
        ),
        out_specs=(
            P(None, "gx", "gy", "gz"),
            P(None, "gx", "gy", "gz"),
            P(None, "gx", "gy", "gz"),
            P("gx", "gy", "gz"),
        ),
        check_vma=False,
    )
```

time: 346 us -> 106 us (0.31)
  the two profiles are of different devices: /device:TPU:56 before, /device:TPU:204 now
where the time goes in v1:
time: 106 us; the launch traced here: 105 us
  Pallas kernels  41 us (39%)
  waiting for transfers between devices  30.4 us (29%)
  starting transfers between devices  28.6 us (27%)
  local copies, waits for them, and re-layouts  4.53 us (4%)
    pallas_call x1, Pallas kernels, on_device(): pl.pallas_call(pair_kernel, out_shape=(f32(*flat_velocity.shape), f32(*fl...  32 us
    ppermute x6, waiting for transfers between devices, shifted(): lax.ppermute(value, axis, [(i, i + step) for i in range(count) if 0 <= i...  30.4 us
    all_to_all x1, starting transfers between devices, on_device(): lax.all_to_all(send, ('gx', 'gz'), split_axis=0, concat_axis=0, tiled=True)  14.8 us
    ppermute x6, starting transfers between devices, shifted(): lax.ppermute(value, axis, [(i, i + step) for i in range(count) if 0 <= i...  13.7 us
    pallas_call x1, Pallas kernels, on_device(): pl.pallas_call(pack_kernel, out_shape=(f32(blocks * 3, 1, FACETS), f32(pe...  6.32 us
    unnamed x26, local copies, waits for them, and re-layouts  4.48 us
  transfers between devices with their start and end apart: 7, of which 6 were waited for; matrix products, arithmetic and copies ran while one was open for 0% of the time, Pallas kernels for 2%

profile of v1, /device:TPU:204, one launch (start us, length us, event | category | flops | bytes accessed | tf_op | source)
XLA Modules:
  0.0 105.3 jit_solution(11039894480557303412)
XLA Ops:
  0.6 0.8 copy.19
  1.4 0.9 copy-done.1
  2.3 0.7 copy-done.5
  3.1 0.7 copy-done.9
  3.7 0.7 copy-done.10
  4.4 0.7 copy-done.11
  5.1 6.3 %pack.1 = (f32[24,1,128]{2,1,0:T(1,128)S(1)}, f32[1664,1,128]{2,1,0:T(1,128)}) custom-call(f32[384,128]{1,0:T(8,128)S(1)} %bitcast.23, f32[24,1,128]{2,1,0:T(1,128)S(1)} %bitcast.29, s32[32,128]{1,0:T(8,128)S(1)} %bitcast.27, s32[256]{0:T(256)S(1)} %bitcast.34, s32[256]{0:T(256)S(1)} %bitcast.35, s32[256]{0:T(256)S(1)} %bitcast.36), custom_call_target="tpu_custom_call" | custom-call | tf_op jit(solution)/shard_map/pack/pallas_call | solution.py:349
  11.4 14.8 %all-to-all-start = ((f32[1664,1,128]{2,1,0:T(1,128)}), f32[1664,1,128]{2,1,0:T(1,128)S(1)}, u32[]{:S(2)}, u32[]{:S(2)}) async-start(f32[1664,1,128]{2,1,0:T(1,128)} %get-tuple-element.28), calls=%async_computation | async-start | bytes 1703936 | tf_op jit(solution)/shard_map/all_to_all | solution.py:365
  26.6 2.6 %collective-permute-start = (f32[1,384]{1,0:T(1,128)S(1)}, f32[1,384]{1,0:T(1,128)S(1)}, u32[]{:S(2)}, u32[]{:S(2)}) collective-permute-start(f32[1,384]{1,0:T(1,128)S(1)} %low_z.1), channel_id=1, source_target_pairs={{1,0},{2,1},{3,2},{4,3},{5,4},{6,5},{7,6},{9,8},{10,9},{11,10},{12... | collective-permute-start | bytes 4616 | tf_op jit(solution)/shard_map/ppermute | solution.py:313
  29.2 16.1 %collective-permute-done = f32[1,384]{1,0:T(1,128)S(1)} collective-permute-done((f32[1,384]{1,0:T(1,128)S(1)}, f32[1,384]{1,0:T(1,128)S(1)}, u32[]{:S(2)}, u32[]{:S(2)}) %collective-permute-start) | collective-permute-done | bytes 1568 | tf_op jit(solution)/shard_map/ppermute | solution.py:313
  45.3 1.9 %collective-permute-start.1 = (f32[51,128]{1,0:T(8,128)S(1)}, f32[51,128]{1,0:T(8,128)S(1)}, u32[]{:S(2)}, u32[]{:S(2)}) collective-permute-start(f32[51,128]{1,0:T(8,128)S(1)} %pad_maximum_fusion), channel_id=1, source_target_pairs={{32,0},{64,32},{96,64},{128,96},{160,128},{192,160},{224,192},{256... | collective-permute-start | bytes 78344 | tf_op jit(solution)/shard_map/ppermute | solution.py:313
  47.3 1.5 %collective-permute-done.1.face_x_ref = f32[51,128]{1,0:T(8,128)S(1)} collective-permute-done((f32[51,128]{1,0:T(8,128)S(1)}, f32[51,128]{1,0:T(8,128)S(1)}, u32[]{:S(2)}, u32[]{:S(2)}) %collective-permute-start.1) | collective-permute-done | bytes 26144 | tf_op jit(solution)/shard_map/ppermute | solution.py:313
  48.8 2.4 %collective-permute-start.2 = (f32[33,128]{1,0:T(8,128)S(1)}, f32[33,128]{1,0:T(8,128)S(1)}, u32[]{:S(2)}, u32[]{:S(2)}) collective-permute-start(f32[33,128]{1,0:T(8,128)S(1)} %pad_maximum_fusion.1), channel_id=1, source_target_pairs={{8,0},{16,8},{24,16},{9,1},{17,9},{25,17},{10,2},{18,10},{26,18},{... | collective-permute-start | bytes 50696 | tf_op jit(solution)/shard_map/ppermute | solution.py:313
  51.3 3.2 %collective-permute-done.2.face_y_ref = f32[33,128]{1,0:T(8,128)S(1)} collective-permute-done((f32[33,128]{1,0:T(8,128)S(1)}, f32[33,128]{1,0:T(8,128)S(1)}, u32[]{:S(2)}, u32[]{:S(2)}) %collective-permute-start.2) | collective-permute-done | bytes 16928 | tf_op jit(solution)/shard_map/ppermute | solution.py:313
  54.5 1.4 %stress.1 = (f32[6,8,16,128]{3,2,1,0:T(8,128)}, f32[8,16,128]{2,1,0:T(8,128)}, f32[3,8,16,128]{3,2,1,0:T(8,128)S(1)}, f32[3,8,16,128]{3,2,1,0:T(8,128)S(1)}, f32...) custom-call(f32[3,8,16,128]{3,2,1,0:T(8,128)S(1)} %copy-done, f32[3,128]{1,0:T(4,128)S(1)} %bitcast.32, ...), custom_call_target="tpu_custom_call" | custom-call | tf_op jit(solution)/shard_map/stress/pallas_call | solution.py:382
  55.9 1.9 %collective-permute-start.3 = (f32[6,9,128]{2,1,0:T(8,128)S(1)}, f32[6,9,128]{2,1,0:T(8,128)S(1)}, u32[]{:S(2)}, u32[]{:S(2)}) collective-permute-start(f32[6,9,128]{2,1,0:T(8,128)S(1)} %get-tuple-element.32), channel_id=1, source_target_pairs={{0,8},{8,16},{16,24},{1,9},{9,17},{17,25},{2,10},{10,18},{18,26},{... | collective-permute-start | bytes 82952 | tf_op jit(solution)/shard_map/ppermute | solution.py:313
  57.8 4.1 %collective-permute-done.3.from_y_ref = f32[6,9,128]{2,1,0:T(8,128)S(1)} collective-permute-done((f32[6,9,128]{2,1,0:T(8,128)S(1)}, f32[6,9,128]{2,1,0:T(8,128)S(1)}, u32[]{:S(2)}, u32[]{:S(2)}) %collective-permute-start.3) | collective-permute-done | bytes 27680 | tf_op jit(solution)/shard_map/ppermute | solution.py:313
  61.9 2.5 %collective-permute-start.4 = (f32[6,16,128]{2,1,0:T(8,128)S(1)}, f32[6,16,128]{2,1,0:T(8,128)S(1)}, u32[]{:S(2)}, u32[]{:S(2)}) collective-permute-start(f32[6,16,128]{2,1,0:T(8,128)S(1)} %scatter-add.4), channel_id=1, source_target_pairs={{0,32},{32,64},{64,96},{96,128},{128,160},{160,192},{192,224},{224... | collective-permute-start | bytes 147464 | tf_op jit(solution)/shard_map/ppermute | solution.py:313
  64.5 2.9 %collective-permute-done.4.from_x_ref = f32[6,16,128]{2,1,0:T(8,128)S(1)} collective-permute-done((f32[6,16,128]{2,1,0:T(8,128)S(1)}, f32[6,16,128]{2,1,0:T(8,128)S(1)}, u32[]{:S(2)}, u32[]{:S(2)}) %collective-permute-start.4) | collective-permute-done | bytes 49184 | tf_op jit(solution)/shard_map/ppermute | solution.py:313
  67.3 0.4 force.1
  67.8 2.4 %collective-permute-start.5 = (f32[1,384]{1,0:T(1,128)S(1)}, f32[1,384]{1,0:T(1,128)S(1)}, u32[]{:S(2)}, u32[]{:S(2)}) collective-permute-start(f32[1,384]{1,0:T(1,128)S(1)} %get-tuple-element.35), channel_id=1, source_target_pairs={{0,1},{1,2},{2,3},{3,4},{4,5},{5,6},{6,7},{8,9},{9,10},{10,11},{11... | collective-permute-start | bytes 4616 | tf_op jit(solution)/shard_map/ppermute | solution.py:313
  70.1 0.5 spread.1.wide_ref
  70.6 2.6 %collective-permute-done.5 = f32[1,384]{1,0:T(1,128)S(1)} collective-permute-done((f32[1,384]{1,0:T(1,128)S(1)}, f32[1,384]{1,0:T(1,128)S(1)}, u32[]{:S(2)}, u32[]{:S(2)}) %collective-permute-start.5) | collective-permute-done | bytes 1568 | tf_op jit(solution)/shard_map/ppermute | solution.py:313
  73.3 32.0 %pairs.1 = (f32[384,128]{1,0:T(8,128)}, f32[384,128]{1,0:T(8,128)}) custom-call(f32[1664,1,128]{2,1,0:T(1,128)S(1)} %all-to-all-done.got_ref, f32[1664,128]{1,0:T(8,128)S(1)} %bitcast.20, f32[24,128,128]{2,1,0:T(8,128)S(1)} %spread.1.wide_ref, s32[32,128]{1,0:T(8,128)S(1)} %bitcast.28, f32[384,128]{1,0:T(8,128)S(1)} %bitcast.25, f32[3,128]{1,0:T(4,128)S(1)} %bitcast.33, ...), custom_call_target="tpu_custom_call" | custom-call | tf_op jit(solution)/shard_map/pairs/pallas_call | solution.py:404
  (33 shorter events, 0.5 us)
Async XLA Ops:
  0.6 25.6 %copy-start = (f32[3,8,16,128]{3,2,1,0:T(8,128)S(1)}, f32[3,8,16,128]{3,2,1,0:T(8,128)}, u32[]{:S(2)}) copy-start(f32[3,8,16,128]{3,2,1,0:T(8,128)} %velocity_ref.1) | copy-start | bytes 589828
  1.4 0.9 copy-start.1
  2.3 0.7 copy-start.5
  3.1 0.7 copy-start.9
  3.7 0.7 copy-start.10
  4.4 0.7 copy-start.11
  5.1 49.4 %copy-start.3 = (f32[6,8,16,128]{3,2,1,0:T(8,128)S(1)}, f32[6,8,16,128]{3,2,1,0:T(8,128)}, u32[]{:S(2)}) copy-start(f32[6,8,16,128]{3,2,1,0:T(8,128)} %stress_ref.1) | copy-start | bytes 1179652
  5.1 49.4 %copy-start.7 = (f32[8,16,128]{2,1,0:T(8,128)S(1)}, f32[8,16,128]{2,1,0:T(8,128)}, u32[]{:S(2)}) copy-start(f32[8,16,128]{2,1,0:T(8,128)} %plastic_ref.1) | copy-start | bytes 196612
  5.1 49.4 %copy-start.8 = (f32[8,16,128]{2,1,0:T(8,128)S(1)}, f32[8,16,128]{2,1,0:T(8,128)}, u32[]{:S(2)}) copy-start(f32[8,16,128]{2,1,0:T(8,128)} %yield_ref.1) | copy-start | bytes 196612
  11.4 61.8 %all-to-all-start = ((f32[1664,1,128]{2,1,0:T(1,128)}), f32[1664,1,128]{2,1,0:T(1,128)S(1)}, u32[]{:S(2)}, u32[]{:S(2)}) async-start(f32[1664,1,128]{2,1,0:T(1,128)} %get-tuple-element.28), calls=%async_computation | async-start | bytes 1703936 | tf_op jit(solution)/shard_map/all_to_all | solution.py:365
  26.6 46.7 %copy-start.2 = (f32[3,8,16,128]{3,2,1,0:T(8,128)S(1)}, f32[3,8,16,128]{3,2,1,0:T(8,128)}, u32[]{:S(2)}) copy-start(f32[3,8,16,128]{3,2,1,0:T(8,128)} %param.14) | copy-start | bytes 589828
  26.6 46.7 %copy-start.4 = (f32[8,16,128]{2,1,0:T(8,128)S(1)}, f32[8,16,128]{2,1,0:T(8,128)}, u32[]{:S(2)}) copy-start(f32[8,16,128]{2,1,0:T(8,128)} %param.15) | copy-start | bytes 196612
  26.6 46.7 %copy-start.6 = (s32[1,1,1,8,4,128]{5,4,3,2,1,0:T(4,128)S(1)}, s32[1,1,1,8,4,128]{5,4,3,2,1,0:T(4,128)}, u32[]{:S(2)}) copy-start(s32[1,1,1,8,4,128]{5,4,3,2,1,0:T(4,128)} %param.20) | copy-start | bytes 49156
  26.6 18.7 %collective-permute-start = (f32[1,384]{1,0:T(1,128)S(1)}, f32[1,384]{1,0:T(1,128)S(1)}, u32[]{:S(2)}, u32[]{:S(2)}) collective-permute-start(f32[1,384]{1,0:T(1,128)S(1)} %low_z.1), channel_id=1, source_target_pairs={{1,0},{2,1},{3,2},{4,3},{5,4},{6,5},{7,6},{9,8},{10,9},{11,10},{12... | collective-permute-start | bytes 4616 | tf_op jit(solution)/shard_map/ppermute | solution.py:313
  45.3 3.5 %collective-permute-start.1 = (f32[51,128]{1,0:T(8,128)S(1)}, f32[51,128]{1,0:T(8,128)S(1)}, u32[]{:S(2)}, u32[]{:S(2)}) collective-permute-start(f32[51,128]{1,0:T(8,128)S(1)} %pad_maximum_fusion), channel_id=1, source_target_pairs={{32,0},{64,32},{96,64},{128,96},{160,128},{192,160},{224,192},{256... | collective-permute-start | bytes 78344 | tf_op jit(solution)/shard_map/ppermute | solution.py:313
  48.8 5.7 %collective-permute-start.2 = (f32[33,128]{1,0:T(8,128)S(1)}, f32[33,128]{1,0:T(8,128)S(1)}, u32[]{:S(2)}, u32[]{:S(2)}) collective-permute-start(f32[33,128]{1,0:T(8,128)S(1)} %pad_maximum_fusion.1), channel_id=1, source_target_pairs={{8,0},{16,8},{24,16},{9,1},{17,9},{25,17},{10,2},{18,10},{26,18},{... | collective-permute-start | bytes 50696 | tf_op jit(solution)/shard_map/ppermute | solution.py:313
  55.9 6.0 %collective-permute-start.3 = (f32[6,9,128]{2,1,0:T(8,128)S(1)}, f32[6,9,128]{2,1,0:T(8,128)S(1)}, u32[]{:S(2)}, u32[]{:S(2)}) collective-permute-start(f32[6,9,128]{2,1,0:T(8,128)S(1)} %get-tuple-element.32), channel_id=1, source_target_pairs={{0,8},{8,16},{16,24},{1,9},{9,17},{17,25},{2,10},{10,18},{18,26},{... | collective-permute-start | bytes 82952 | tf_op jit(solution)/shard_map/ppermute | solution.py:313
  61.9 5.4 %collective-permute-start.4 = (f32[6,16,128]{2,1,0:T(8,128)S(1)}, f32[6,16,128]{2,1,0:T(8,128)S(1)}, u32[]{:S(2)}, u32[]{:S(2)}) collective-permute-start(f32[6,16,128]{2,1,0:T(8,128)S(1)} %scatter-add.4), channel_id=1, source_target_pairs={{0,32},{32,64},{64,96},{96,128},{128,160},{160,192},{192,224},{224... | collective-permute-start | bytes 147464 | tf_op jit(solution)/shard_map/ppermute | solution.py:313
  67.8 5.5 %collective-permute-start.5 = (f32[1,384]{1,0:T(1,128)S(1)}, f32[1,384]{1,0:T(1,128)S(1)}, u32[]{:S(2)}, u32[]{:S(2)}) collective-permute-start(f32[1,384]{1,0:T(1,128)S(1)} %get-tuple-element.35), channel_id=1, source_target_pairs={{0,1},{1,2},{2,3},{3,4},{4,5},{5,6},{6,7},{8,9},{9,10},{10,11},{11... | collective-permute-start | bytes 4616 | tf_op jit(solution)/shard_map/ppermute | solution.py:313

commit v2 on v1

--- a/solution.py
+++ b/solution.py
@@ -7,6 +7,8 @@
 
 FACETS = 128
 SLOTS = 4
+CENTER = 2.0
+GROUP = 4
 ROWS = 13
 TIME_STEP = 0.25
 SHEAR_MODULUS = 1.0
@@ -17,7 +19,7 @@
 VOIGT = ((0, 3, 5), (3, 1, 4), (5, 4, 2))
 NT = (((1,), (1,)), ((), ()))
 VMEM = pl.BlockSpec(memory_space=pltpu.VMEM)
-SMEM = pl.BlockSpec(memory_space=pltpu.SMEM)
+HBM = pl.BlockSpec(memory_space=pltpu.HBM)
 
 
 def params(mib):
@@ -47,15 +49,12 @@
     face_ref[...] = lane_pick(velocity_ref[...], 0)
 
 
-def pack_kernel(
-    disp_ref, anchor_ref, nodes_ref, source_ref, dest_ref, target_ref, cent_ref, send_ref, count, slot_target
-):
-    peers = send_ref.shape[0] // ROWS
-    pairs = source_ref.shape[0]
+def gather_kernel(disp_ref, anchor_ref, nodes_ref, cent_ref):
     high, rest = split_2(disp_ref[...])
     table = jnp.concatenate([high, rest], axis=1)
     iota = lax.broadcasted_iota(jnp.int32, (128, 4 * FACETS), 0)
-    for block in range(anchor_ref.shape[0] // 3):
+    blocks = anchor_ref.shape[0] // 3
+    for block in range(blocks):
         ids = jnp.concatenate([nodes_ref[block * 4 + m : block * 4 + m + 1, :] for m in range(4)], axis=1)
         here = jnp.where(iota == (ids & 127), 1.0, 0.0).astype(jnp.bfloat16)
         picked = jnp.dot(table, jnp.concatenate([here, here], axis=0), preferred_element_type=jnp.float32)
@@ -64,7 +63,21 @@
             kept = jnp.where(in_row, picked[c * 128 : (c + 1) * 128], 0.0)
             total = kept[:, :128] + kept[:, 128:256] + kept[:, 256:384] + kept[:, 384:]
             total = jnp.sum(total, axis=0, keepdims=True)
-            cent_ref[block * 3 + c] = anchor_ref[block * 3 + c] + 0.25 * total
+            cent_ref[block * 3 + c] = anchor_ref[c * blocks + block : c * blocks + block + 1, :] + 0.25 * total
+
+
+def place_kernel(
+    cent_ref, source_hbm, dest_hbm, target_hbm, send_ref, source_ref, dest_ref, target_ref, count, slot_target, sems
+):
+    peers = send_ref.shape[0] // ROWS
+    pairs = source_ref.shape[0]
+    copies = [
+        pltpu.make_async_copy(source_hbm, source_ref, sems.at[0]),
+        pltpu.make_async_copy(dest_hbm, dest_ref, sems.at[1]),
+        pltpu.make_async_copy(target_hbm, target_ref, sems.at[2]),
+    ]
+    for copy in copies:
+        copy.start()
     send_ref[...] = jnp.zeros(send_ref.shape, jnp.float32)
 
     def clear(peer, carry):
@@ -73,7 +86,9 @@
             slot_target[peer * SLOTS + k] = -1
         return carry
 
-    lax.fori_loop(0, peers, clear, 0)
+    lax.fori_loop(0, peers, clear, 0, unroll=4)
+    for copy in copies:
+        copy.wait()
 
     def place(pair, carry):
         dest = dest_ref[pair]
@@ -96,9 +111,22 @@
     lax.fori_loop(0, peers, write_targets, 0, unroll=4)
 
 
-def spread_kernel(cent_ref, wide_ref):
-    for r in range(wide_ref.shape[0]):
-        wide_ref[r] = jnp.broadcast_to(cent_ref[r], (FACETS, FACETS)).T
+def split_3(value):
+    high = value.astype(jnp.bfloat16).astype(jnp.float32)
+    rest = value - high
+    middle = rest.astype(jnp.bfloat16).astype(jnp.float32)
+    return high, middle, rest - middle
+
+
+def own_kernel(cent_ref, own_ref):
+    for block in range(own_ref.shape[0]):
+        x, y, z = [cent_ref[block * 3 + c] - CENTER for c in range(3)]
+        one = jnp.ones_like(x)
+        rows = [2.0 * x, 2.0 * y, 2.0 * z, one, REACH_SQUARED - (x * x + y * y + z * z)]
+        features = jnp.concatenate(rows + [jnp.zeros((3, FACETS), jnp.float32)], axis=0)
+        high, middle, low = split_3(features)
+        parts = jnp.concatenate([high, high, high, middle, middle, low, jnp.zeros((80, FACETS), jnp.float32)], axis=0)
+        own_ref[block] = parts.T.astype(jnp.bfloat16)
 
 
 def stress_kernel(
@@ -218,10 +246,9 @@
 
 
 def pair_kernel(
-    got_ref, got_rows_ref, wide_ref, nodes_ref, internal_ref, from_z_ref, velocity_ref, disp_ref, mass_ref,
-    velocity_out, disp_out, targets, target_vec, sums, slots, count, semaphore,
+    got_ref, got_rows_ref, own_ref, sums, targets, target_vec, slots, count, even, odd, semaphore
 ):
-    blocks = wide_ref.shape[0] // 3
+    blocks = own_ref.shape[0]
     peers = got_ref.shape[0] // ROWS
     target_rows = got_rows_ref[pl.ds(ROWS - 1, peers, stride=ROWS), :]
     if peers < 128:
@@ -244,44 +271,79 @@
         return carry
 
     lax.fori_loop(0, peers, sort_peer, 0, unroll=2)
+    sub = lax.broadcasted_iota(jnp.int32, (8, FACETS), 0)
 
     def one_block(block, carry):
         number = count[block]
-        for start in range(0, FACETS, 32):
-            own = [wide_ref[block * 3 + c, start : start + 32, :] for c in range(3)]
-
-            def group(step, total):
-                total = list(total)
-                for k in range(4):
-                    place = step * 4 + k
-                    inside = place < number
-                    base = slots[block * room + jnp.where(inside, place, 0)]
-                    away = jnp.where(inside, 0.0, 1.0e4)
-                    offset = [
-                        own[0] - (got_ref[base] + away), own[1] - got_ref[base + 1], own[2] - got_ref[base + 2]
-                    ]
-                    distance = offset[0] * offset[0] + offset[1] * offset[1] + offset[2] * offset[2]
-                    weight = PENALTY * jnp.maximum(REACH_SQUARED - distance, 0.0)
-                    total = [total[c] + weight * offset[c] for c in range(3)]
-                return tuple(total)
-
-            zero = jnp.zeros((32, FACETS), jnp.float32)
-            total = lax.fori_loop(0, (number + 3) >> 2, group, (zero, zero, zero))
-            for c in range(3):
-                sums[block * 3 + c, start : start + 32, :] = total[c]
+        for q in range(4):
+            sums[block * 4 + q] = jnp.zeros((FACETS, FACETS), jnp.float32)
+
+        def base_of(place):
+            inside = place < number
+            return inside, jnp.where(inside, slots[block * room + jnp.where(inside, place, 0)], 0)
+
+        def reach(step, out):
+            columns = []
+            for k in range(GROUP):
+                inside, base = base_of(step * GROUP + k)
+                x, y, z = [jnp.broadcast_to(got_ref[base + c], (8, FACETS)) - CENTER for c in range(3)]
+                away = x * x + y * y + z * z + jnp.where(inside, 0.0, 1.0e6)
+                value = jnp.where(sub == 4, 1.0, 0.0)
+                for index, part in enumerate((x, y, z, -away)):
+                    value = jnp.where(sub == index, part, value)
+                high, middle, low = split_3(value)
+                columns.append(jnp.concatenate([high, middle, low, high, middle, high], axis=0).astype(jnp.bfloat16))
+            out[...] = jnp.dot(
+                own_ref[block][:, :48], jnp.concatenate(columns, axis=1), preferred_element_type=jnp.float32
+            )
+
+        def add(step, near):
+            rows = []
+            for k in range(GROUP):
+                base = base_of(step * GROUP + k)[1]
+                rows.append([got_ref[base + c] - CENTER for c in range(3)])
+            for start in range(0, FACETS, 32):
+                part = slice(start, start + 32)
+                total = [sums[block * 4 + q, part, :] for q in range(4)]
+                for k in range(GROUP):
+                    weight = PENALTY * jnp.maximum(near[part, k * FACETS : (k + 1) * FACETS], 0.0)
+                    total[3] = total[3] + weight
+                    for c in range(3):
+                        total[c] = total[c] + weight * rows[k][c]
+                for q in range(4):
+                    sums[block * 4 + q, part, :] = total[q]
+
+        reach(0, even)
+
+        def two(step, carry):
+            reach(2 * step + 1, odd)
+            add(2 * step, even)
+            reach(2 * step + 2, even)
+            add(2 * step + 1, odd)
+            return carry
+
+        lax.fori_loop(0, (number + 2 * GROUP - 1) // (2 * GROUP), two, 0)
         return carry
 
     lax.fori_loop(0, blocks, one_block, 0)
+
+
+def scatter_kernel(sums_ref, cent_ref, nodes_ref, contact_ref):
+    blocks = cent_ref.shape[0] // 3
     ones = jnp.ones((8, FACETS), jnp.float32)
     iota = lax.broadcasted_iota(jnp.int32, (128, FACETS), 0)
     contact = jnp.zeros((384, 128), jnp.float32)
     for block in range(blocks):
         left, right = ([], [])
+        total = [
+            lax.dot_general(
+                ones, sums_ref[block * 4 + q], NT, precision=lax.Precision.HIGHEST, preferred_element_type=jnp.float32
+            )[0:1]
+            for q in range(4)
+        ]
         parts = []
         for c in range(3):
-            force = lax.dot_general(
-                ones, sums[block * 3 + c], NT, precision=lax.Precision.HIGHEST, preferred_element_type=jnp.float32
-            )[0:1]
+            force = (cent_ref[block * 3 + c] - CENTER) * total[3] - total[c]
             high, rest = split_2(0.25 * force)
             parts.append((high.astype(jnp.float32), rest.astype(jnp.float32)))
         for m in range(4):
@@ -298,12 +360,18 @@
         contact = contact + lax.dot_general(
             jnp.concatenate(left, axis=1), jnp.concatenate(right, axis=1), NT, preferred_element_type=jnp.float32
         )
+    contact_ref[...] = contact
+
+
+def update_kernel(
+    contact_ref, internal_ref, from_z_ref, velocity_ref, disp_ref, mass_ref, velocity_out, disp_out
+):
     columns = columns_of(from_z_ref[...])
     lane = lax.broadcasted_iota(jnp.int32, (128, 128), 1)
     for c in range(3):
         rows = slice(c * 128, c * 128 + 128)
         internal = internal_ref[rows, :] + jnp.where(lane == 0, columns[:, c : c + 1], 0.0)
-        velocity = velocity_ref[rows, :] + TIME_STEP * (contact[rows] - internal) / mass_ref[...]
+        velocity = velocity_ref[rows, :] + TIME_STEP * (contact_ref[rows, :] - internal) / mass_ref[...]
         velocity_out[rows, :] = velocity
         disp_out[rows, :] = disp_ref[rows, :] + TIME_STEP * velocity
 
@@ -337,35 +405,37 @@
     flat_velocity = velocity.reshape(-1, size_z)
     flat_disp = displacement.reshape(-1, size_z)
     nodes = facet_nodes.reshape(blocks * 4, FACETS)
-    anchors = facet_anchor.reshape(blocks * 3, 1, FACETS)
+    anchors = facet_anchor.reshape(blocks, 3, FACETS).transpose(1, 0, 2).reshape(3 * blocks, FACETS)
+    barrier = lax.optimization_barrier
 
     low_z = pl.pallas_call(
         low_z_kernel, out_shape=f32(1, flat_velocity.shape[0]), compiler_params=params(8), name="low_z"
     )(flat_velocity)
-    face_z = shifted(low_z, "gz", -1).reshape(3, 128)
+    face_z = shifted(low_z, "gz", -1)
+    centroids = pl.pallas_call(
+        gather_kernel, out_shape=f32(blocks * 3, 1, FACETS), compiler_params=params(16), name="gather"
+    )(flat_disp, anchors, nodes)
+    face_z, centroids = barrier((face_z, centroids))
+    face_z = face_z.reshape(3, 128)
     face_x = shifted(
         jnp.concatenate([velocity[:, 0].reshape(48, size_z), face_z], axis=0), "gx", -1
     )
-    centroids, send = pl.pallas_call(
-        pack_kernel,
-        out_shape=(f32(blocks * 3, 1, FACETS), f32(peers * ROWS, 1, FACETS)),
-        in_specs=[VMEM, VMEM, VMEM, SMEM, SMEM, SMEM],
-        out_specs=(VMEM, VMEM),
-        scratch_shapes=[pltpu.SMEM((peers,), jnp.int32), pltpu.SMEM((peers * SLOTS,), jnp.int32)],
+    send = pl.pallas_call(
+        place_kernel,
+        out_shape=f32(peers * ROWS, 1, FACETS),
+        in_specs=[VMEM, HBM, HBM, HBM],
+        out_specs=VMEM,
+        scratch_shapes=[
+            pltpu.SMEM((pairs,), jnp.int32),
+            pltpu.SMEM((pairs,), jnp.int32),
+            pltpu.SMEM((pairs,), jnp.int32),
+            pltpu.SMEM((peers,), jnp.int32),
+            pltpu.SMEM((peers * SLOTS,), jnp.int32),
+            pltpu.SemaphoreType.DMA((3,)),
+        ],
         compiler_params=params(16),
-        name="pack",
-    )(
-        flat_disp,
-        anchors,
-        nodes,
-        pair_source.reshape(pairs),
-        pair_dest.reshape(pairs),
-        pair_target.reshape(pairs),
-    )
-    got = lax.all_to_all(send, ("gx", "gz"), split_axis=0, concat_axis=0, tiled=True)
-    wide = pl.pallas_call(
-        spread_kernel, out_shape=f32(blocks * 3, FACETS, FACETS), compiler_params=params(8), name="spread"
-    )(centroids)
+        name="place",
+    )(centroids, pair_source.reshape(pairs), pair_dest.reshape(pairs), pair_target.reshape(pairs))
     face_y = shifted(
         jnp.concatenate(
             [
@@ -379,6 +449,14 @@
         "gy",
         -1,
     )
+    send, face_y, face_x = barrier((send, face_y, face_x))
+    got = lax.all_to_all(send, ("gx", "gz"), split_axis=0, concat_axis=0, tiled=True)
+    own = pl.pallas_call(
+        own_kernel,
+        out_shape=jax.ShapeDtypeStruct((blocks, FACETS, 128), jnp.bfloat16),
+        compiler_params=params(8),
+        name="own",
+    )(centroids)
     stress_new, plastic_new, upper, lower, edge_y, edge_x = pl.pallas_call(
         stress_kernel,
         out_shape=(
@@ -393,34 +471,46 @@
         name="stress",
     )(velocity, face_z, face_x, face_y, stress, plastic, yield_stress)
     from_y = shifted(edge_y, "gy", 1)
-    from_x = shifted(edge_x.at[:, 0].add(from_y[:, size_x]), "gx", 1)
+    to_x = edge_x.at[:, 0].add(from_y[:, size_x])
+    got, own, to_x = barrier((got, own, to_x))
+    from_x = shifted(to_x, "gx", 1)
+    sums = pl.pallas_call(
+        pair_kernel,
+        out_shape=f32(blocks * 4, FACETS, FACETS),
+        scratch_shapes=[
+            pltpu.SMEM((8, 128), jnp.int32),
+            pltpu.VMEM((8, 128), jnp.int32),
+            pltpu.SMEM(((blocks + 1) * SLOTS * peers,), jnp.int32),
+            pltpu.SMEM((blocks + 1,), jnp.int32),
+            pltpu.VMEM((FACETS, GROUP * FACETS), jnp.float32),
+            pltpu.VMEM((FACETS, GROUP * FACETS), jnp.float32),
+            pltpu.SemaphoreType.DMA,
+        ],
+        compiler_params=params(16),
+        cost_estimate=pl.CostEstimate(flops=2 * 10**9, bytes_accessed=2**22, transcendentals=0),
+        name="pairs",
+    )(got, got.reshape(peers * ROWS, FACETS), own)
+    from_x, sums = barrier((from_x, sums))
     internal, high_z = pl.pallas_call(
         force_kernel,
         out_shape=(f32(*velocity.shape), f32(1, flat_velocity.shape[0])),
         compiler_params=params(8),
         name="force",
     )(upper, lower, from_y, from_x)
-    from_z = shifted(high_z, "gz", 1).reshape(3, 128)
+    from_z = shifted(high_z, "gz", 1)
+    contact = pl.pallas_call(
+        scatter_kernel, out_shape=f32(384, 128), compiler_params=params(16), name="scatter"
+    )(sums, centroids, nodes)
+    from_z, contact = barrier((from_z, contact))
     velocity_new, displacement_new = pl.pallas_call(
-        pair_kernel,
+        update_kernel,
         out_shape=(f32(*flat_velocity.shape), f32(*flat_velocity.shape)),
-        scratch_shapes=[
-            pltpu.SMEM((8, 128), jnp.int32),
-            pltpu.VMEM((8, 128), jnp.int32),
-            pltpu.VMEM((blocks * 3, FACETS, FACETS), jnp.float32),
-            pltpu.SMEM(((blocks + 1) * SLOTS * peers,), jnp.int32),
-            pltpu.SMEM((blocks + 1,), jnp.int32),
-            pltpu.SemaphoreType.DMA,
-        ],
-        compiler_params=params(24),
-        name="pairs",
+        compiler_params=params(8),
+        name="update",
     )(
-        got,
-        got.reshape(peers * ROWS, FACETS),
-        wide,
-        nodes,
+        contact,
         internal.reshape(-1, size_z),
-        from_z,
+        from_z.reshape(3, 128),
         flat_velocity,
         flat_disp,
         mass.reshape(-1, size_z),

time: 106 us -> 100 us (0.943)
  the two profiles are of different devices: /device:TPU:204 before, /device:TPU:4 now
where the time goes in v2:
time: 100 us; the launch traced here: 99.8 us
  Pallas kernels  38.2 us (38%)
  starting transfers between devices  32.3 us (32%)
  waiting for transfers between devices  21.4 us (21%)
  local copies, waits for them, and re-layouts  7.02 us (7%)
    pallas_call x1, Pallas kernels, on_device(): pl.pallas_call(pair_kernel, out_shape=f32(blocks * 4, FACETS, FACETS), sc...  24 us
    all_to_all x1, starting transfers between devices, on_device(): lax.all_to_all(send, ('gx', 'gz'), split_axis=0, concat_axis=0, tiled=True)  20.3 us
    all_to_all x1, waiting for transfers between devices, on_device(): lax.all_to_all(send, ('gx', 'gz'), split_axis=0, concat_axis=0, tiled=True)  18 us
    ppermute x6, starting transfers between devices, shifted(): lax.ppermute(value, axis, [(i, i + step) for i in range(count) if 0 <= i...  12 us
    pallas_call x1, Pallas kernels, on_device(): pl.pallas_call(scatter_kernel, out_shape=f32(384, 128), compiler_params=p...  5.72 us
    unnamed x29, local copies, waits for them, and re-layouts  5.34 us
    pallas_call x1, Pallas kernels, on_device(): pl.pallas_call(place_kernel, out_shape=f32(peers * ROWS, 1, FACETS), in_s...  3.85 us
    ppermute x6, waiting for transfers between devices, shifted(): lax.ppermute(value, axis, [(i, i + step) for i in range(count) if 0 <= i...  3.33 us
  transfers between devices with their start and end apart: 7, of which 3 were waited for; matrix products, arithmetic and copies ran while one was open for 2% of the time, Pallas kernels for 37%

profile of v2, /device:TPU:4, one launch (start us, length us, event | category | flops | bytes accessed | tf_op | source)
XLA Modules:
  0.0 99.8 jit_solution(14901597462563272837)
XLA Ops:
  0.6 0.9 copy-done
  1.9 1.3 %collective-permute-start = (f32[1,384]{1,0:T(1,128)S(1)}, f32[1,384]{1,0:T(1,128)S(1)}, u32[]{:S(2)}, u32[]{:S(2)}) collective-permute-start(f32[1,384]{1,0:T(1,128)S(1)} %low_z.1), channel_id=1, source_target_pairs={{1,0},{2,1},{3,2},{4,3},{5,4},{6,5},{7,6},{9,8},{10,9},{11,10},{12... | collective-permute-start | bytes 4616 | tf_op jit(solution)/shard_map/ppermute | solution.py:381
  3.2 0.7 slice.41
  3.9 0.9 copy-done.2
  4.9 0.7 copy-done.5
  5.6 0.7 copy-done.10
  6.3 1.3 %gather.1.cent_ref = f32[24,1,128]{2,1,0:T(1,128)S(1)} custom-call(f32[384,128]{1,0:T(8,128)S(1)} %bitcast.27, f32[24,128]{1,0:T(8,128)S(1)} %bitcast.36, s32[32,128]{1,0:T(8,128)S(1)} %bitcast.30), custom_call_target="tpu_custom_call" | custom-call | tf_op jit(solution)/shard_map/gather/pallas_call | solution.py:415
  7.7 1.3 %collective-permute-start.1 = (f32[51,128]{1,0:T(8,128)S(1)}, f32[51,128]{1,0:T(8,128)S(1)}, u32[]{:S(2)}, u32[]{:S(2)}) collective-permute-start(f32[51,128]{1,0:T(8,128)S(1)} %pad_maximum_fusion), channel_id=1, source_target_pairs={{32,0},{64,32},{96,64},{128,96},{160,128},{192,160},{224,192},{256... | collective-permute-start | bytes 78344 | tf_op jit(solution)/shard_map/ppermute | solution.py:381
  9.0 0.9 slice.40
  9.9 0.9 collective-permute-done.1.face_x_ref
  10.8 2.4 %collective-permute-start.2 = (f32[33,128]{1,0:T(8,128)S(1)}, f32[33,128]{1,0:T(8,128)S(1)}, u32[]{:S(2)}, u32[]{:S(2)}) collective-permute-start(f32[33,128]{1,0:T(8,128)S(1)} %pad_maximum_fusion.1), channel_id=1, source_target_pairs={{8,0},{16,8},{24,16},{9,1},{17,9},{25,17},{10,2},{18,10},{26,18},{... | collective-permute-start | bytes 50696 | tf_op jit(solution)/shard_map/ppermute | solution.py:381
  13.9 0.7 copy-done.12
  14.6 0.7 copy-done.13
  15.3 3.8 %place.1 = f32[1664,1,128]{2,1,0:T(1,128)} custom-call(f32[24,1,128]{2,1,0:T(1,128)S(1)} %gather.1.cent_ref, s32[256]{0:T(256)S(1)} %bitcast.38, s32[256]{0:T(256)S(1)} %bitcast.39, s32[256]{0:T(256)S(1)} %bitcast.40), custom_call_target="tpu_custom_call" | custom-call | tf_op jit(solution)/shard_map/place/pallas_call | solution.py:423
  19.2 20.3 %all-to-all-start = ((f32[1664,1,128]{2,1,0:T(1,128)}), f32[1664,1,128]{2,1,0:T(1,128)S(1)}, u32[]{:S(2)}, u32[]{:S(2)}) async-start(f32[1664,1,128]{2,1,0:T(1,128)} %place.1), calls=%async_computation | async-start | bytes 1703936 | tf_op jit(solution)/shard_map/all_to_all | solution.py:453
  39.5 1.4 %stress.1 = (f32[6,8,16,128]{3,2,1,0:T(8,128)}, f32[8,16,128]{2,1,0:T(8,128)}, f32[3,8,16,128]{3,2,1,0:T(8,128)S(1)}, f32[3,8,16,128]{3,2,1,0:T(8,128)S(1)}, f32...) custom-call(f32[3,8,16,128]{3,2,1,0:T(8,128)S(1)} %copy-done.1, f32[3,128]{1,0:T(4,128)S(1)} %bitcast.35, ...), custom_call_target="tpu_custom_call" | custom-call | tf_op jit(solution)/shard_map/stress/pallas_call | solution.py:460
  40.9 3.4 %collective-permute-start.3 = (f32[6,9,128]{2,1,0:T(8,128)S(1)}, f32[6,9,128]{2,1,0:T(8,128)S(1)}, u32[]{:S(2)}, u32[]{:S(2)}) collective-permute-start(f32[6,9,128]{2,1,0:T(8,128)S(1)} %get-tuple-element.44), channel_id=1, source_target_pairs={{0,8},{8,16},{16,24},{1,9},{9,17},{17,25},{2,10},{10,18},{18,26},{... | collective-permute-start | bytes 82952 | tf_op jit(solution)/shard_map/ppermute | solution.py:381
  44.4 2.4 %collective-permute-done.3.from_y_ref = f32[6,9,128]{2,1,0:T(8,128)S(1)} collective-permute-done((f32[6,9,128]{2,1,0:T(8,128)S(1)}, f32[6,9,128]{2,1,0:T(8,128)S(1)}, u32[]{:S(2)}, u32[]{:S(2)}) %collective-permute-start.3) | collective-permute-done | bytes 27680 | tf_op jit(solution)/shard_map/ppermute | solution.py:381
  46.9 18.0 %all-to-all-done.got_ref = f32[1664,1,128]{2,1,0:T(1,128)S(1)} async-done(((f32[1664,1,128]{2,1,0:T(1,128)}), f32[1664,1,128]{2,1,0:T(1,128)S(1)}, u32[]{:S(2)}, u32[]{:S(2)}) %all-to-all-start) | async-done | bytes 852000 | tf_op jit(solution)/shard_map/all_to_all | solution.py:453
  64.9 2.3 %collective-permute-start.4 = (f32[6,16,128]{2,1,0:T(8,128)S(1)}, f32[6,16,128]{2,1,0:T(8,128)S(1)}, u32[]{:S(2)}, u32[]{:S(2)}) collective-permute-start(f32[6,16,128]{2,1,0:T(8,128)S(1)} %scatter-add.4), channel_id=1, source_target_pairs={{0,32},{32,64},{64,96},{96,128},{128,160},{160,192},{192,224},{224... | collective-permute-start | bytes 147464 | tf_op jit(solution)/shard_map/ppermute | solution.py:381
  67.3 24.0 %pairs.1.sums_ref = f32[32,128,128]{2,1,0:T(8,128)S(1)} custom-call(f32[1664,1,128]{2,1,0:T(1,128)S(1)} %all-to-all-done.got_ref, f32[1664,128]{1,0:T(8,128)S(1)} %bitcast.26, bf16[8,128,128]{2,1,0:T(8,128)(2,1)S(1)} %own.1.own_ref), custom_call_target="tpu_custom_call" | custom-call | flops 2000000000 | bytes 4194304 | tf_op jit(solution)/shard_map/pairs/pallas_call | solution.py:477
  91.8 1.3 %collective-permute-start.5 = (f32[1,384]{1,0:T(1,128)S(1)}, f32[1,384]{1,0:T(1,128)S(1)}, u32[]{:S(2)}, u32[]{:S(2)}) collective-permute-start(f32[1,384]{1,0:T(1,128)S(1)} %get-tuple-element.51), channel_id=1, source_target_pairs={{0,1},{1,2},{2,3},{3,4},{4,5},{5,6},{6,7},{8,9},{9,10},{10,11},{11... | collective-permute-start | bytes 4616 | tf_op jit(solution)/shard_map/ppermute | solution.py:381
  93.1 5.7 %scatter.1.contact_ref = f32[384,128]{1,0:T(8,128)S(1)} custom-call(f32[32,128,128]{2,1,0:T(8,128)S(1)} %pairs.1.sums_ref, f32[24,1,128]{2,1,0:T(1,128)S(1)} %gather.1.cent_ref, s32[32,128]{1,0:T(8,128)S(1)} %bitcast.31), custom_call_target="tpu_custom_call" | custom-call | tf_op jit(solution)/shard_map/scatter/pallas_call | solution.py:501
  98.8 1.0 update.1
  (39 shorter events, 1.7 us)
Async XLA Ops:
  0.6 0.9 copy-start
  1.6 37.9 %copy-start.1 = (f32[3,8,16,128]{3,2,1,0:T(8,128)S(1)}, f32[3,8,16,128]{3,2,1,0:T(8,128)}, u32[]{:S(2)}) copy-start(f32[3,8,16,128]{3,2,1,0:T(8,128)} %velocity_ref.1) | copy-start | bytes 589828
  1.9 5.7 %collective-permute-start = (f32[1,384]{1,0:T(1,128)S(1)}, f32[1,384]{1,0:T(1,128)S(1)}, u32[]{:S(2)}, u32[]{:S(2)}) collective-permute-start(f32[1,384]{1,0:T(1,128)S(1)} %low_z.1), channel_id=1, source_target_pairs={{1,0},{2,1},{3,2},{4,3},{5,4},{6,5},{7,6},{9,8},{10,9},{11,10},{12... | collective-permute-start | bytes 4616 | tf_op jit(solution)/shard_map/ppermute | solution.py:381
  3.9 0.9 copy-start.2
  4.9 0.7 copy-start.5
  5.6 0.7 copy-start.10
  6.3 33.2 %copy-start.4 = (f32[6,8,16,128]{3,2,1,0:T(8,128)S(1)}, f32[6,8,16,128]{3,2,1,0:T(8,128)}, u32[]{:S(2)}) copy-start(f32[6,8,16,128]{3,2,1,0:T(8,128)} %stress_ref.1) | copy-start | bytes 1179652
  6.3 33.2 %copy-start.7 = (f32[8,16,128]{2,1,0:T(8,128)S(1)}, f32[8,16,128]{2,1,0:T(8,128)}, u32[]{:S(2)}) copy-start(f32[8,16,128]{2,1,0:T(8,128)} %plastic_ref.1) | copy-start | bytes 196612
  6.3 33.2 %copy-start.8 = (f32[8,16,128]{2,1,0:T(8,128)S(1)}, f32[8,16,128]{2,1,0:T(8,128)}, u32[]{:S(2)}) copy-start(f32[8,16,128]{2,1,0:T(8,128)} %yield_ref.1) | copy-start | bytes 196612
  7.7 3.1 %collective-permute-start.1 = (f32[51,128]{1,0:T(8,128)S(1)}, f32[51,128]{1,0:T(8,128)S(1)}, u32[]{:S(2)}, u32[]{:S(2)}) collective-permute-start(f32[51,128]{1,0:T(8,128)S(1)} %pad_maximum_fusion), channel_id=1, source_target_pairs={{32,0},{64,32},{96,64},{128,96},{160,128},{192,160},{224,192},{256... | collective-permute-start | bytes 78344 | tf_op jit(solution)/shard_map/ppermute | solution.py:381
  10.8 8.4 %collective-permute-start.2 = (f32[33,128]{1,0:T(8,128)S(1)}, f32[33,128]{1,0:T(8,128)S(1)}, u32[]{:S(2)}, u32[]{:S(2)}) collective-permute-start(f32[33,128]{1,0:T(8,128)S(1)} %pad_maximum_fusion.1), channel_id=1, source_target_pairs={{8,0},{16,8},{24,16},{9,1},{17,9},{25,17},{10,2},{18,10},{26,18},{... | collective-permute-start | bytes 50696 | tf_op jit(solution)/shard_map/ppermute | solution.py:381
  13.2 0.7 copy-start.11
  13.9 0.7 copy-start.12
  14.6 0.7 copy-start.13
  19.2 45.8 %all-to-all-start = ((f32[1664,1,128]{2,1,0:T(1,128)}), f32[1664,1,128]{2,1,0:T(1,128)S(1)}, u32[]{:S(2)}, u32[]{:S(2)}) async-start(f32[1664,1,128]{2,1,0:T(1,128)} %place.1), calls=%async_computation | async-start | bytes 1703936 | tf_op jit(solution)/shard_map/all_to_all | solution.py:453
  40.9 6.0 %collective-permute-start.3 = (f32[6,9,128]{2,1,0:T(8,128)S(1)}, f32[6,9,128]{2,1,0:T(8,128)S(1)}, u32[]{:S(2)}, u32[]{:S(2)}) collective-permute-start(f32[6,9,128]{2,1,0:T(8,128)S(1)} %get-tuple-element.44), channel_id=1, source_target_pairs={{0,8},{8,16},{16,24},{1,9},{9,17},{17,25},{2,10},{10,18},{18,26},{... | collective-permute-start | bytes 82952 | tf_op jit(solution)/shard_map/ppermute | solution.py:381
  64.9 26.4 %collective-permute-start.4 = (f32[6,16,128]{2,1,0:T(8,128)S(1)}, f32[6,16,128]{2,1,0:T(8,128)S(1)}, u32[]{:S(2)}, u32[]{:S(2)}) collective-permute-start(f32[6,16,128]{2,1,0:T(8,128)S(1)} %scatter-add.4), channel_id=1, source_target_pairs={{0,32},{32,64},{64,96},{96,128},{128,160},{160,192},{192,224},{224... | collective-permute-start | bytes 147464 | tf_op jit(solution)/shard_map/ppermute | solution.py:381
  67.3 25.8 %copy-start.6 = (s32[1,1,1,8,4,128]{5,4,3,2,1,0:T(4,128)S(1)}, s32[1,1,1,8,4,128]{5,4,3,2,1,0:T(4,128)}, u32[]{:S(2)}) copy-start(s32[1,1,1,8,4,128]{5,4,3,2,1,0:T(4,128)} %param.20) | copy-start | bytes 49156
  91.3 7.5 %copy-start.3 = (f32[3,8,16,128]{3,2,1,0:T(8,128)S(1)}, f32[3,8,16,128]{3,2,1,0:T(8,128)}, u32[]{:S(2)}) copy-start(f32[3,8,16,128]{3,2,1,0:T(8,128)} %param.14) | copy-start | bytes 589828
  91.3 7.5 %copy-start.9 = (f32[8,16,128]{2,1,0:T(8,128)S(1)}, f32[8,16,128]{2,1,0:T(8,128)}, u32[]{:S(2)}) copy-start(f32[8,16,128]{2,1,0:T(8,128)} %param.15) | copy-start | bytes 196612
  91.8 7.0 %collective-permute-start.5 = (f32[1,384]{1,0:T(1,128)S(1)}, f32[1,384]{1,0:T(1,128)S(1)}, u32[]{:S(2)}, u32[]{:S(2)}) collective-permute-start(f32[1,384]{1,0:T(1,128)S(1)} %get-tuple-element.51), channel_id=1, source_target_pairs={{0,1},{1,2},{2,3},{3,4},{4,5},{5,6},{6,7},{8,9},{9,10},{10,11},{11... | collective-permute-start | bytes 4616 | tf_op jit(solution)/shard_map/ppermute | solution.py:381

commit v3 on v2

--- a/solution.py
+++ b/solution.py
@@ -8,7 +8,7 @@
 FACETS = 128
 SLOTS = 4
 CENTER = 2.0
-GROUP = 4
+GROUP = 8
 ROWS = 13
 TIME_STEP = 0.25
 SHEAR_MODULUS = 1.0
@@ -45,8 +45,22 @@
     return padded.T
 
 
-def low_z_kernel(velocity_ref, face_ref):
-    face_ref[...] = lane_pick(velocity_ref[...], 0)
+def rows_of(row):
+    return [row[:, c * 128 : (c + 1) * 128] for c in range(row.shape[1] // 128)]
+
+
+def faces_kernel(velocity_ref, low_z_ref, low_x_ref, low_y_ref):
+    for c in range(3):
+        planes = [velocity_ref[c, x] for x in range(velocity_ref.shape[1])]
+        low_z_ref[:, c * 128 : (c + 1) * 128] = lane_pick(jnp.concatenate(planes, axis=0), 0)
+        low_x_ref[c * 16 : (c + 1) * 16, :] = planes[0]
+        low_y_ref[c * 8 : (c + 1) * 8, :] = jnp.concatenate([plane[0:1] for plane in planes], axis=0)
+
+
+def edges_kernel(low_y_ref, face_x_ref, face_z_ref, face_xz_ref, out_ref):
+    rows = [face_x_ref[c * 16 : c * 16 + 1, :] for c in range(3)]
+    rows = rows + rows_of(face_z_ref[...]) + rows_of(face_xz_ref[...])
+    out_ref[...] = jnp.concatenate([low_y_ref[...]] + rows + [jnp.zeros((7, 128), jnp.float32)], axis=0)
 
 
 def gather_kernel(disp_ref, anchor_ref, nodes_ref, cent_ref):
@@ -78,8 +92,6 @@
     ]
     for copy in copies:
         copy.start()
-    send_ref[...] = jnp.zeros(send_ref.shape, jnp.float32)
-
     def clear(peer, carry):
         count[peer] = 0
         for k in range(SLOTS):
@@ -130,12 +142,12 @@
 
 
 def stress_kernel(
-    velocity_ref, face_z_ref, face_x_ref, face_y_ref, stress_ref, plastic_ref, yield_ref,
+    velocity_ref, face_z_ref, face_x_ref, face_xz_ref, face_y_ref, stress_ref, plastic_ref, yield_ref,
     stress_out, plastic_out, upper_out, lower_out, edge_y_out, edge_x_out,
 ):
     nx = velocity_ref.shape[1]
     columns = columns_of(
-        jnp.concatenate([face_z_ref[...], face_x_ref[48:51, :], face_y_ref[27:33, :]], axis=0)
+        jnp.concatenate(rows_of(face_z_ref[...]) + rows_of(face_xz_ref[...]) + [face_y_ref[27:33, :]], axis=0)
     )
     lane = lax.broadcasted_iota(jnp.int32, (16, 128), 1)
     row = lax.broadcasted_iota(jnp.int32, (16, 128), 0)
@@ -228,128 +240,181 @@
             before, edge_before = here, edge_here
 
 
-def force_kernel(upper_ref, lower_ref, from_y_ref, from_x_ref, internal_out, face_out):
+def force_kernel(upper_ref, edge_x_ref, from_y_ref, to_x_ref, to_z_ref, to_xz_ref):
     nx = upper_ref.shape[1]
-    lane = lax.broadcasted_iota(jnp.int32, (16, 128), 1)
     row = lax.broadcasted_iota(jnp.int32, (16, 128), 0)
+
+    def with_y(plane, c, x):
+        return plane + jnp.where(row == 0, from_y_ref[c, x : x + 1, :], 0.0)
+
+    corner = []
+    for c in range(6):
+        plane = with_y(edge_x_ref[c], c, nx)
+        to_x_ref[c] = plane
+        corner.append(plane)
+    to_xz_ref[...] = lane_pick(jnp.concatenate(corner[:3] + [jnp.zeros((80, 128), jnp.float32)], axis=0), 127)
     for c in range(3):
-        planes = []
-        for x in range(nx):
-            upper = upper_ref[c, x] + jnp.where(row == 0, from_y_ref[c, x : x + 1, :], 0.0)
-            lower = lower_ref[c, x] + jnp.where(row == 0, from_y_ref[3 + c, x : x + 1, :], 0.0)
-            if x == 0:
-                upper = upper + from_x_ref[c]
-                lower = lower + from_x_ref[3 + c]
-            planes.append(upper)
-            internal_out[c, x] = lower + jnp.where(lane == 0, 0.0, pltpu.roll(upper, 1, 1))
-        face_out[:, c * 128 : (c + 1) * 128] = lane_pick(jnp.concatenate(planes, axis=0), 127)
+        planes = [with_y(upper_ref[c, x], c, x) for x in range(nx)]
+        to_z_ref[:, c * 128 : (c + 1) * 128] = lane_pick(jnp.concatenate(planes, axis=0), 127)
 
 
 def pair_kernel(
-    got_ref, got_rows_ref, own_ref, sums, targets, target_vec, slots, count, even, odd, semaphore
+    got_ref, got_rows_ref, own_ref, sums, targets, target_vec, slots, group_block, counts, features, middle_rows,
+    even, odd, semaphore,
 ):
     blocks = own_ref.shape[0]
     peers = got_ref.shape[0] // ROWS
+    total_slots = peers * SLOTS
     target_rows = got_rows_ref[pl.ds(ROWS - 1, peers, stride=ROWS), :]
     if peers < 128:
         target_rows = jnp.concatenate([target_rows, jnp.full((128 - peers, 128), -1.0)], axis=0)
     target_vec[...] = target_rows.T[0:8, :].astype(jnp.int32)
     copy = pltpu.make_async_copy(target_vec, targets, semaphore)
     copy.start()
+    sums[...] = jnp.zeros(sums.shape, jnp.float32)
+    sub = lax.broadcasted_iota(jnp.int32, (8, FACETS), 0)
+    far = jnp.where(sub == 3, -1.0e6, 0.0)
+    features[total_slots] = jnp.concatenate([far, jnp.zeros((40, FACETS), jnp.float32)], axis=0).astype(jnp.bfloat16)
+    for k in range(SLOTS):
+        for block in range(blocks + 1):
+            counts[k][block] = 0
+    for c in range(3):
+        middle_rows[3 * total_slots + c] = jnp.zeros((1, FACETS), jnp.float32)
     copy.wait()
-    for block in range(blocks + 1):
-        count[block] = 0
-    room = SLOTS * peers
+
+    def prepare(peer, carry):
+        for k in range(SLOTS):
+            target = targets[k, peer]
+            block = jnp.where(target < 0, blocks, target)
+            counts[k][block] = counts[k][block] + 1
+            x, y, z = [
+                jnp.broadcast_to(got_ref[peer * ROWS + 3 * k + c], (8, FACETS)) - CENTER for c in range(3)
+            ]
+            away = x * x + y * y + z * z
+            value = jnp.where(sub == 4, 1.0, -away)
+            for index, part in enumerate((x, y, z)):
+                middle_rows[3 * (peer * SLOTS + k) + index] = part[0:1]
+                value = jnp.where(sub == index, part, value)
+            value = jnp.where(sub > 4, 0.0, value)
+            high, middle, low = split_3(value)
+            features[peer * SLOTS + k] = jnp.concatenate(
+                [high, middle, low, high, middle, high], axis=0
+            ).astype(jnp.bfloat16)
+        return carry
+
+    lax.fori_loop(0, peers, prepare, 0, unroll=2)
+    place = 0
+    for block in range(blocks):
+        first = place
+        for k in range(SLOTS):
+            number = counts[k][block]
+            counts[k][block] = place
+            place = place + number
+        for k in range(GROUP):
+            slots[place + k] = total_slots
+        place = (place + (GROUP - 1)) & ~(GROUP - 1)
+
+        def name_groups(group, carry):
+            group_block[group] = block
+            return carry
+
+        lax.fori_loop(first // GROUP, place // GROUP, name_groups, 0)
+    for k in range(6 * GROUP):
+        slots[place + k] = total_slots
+    for k in range(6):
+        group_block[place // GROUP + k] = 0
+    unused = unused_from(blocks, peers)
+    for k in range(SLOTS):
+        number = counts[k][blocks]
+        counts[k][blocks] = unused
+        unused = unused + number
 
     def sort_peer(peer, carry):
         for k in range(SLOTS):
             target = targets[k, peer]
             block = jnp.where(target < 0, blocks, target)
-            place = count[block]
-            count[block] = place + 1
-            slots[block * room + place] = peer * ROWS + 3 * k
+            spot = counts[k][block]
+            counts[k][block] = spot + 1
+            slots[spot] = peer * SLOTS + k
         return carry
 
     lax.fori_loop(0, peers, sort_peer, 0, unroll=2)
-    sub = lax.broadcasted_iota(jnp.int32, (8, FACETS), 0)
-
-    def one_block(block, carry):
-        number = count[block]
-        for q in range(4):
-            sums[block * 4 + q] = jnp.zeros((FACETS, FACETS), jnp.float32)
-
-        def base_of(place):
-            inside = place < number
-            return inside, jnp.where(inside, slots[block * room + jnp.where(inside, place, 0)], 0)
-
-        def reach(step, out):
-            columns = []
-            for k in range(GROUP):
-                inside, base = base_of(step * GROUP + k)
-                x, y, z = [jnp.broadcast_to(got_ref[base + c], (8, FACETS)) - CENTER for c in range(3)]
-                away = x * x + y * y + z * z + jnp.where(inside, 0.0, 1.0e6)
-                value = jnp.where(sub == 4, 1.0, 0.0)
-                for index, part in enumerate((x, y, z, -away)):
-                    value = jnp.where(sub == index, part, value)
-                high, middle, low = split_3(value)
-                columns.append(jnp.concatenate([high, middle, low, high, middle, high], axis=0).astype(jnp.bfloat16))
-            out[...] = jnp.dot(
-                own_ref[block][:, :48], jnp.concatenate(columns, axis=1), preferred_element_type=jnp.float32
+
+    def reach(step, out):
+        for half in range(2):
+            group = 2 * step + half
+            columns = [features[slots[group * GROUP + k]] for k in range(GROUP)]
+            out[:, half * GROUP * FACETS : (half + 1) * GROUP * FACETS] = jnp.dot(
+                own_ref[group_block[group]][:, :48],
+                jnp.concatenate(columns, axis=1),
+                preferred_element_type=jnp.float32,
             )
 
-        def add(step, near):
-            rows = []
-            for k in range(GROUP):
-                base = base_of(step * GROUP + k)[1]
-                rows.append([got_ref[base + c] - CENTER for c in range(3)])
+    def add(step, near):
+        for half in range(2):
+            group = 2 * step + half
+            block = group_block[group]
+            bases = [3 * slots[group * GROUP + k] for k in range(GROUP)]
             for start in range(0, FACETS, 32):
                 part = slice(start, start + 32)
                 total = [sums[block * 4 + q, part, :] for q in range(4)]
                 for k in range(GROUP):
-                    weight = PENALTY * jnp.maximum(near[part, k * FACETS : (k + 1) * FACETS], 0.0)
+                    column = (half * GROUP + k) * FACETS
+                    weight = jnp.maximum(near[part, column : column + FACETS], 0.0)
                     total[3] = total[3] + weight
                     for c in range(3):
-                        total[c] = total[c] + weight * rows[k][c]
+                        total[c] = total[c] + weight * middle_rows[bases[k] + c]
                 for q in range(4):
                     sums[block * 4 + q, part, :] = total[q]
 
-        reach(0, even)
-
-        def two(step, carry):
-            reach(2 * step + 1, odd)
-            add(2 * step, even)
-            reach(2 * step + 2, even)
-            add(2 * step + 1, odd)
-            return carry
-
-        lax.fori_loop(0, (number + 2 * GROUP - 1) // (2 * GROUP), two, 0)
+    reach(0, even)
+
+    def two(step, carry):
+        reach(2 * step + 1, odd)
+        add(2 * step, even)
+        reach(2 * step + 2, even)
+        add(2 * step + 1, odd)
         return carry
 
-    lax.fori_loop(0, blocks, one_block, 0)
+    lax.fori_loop(0, (place // GROUP + 3) // 4, two, 0)
+
+
+def unused_from(blocks, peers):
+    return SLOTS * peers + (blocks + 6) * GROUP
+
+
+def pair_scratch(blocks, peers):
+    return [
+        pltpu.SMEM((8, 128), jnp.int32),
+        pltpu.VMEM((8, 128), jnp.int32),
+        pltpu.SMEM((unused_from(blocks, peers) + SLOTS * peers,), jnp.int32),
+        pltpu.SMEM((SLOTS * peers // GROUP + blocks + 8,), jnp.int32),
+        [pltpu.SMEM((blocks + 1,), jnp.int32) for _ in range(SLOTS)],
+        pltpu.VMEM((peers * SLOTS + 1, 48, FACETS), jnp.bfloat16),
+        pltpu.VMEM((3 * peers * SLOTS + 3, 1, FACETS), jnp.float32),
+        pltpu.VMEM((FACETS, 2 * GROUP * FACETS), jnp.float32),
+        pltpu.VMEM((FACETS, 2 * GROUP * FACETS), jnp.float32),
+        pltpu.SemaphoreType.DMA,
+    ]
 
 
 def scatter_kernel(sums_ref, cent_ref, nodes_ref, contact_ref):
     blocks = cent_ref.shape[0] // 3
-    ones = jnp.ones((8, FACETS), jnp.float32)
-    iota = lax.broadcasted_iota(jnp.int32, (128, FACETS), 0)
-    contact = jnp.zeros((384, 128), jnp.float32)
+    high_iota = lax.broadcasted_iota(jnp.int32, (64, FACETS), 0)
+    low_iota = lax.broadcasted_iota(jnp.int32, (256, FACETS), 0)
+    contact = jnp.zeros((192, 256), jnp.float32)
     for block in range(blocks):
         left, right = ([], [])
-        total = [
-            lax.dot_general(
-                ones, sums_ref[block * 4 + q], NT, precision=lax.Precision.HIGHEST, preferred_element_type=jnp.float32
-            )[0:1]
-            for q in range(4)
-        ]
+        total = [jnp.sum(sums_ref[block * 4 + q].T, axis=0, keepdims=True) for q in range(4)]
         parts = []
         for c in range(3):
             force = (cent_ref[block * 3 + c] - CENTER) * total[3] - total[c]
-            high, rest = split_2(0.25 * force)
+            high, rest = split_2(0.25 * PENALTY * force)
             parts.append((high.astype(jnp.float32), rest.astype(jnp.float32)))
         for m in range(4):
             ids = nodes_ref[block * 4 + m : block * 4 + m + 1, :]
-            here = jnp.where(iota == (ids & 127), 1.0, 0.0).astype(jnp.bfloat16)
-            in_row = iota == (ids >> 7)
+            here = jnp.where(low_iota == (ids & 255), 1.0, 0.0).astype(jnp.bfloat16)
+            in_row = high_iota == (ids >> 8)
             for part in range(2):
                 left.append(
                     jnp.concatenate(
@@ -360,25 +425,48 @@
         contact = contact + lax.dot_general(
             jnp.concatenate(left, axis=1), jnp.concatenate(right, axis=1), NT, preferred_element_type=jnp.float32
         )
-    contact_ref[...] = contact
+    contact_ref[pl.ds(0, 192, stride=2), :] = contact[:, :128]
+    contact_ref[pl.ds(1, 192, stride=2), :] = contact[:, 128:]
 
 
 def update_kernel(
-    contact_ref, internal_ref, from_z_ref, velocity_ref, disp_ref, mass_ref, velocity_out, disp_out
+    contact_ref, upper_ref, lower_ref, from_y_ref, from_x_ref, from_z_ref, from_xz_ref, velocity_ref, disp_ref,
+    mass_ref, velocity_out, disp_out,
 ):
-    columns = columns_of(from_z_ref[...])
-    lane = lax.broadcasted_iota(jnp.int32, (128, 128), 1)
+    nx = velocity_ref.shape[1]
+    columns = columns_of(jnp.concatenate(rows_of(from_z_ref[...]) + [from_xz_ref[...]], axis=0))
+    lane = lax.broadcasted_iota(jnp.int32, (16, 128), 1)
+    row = lax.broadcasted_iota(jnp.int32, (16, 128), 0)
     for c in range(3):
-        rows = slice(c * 128, c * 128 + 128)
-        internal = internal_ref[rows, :] + jnp.where(lane == 0, columns[:, c : c + 1], 0.0)
-        velocity = velocity_ref[rows, :] + TIME_STEP * (contact_ref[rows, :] - internal) / mass_ref[...]
-        velocity_out[rows, :] = velocity
-        disp_out[rows, :] = disp_ref[rows, :] + TIME_STEP * velocity
+        for x in range(nx):
+            upper = upper_ref[c, x] + jnp.where(row == 0, from_y_ref[c, x : x + 1, :], 0.0)
+            lower = lower_ref[c, x] + jnp.where(row == 0, from_y_ref[3 + c, x : x + 1, :], 0.0)
+            below = columns[x * 16 : x * 16 + 16, c : c + 1]
+            if x == 0:
+                upper = upper + from_x_ref[c]
+                lower = lower + from_x_ref[3 + c]
+                below = below + columns[c * 16 : c * 16 + 16, 3:4]
+            internal = lower + jnp.where(lane == 0, below, pltpu.roll(upper, 1, 1))
+            contact = contact_ref[c * 128 + x * 16 : c * 128 + x * 16 + 16, :]
+            velocity = velocity_ref[c, x] + TIME_STEP * (contact - internal) / mass_ref[x]
+            velocity_out[c, x] = velocity
+            disp_out[c, x] = disp_ref[c, x] + TIME_STEP * velocity
 
 
 def shifted(value, axis, step):
     count = lax.axis_size(axis)
     return lax.ppermute(value, axis, [(i, i + step) for i in range(count) if 0 <= i + step < count])
+
+
+def shifted_xz(value, step):
+    count_x, count_z = lax.axis_size("gx"), lax.axis_size("gz")
+    pairs = [
+        (i * count_z + j, (i + step) * count_z + j + step)
+        for i in range(count_x)
+        for j in range(count_z)
+        if 0 <= i + step < count_x and 0 <= j + step < count_z
+    ]
+    return lax.ppermute(value, ("gx", "gz"), pairs)
 
 
 def f32(*shape):
@@ -402,24 +490,20 @@
     blocks = facet_anchor.shape[3]
     pairs = pair_source.shape[3]
     peers = lax.axis_size("gx") * lax.axis_size("gz")
-    flat_velocity = velocity.reshape(-1, size_z)
     flat_disp = displacement.reshape(-1, size_z)
     nodes = facet_nodes.reshape(blocks * 4, FACETS)
     anchors = facet_anchor.reshape(blocks, 3, FACETS).transpose(1, 0, 2).reshape(3 * blocks, FACETS)
     barrier = lax.optimization_barrier
 
-    low_z = pl.pallas_call(
-        low_z_kernel, out_shape=f32(1, flat_velocity.shape[0]), compiler_params=params(8), name="low_z"
-    )(flat_velocity)
+    low_z, low_x, low_y = pl.pallas_call(
+        faces_kernel, out_shape=(f32(1, 384), f32(48, size_z), f32(24, size_z)), compiler_params=params(8), name="faces"
+    )(velocity)
     face_z = shifted(low_z, "gz", -1)
+    face_x = shifted(low_x, "gx", -1)
+    face_xz = shifted_xz(low_z, -1)
     centroids = pl.pallas_call(
         gather_kernel, out_shape=f32(blocks * 3, 1, FACETS), compiler_params=params(16), name="gather"
     )(flat_disp, anchors, nodes)
-    face_z, centroids = barrier((face_z, centroids))
-    face_z = face_z.reshape(3, 128)
-    face_x = shifted(
-        jnp.concatenate([velocity[:, 0].reshape(48, size_z), face_z], axis=0), "gx", -1
-    )
     send = pl.pallas_call(
         place_kernel,
         out_shape=f32(peers * ROWS, 1, FACETS),
@@ -436,21 +520,12 @@
         compiler_params=params(16),
         name="place",
     )(centroids, pair_source.reshape(pairs), pair_dest.reshape(pairs), pair_target.reshape(pairs))
-    face_y = shifted(
-        jnp.concatenate(
-            [
-                velocity[:, :, 0].reshape(24, size_z),
-                face_x[:48].reshape(3, 16, size_z)[:, 0],
-                face_z,
-                face_x[48:],
-            ],
-            axis=0,
-        ),
-        "gy",
-        -1,
+    send, face_x, face_z, face_xz = barrier((send, face_x, face_z, face_xz))
+    got = lax.all_to_all(send, ("gx", "gz"), split_axis=0, concat_axis=0, tiled=True)
+    edges = pl.pallas_call(edges_kernel, out_shape=f32(40, size_z), compiler_params=params(8), name="edges")(
+        low_y, face_x, face_z, face_xz
     )
-    send, face_y, face_x = barrier((send, face_y, face_x))
-    got = lax.all_to_all(send, ("gx", "gz"), split_axis=0, concat_axis=0, tiled=True)
+    face_y = shifted(edges, "gy", -1)
     own = pl.pallas_call(
         own_kernel,
         out_shape=jax.ShapeDtypeStruct((blocks, FACETS, 128), jnp.bfloat16),
@@ -469,58 +544,35 @@
         ),
         compiler_params=params(16),
         name="stress",
-    )(velocity, face_z, face_x, face_y, stress, plastic, yield_stress)
+    )(velocity, face_z, face_x, face_xz, face_y, stress, plastic, yield_stress)
     from_y = shifted(edge_y, "gy", 1)
-    to_x = edge_x.at[:, 0].add(from_y[:, size_x])
-    got, own, to_x = barrier((got, own, to_x))
+    to_x, to_z, to_xz = pl.pallas_call(
+        force_kernel,
+        out_shape=(f32(6, size_y, size_z), f32(1, 384), f32(1, 128)),
+        compiler_params=params(8),
+        name="force",
+    )(upper, edge_x, from_y)
     from_x = shifted(to_x, "gx", 1)
+    from_z = shifted(to_z, "gz", 1)
+    from_xz = shifted_xz(to_xz, 1)
+    got, own, from_x, from_z, from_xz = barrier((got, own, from_x, from_z, from_xz))
     sums = pl.pallas_call(
         pair_kernel,
         out_shape=f32(blocks * 4, FACETS, FACETS),
-        scratch_shapes=[
-            pltpu.SMEM((8, 128), jnp.int32),
-            pltpu.VMEM((8, 128), jnp.int32),
-            pltpu.SMEM(((blocks + 1) * SLOTS * peers,), jnp.int32),
-            pltpu.SMEM((blocks + 1,), jnp.int32),
-            pltpu.VMEM((FACETS, GROUP * FACETS), jnp.float32),
-            pltpu.VMEM((FACETS, GROUP * FACETS), jnp.float32),
-            pltpu.SemaphoreType.DMA,
-        ],
-        compiler_params=params(16),
-        cost_estimate=pl.CostEstimate(flops=2 * 10**9, bytes_accessed=2**22, transcendentals=0),
+        scratch_shapes=pair_scratch(blocks, peers),
+        compiler_params=params(24),
         name="pairs",
     )(got, got.reshape(peers * ROWS, FACETS), own)
-    from_x, sums = barrier((from_x, sums))
-    internal, high_z = pl.pallas_call(
-        force_kernel,
-        out_shape=(f32(*velocity.shape), f32(1, flat_velocity.shape[0])),
-        compiler_params=params(8),
-        name="force",
-    )(upper, lower, from_y, from_x)
-    from_z = shifted(high_z, "gz", 1)
     contact = pl.pallas_call(
         scatter_kernel, out_shape=f32(384, 128), compiler_params=params(16), name="scatter"
     )(sums, centroids, nodes)
-    from_z, contact = barrier((from_z, contact))
     velocity_new, displacement_new = pl.pallas_call(
         update_kernel,
-        out_shape=(f32(*flat_velocity.shape), f32(*flat_velocity.shape)),
+        out_shape=(f32(*velocity.shape), f32(*velocity.shape)),
         compiler_params=params(8),
         name="update",
-    )(
-        contact,
-        internal.reshape(-1, size_z),
-        from_z.reshape(3, 128),
-        flat_velocity,
-        flat_disp,
-        mass.reshape(-1, size_z),
-    )
-    return (
-        velocity_new.reshape(velocity.shape),
-        displacement_new.reshape(velocity.shape),
-        stress_new,
-        plastic_new,
-    )
+    )(contact, upper, lower, from_y, from_x, from_z, from_xz, velocity, displacement, mass)
+    return (velocity_new, displacement_new, stress_new, plastic_new)
 
 
 def solution(mesh):

time: 100 us -> 84.1 us (0.84)
  the two profiles are of different devices: /device:TPU:4 before, /device:TPU:56 now
where the time goes in v3:
time: 84.1 us; the launch traced here: 83.5 us
  starting transfers between devices  31.6 us (38%)
  Pallas kernels  29.2 us (35%)
  waiting for transfers between devices  16.4 us (20%)
  local copies, waits for them, and re-layouts  5.33 us (6%)
  between operations  0.87 us (1%)
    pallas_call x1, Pallas kernels, on_device(): pl.pallas_call(pair_kernel, out_shape=f32(blocks * 4, FACETS, FACETS), sc...  19.3 us
    all_to_all x1, starting transfers between devices, on_device(): lax.all_to_all(send, ('gx', 'gz'), split_axis=0, concat_axis=0, tiled=True)  17.8 us
    ppermute x6, starting transfers between devices, shifted(): lax.ppermute(value, axis, [(i, i + step) for i in range(count) if 0 <= i...  12.5 us
    ppermute x6, waiting for transfers between devices, shifted(): lax.ppermute(value, axis, [(i, i + step) for i in range(count) if 0 <= i...  9.47 us
    all_to_all x1, waiting for transfers between devices, on_device(): lax.all_to_all(send, ('gx', 'gz'), split_axis=0, concat_axis=0, tiled=True)  6.97 us
    unnamed x28, local copies, waits for them, and re-layouts  5.33 us
    pallas_call x1, Pallas kernels, on_device(): pl.pallas_call(place_kernel, out_shape=f32(peers * ROWS, 1, FACETS), in_s...  3.46 us
  transfers between devices with their start and end apart: 9, of which 4 were waited for; matrix products, arithmetic and copies ran while one was open for 0% of the time, Pallas kernels for 8%

profile of v3, /device:TPU:56, one launch (start us, length us, event | category | flops | bytes accessed | tf_op | source)
XLA Modules:
  0.0 83.5 jit_solution(1502775883804316276)
XLA Ops:
  0.6 0.9 %copy-done = f32[3,8,16,128]{3,2,1,0:T(8,128)S(1)} copy-done((f32[3,8,16,128]{3,2,1,0:T(8,128)S(1)}, f32[3,8,16,128]{3,2,1,0:T(8,128)}, u32[]{:S(2)}) %copy-start) | copy-done | bytes 196632
  1.9 1.3 %collective-permute-start = (f32[48,128]{1,0:T(8,128)S(1)}, f32[48,128]{1,0:T(8,128)S(1)}, u32[]{:S(2)}, u32[]{:S(2)}) collective-permute-start(f32[48,128]{1,0:T(8,128)S(1)} %get-tuple-element.27), channel_id=1, source_target_pairs={{32,0},{64,32},{96,64},{128,96},{160,128},{192,160},{224,192},{256... | collective-permute-start | bytes 73736 | tf_op jit(solution)/shard_map/ppermute | solution.py:458
  3.9 3.9 %collective-permute-start.1 = (f32[1,384]{1,0:T(1,128)S(1)}, f32[1,384]{1,0:T(1,128)S(1)}, u32[]{:S(2)}, u32[]{:S(2)}) collective-permute-start(f32[1,384]{1,0:T(1,128)S(1)} %get-tuple-element.28), channel_id=1, source_target_pairs={{1,0},{2,1},{3,2},{4,3},{5,4},{6,5},{7,6},{9,8},{10,9},{11,10},{12... | collective-permute-start | bytes 4616 | tf_op jit(solution)/shard_map/ppermute | solution.py:458
  7.8 0.9 %copy-done.2 = f32[3,8,16,128]{3,2,1,0:T(8,128)S(1)} copy-done((f32[3,8,16,128]{3,2,1,0:T(8,128)S(1)}, f32[3,8,16,128]{3,2,1,0:T(8,128)}, u32[]{:S(2)}) %copy-start.2) | copy-done | bytes 196632
  8.8 0.7 copy-done.5
  9.5 0.7 copy-done.10
  10.2 1.3 %gather.1.cent_ref = f32[24,1,128]{2,1,0:T(1,128)S(1)} custom-call(f32[384,128]{1,0:T(8,128)S(1)} %bitcast.12, f32[24,128]{1,0:T(8,128)S(1)} %bitcast.15, s32[32,128]{1,0:T(8,128)S(1)} %bitcast.13), custom_call_target="tpu_custom_call" | custom-call | tf_op jit(solution)/shard_map/gather/pallas_call | solution.py:504
  11.5 0.7 copy-done.11
  12.2 0.7 copy-done.12
  12.9 0.7 copy-done.13
  13.6 3.5 %place.1 = f32[1664,1,128]{2,1,0:T(1,128)} custom-call(f32[24,1,128]{2,1,0:T(1,128)S(1)} %gather.1.cent_ref, s32[256]{0:T(256)S(1)} %bitcast.16, s32[256]{0:T(256)S(1)} %bitcast.17, s32[256]{0:T(256)S(1)} %bitcast.18), custom_call_target="tpu_custom_call" | custom-call | tf_op jit(solution)/shard_map/place/pallas_call | solution.py:507
  17.1 17.8 %all-to-all-start = ((f32[1664,1,128]{2,1,0:T(1,128)}), f32[1664,1,128]{2,1,0:T(1,128)S(1)}, u32[]{:S(2)}, u32[]{:S(2)}) async-start(f32[1664,1,128]{2,1,0:T(1,128)} %place.1), calls=%async_computation | async-start | bytes 1703936 | tf_op jit(solution)/shard_map/all_to_all | solution.py:524
  34.9 1.3 %collective-permute-start.3 = (f32[40,128]{1,0:T(8,128)S(1)}, f32[40,128]{1,0:T(8,128)S(1)}, u32[]{:S(2)}, u32[]{:S(2)}) collective-permute-start(f32[40,128]{1,0:T(8,128)S(1)} %edges.1), channel_id=1, source_target_pairs={{8,0},{16,8},{24,16},{9,1},{17,9},{25,17},{10,2},{18,10},{26,18},{... | collective-permute-start | bytes 61448 | tf_op jit(solution)/shard_map/ppermute | solution.py:458
  36.2 4.4 %collective-permute-done.3.face_y_ref = f32[40,128]{1,0:T(8,128)S(1)} collective-permute-done((f32[40,128]{1,0:T(8,128)S(1)}, f32[40,128]{1,0:T(8,128)S(1)}, u32[]{:S(2)}, u32[]{:S(2)}) %collective-permute-start.3) | collective-permute-done | bytes 20512 | tf_op jit(solution)/shard_map/ppermute | solution.py:458
  40.6 1.4 %stress.1 = (f32[6,8,16,128]{3,2,1,0:T(8,128)}, f32[8,16,128]{2,1,0:T(8,128)}, f32[3,8,16,128]{3,2,1,0:T(8,128)S(1)}, f32[3,8,16,128]{3,2,1,0:T(8,128)S(1)}, f32...) custom-call(f32[3,8,16,128]{3,2,1,0:T(8,128)S(1)} %copy-done.1, f32[1,384]{1,0:T(1,128)S(1)} %collective-permute-done.1.face_z_ref, ...), custom_call_target="tpu_custom_call" | custom-call | tf_op jit(solution)/shard_map/stress/pallas_call | solution.py:535
  42.0 3.4 %collective-permute-start.4 = (f32[6,9,128]{2,1,0:T(8,128)S(1)}, f32[6,9,128]{2,1,0:T(8,128)S(1)}, u32[]{:S(2)}, u32[]{:S(2)}) collective-permute-start(f32[6,9,128]{2,1,0:T(8,128)S(1)} %get-tuple-element.36), channel_id=1, source_target_pairs={{0,8},{8,16},{16,24},{1,9},{9,17},{17,25},{2,10},{10,18},{18,26},{... | collective-permute-start | bytes 82952 | tf_op jit(solution)/shard_map/ppermute | solution.py:458
  45.4 1.7 %collective-permute-done.4.from_y_ref = f32[6,9,128]{2,1,0:T(8,128)S(1)} collective-permute-done((f32[6,9,128]{2,1,0:T(8,128)S(1)}, f32[6,9,128]{2,1,0:T(8,128)S(1)}, u32[]{:S(2)}, u32[]{:S(2)}) %collective-permute-start.4) | collective-permute-done | bytes 27680 | tf_op jit(solution)/shard_map/ppermute | solution.py:458
  47.6 1.3 %collective-permute-start.5 = (f32[6,16,128]{2,1,0:T(8,128)S(1)}, f32[6,16,128]{2,1,0:T(8,128)S(1)}, u32[]{:S(2)}, u32[]{:S(2)}) collective-permute-start(f32[6,16,128]{2,1,0:T(8,128)S(1)} %get-tuple-element.37), channel_id=1, source_target_pairs={{0,32},{32,64},{64,96},{96,128},{128,160},{160,192},{192,224},{224... | collective-permute-start | bytes 147464 | tf_op jit(solution)/shard_map/ppermute | solution.py:458
  48.9 1.3 %collective-permute-start.6 = (f32[1,384]{1,0:T(1,128)S(1)}, f32[1,384]{1,0:T(1,128)S(1)}, u32[]{:S(2)}, u32[]{:S(2)}) collective-permute-start(f32[1,384]{1,0:T(1,128)S(1)} %get-tuple-element.38), channel_id=1, source_target_pairs={{0,1},{1,2},{2,3},{3,4},{4,5},{5,6},{6,7},{8,9},{9,10},{10,11},{11... | collective-permute-start | bytes 4616 | tf_op jit(solution)/shard_map/ppermute | solution.py:458
  51.1 3.4 %collective-permute-done.6.from_z_ref = f32[1,384]{1,0:T(1,128)S(1)} collective-permute-done((f32[1,384]{1,0:T(1,128)S(1)}, f32[1,384]{1,0:T(1,128)S(1)}, u32[]{:S(2)}, u32[]{:S(2)}) %collective-permute-start.6) | collective-permute-done | bytes 1568 | tf_op jit(solution)/shard_map/ppermute | solution.py:458
  54.4 7.0 %all-to-all-done.got_ref = f32[1664,1,128]{2,1,0:T(1,128)S(1)} async-done(((f32[1664,1,128]{2,1,0:T(1,128)}), f32[1664,1,128]{2,1,0:T(1,128)S(1)}, u32[]{:S(2)}, u32[]{:S(2)}) %all-to-all-start) | async-done | bytes 852000 | tf_op jit(solution)/shard_map/all_to_all | solution.py:524
  61.4 19.3 %pairs.1.sums_ref = f32[32,128,128]{2,1,0:T(8,128)S(1)} custom-call(f32[1664,1,128]{2,1,0:T(1,128)S(1)} %all-to-all-done.got_ref, f32[1664,128]{1,0:T(8,128)S(1)} %bitcast.11, bf16[8,128,128]{2,1,0:T(8,128)(2,1)S(1)} %own.1.own_ref), custom_call_target="tpu_custom_call" | custom-call | tf_op jit(solution)/shard_map/pairs/pallas_call | solution.py:559
  80.8 1.7 %scatter.1.contact_ref = f32[384,128]{1,0:T(8,128)S(1)} custom-call(f32[32,128,128]{2,1,0:T(8,128)S(1)} %pairs.1.sums_ref, f32[24,1,128]{2,1,0:T(1,128)S(1)} %gather.1.cent_ref, s32[32,128]{1,0:T(8,128)S(1)} %bitcast.14), custom_call_target="tpu_custom_call" | custom-call | tf_op jit(solution)/shard_map/scatter/pallas_call | solution.py:566
  82.4 1.0 %update.1 = (f32[3,8,16,128]{3,2,1,0:T(8,128)}, f32[3,8,16,128]{3,2,1,0:T(8,128)}) custom-call(f32[384,128]{1,0:T(8,128)S(1)} %scatter.1.contact_ref, f32[3,8,16,128]{3,2,1,0:T(8,128)S(1)} %get-tuple-element.34.upper_ref, f32[3,8,16,128]{3,2,1,0:T(8,128)S(1)} %get-tuple-element.42.lower_ref, f32[6,9,128]{2,1,0:T(8,128)S(1)} %collective-permute-done.4.from_y_ref, ...), custom_call_target="tpu_custom_call" | custom-call | tf_op jit(solution)/shard_map/update/pallas_call | solution.py:569
  (32 shorter events, 2.4 us)
Async XLA Ops:
  0.6 0.9 %copy-start = (f32[3,8,16,128]{3,2,1,0:T(8,128)S(1)}, f32[3,8,16,128]{3,2,1,0:T(8,128)}, u32[]{:S(2)}) copy-start(f32[3,8,16,128]{3,2,1,0:T(8,128)} %velocity_ref.5) | copy-start | bytes 589828
  1.6 39.0 %copy-start.1 = (f32[3,8,16,128]{3,2,1,0:T(8,128)S(1)}, f32[3,8,16,128]{3,2,1,0:T(8,128)}, u32[]{:S(2)}) copy-start(f32[3,8,16,128]{3,2,1,0:T(8,128)} %velocity_ref.5) | copy-start | bytes 589828
  1.9 15.1 %collective-permute-start = (f32[48,128]{1,0:T(8,128)S(1)}, f32[48,128]{1,0:T(8,128)S(1)}, u32[]{:S(2)}, u32[]{:S(2)}) collective-permute-start(f32[48,128]{1,0:T(8,128)S(1)} %get-tuple-element.27), channel_id=1, source_target_pairs={{32,0},{64,32},{96,64},{128,96},{160,128},{192,160},{224,192},{256... | collective-permute-start | bytes 73736 | tf_op jit(solution)/shard_map/ppermute | solution.py:458
  3.3 13.8 %collective-permute-start.2 = (f32[1,384]{1,0:T(1,128)S(1)}, f32[1,384]{1,0:T(1,128)S(1)}, u32[]{:S(2)}, u32[]{:S(2)}) collective-permute-start(f32[1,384]{1,0:T(1,128)S(1)} %get-tuple-element.28), channel_id=1, source_target_pairs={{33,0},{34,1},{35,2},{36,3},{37,4},{38,5},{39,6},{65,32},{66,33},{... | collective-permute-start | bytes 4616 | tf_op jit(solution)/shard_map/ppermute | solution.py:469
  3.9 13.1 %collective-permute-start.1 = (f32[1,384]{1,0:T(1,128)S(1)}, f32[1,384]{1,0:T(1,128)S(1)}, u32[]{:S(2)}, u32[]{:S(2)}) collective-permute-start(f32[1,384]{1,0:T(1,128)S(1)} %get-tuple-element.28), channel_id=1, source_target_pairs={{1,0},{2,1},{3,2},{4,3},{5,4},{6,5},{7,6},{9,8},{10,9},{11,10},{12... | collective-permute-start | bytes 4616 | tf_op jit(solution)/shard_map/ppermute | solution.py:458
  7.8 0.9 %copy-start.2 = (f32[3,8,16,128]{3,2,1,0:T(8,128)S(1)}, f32[3,8,16,128]{3,2,1,0:T(8,128)}, u32[]{:S(2)}) copy-start(f32[3,8,16,128]{3,2,1,0:T(8,128)} %disp_ref.1) | copy-start | bytes 589828
  8.8 0.7 copy-start.5
  9.5 0.7 copy-start.10
  10.2 30.4 %copy-start.4 = (f32[6,8,16,128]{3,2,1,0:T(8,128)S(1)}, f32[6,8,16,128]{3,2,1,0:T(8,128)}, u32[]{:S(2)}) copy-start(f32[6,8,16,128]{3,2,1,0:T(8,128)} %stress_ref.1) | copy-start | bytes 1179652
  10.2 30.4 %copy-start.7 = (f32[8,16,128]{2,1,0:T(8,128)S(1)}, f32[8,16,128]{2,1,0:T(8,128)}, u32[]{:S(2)}) copy-start(f32[8,16,128]{2,1,0:T(8,128)} %plastic_ref.1) | copy-start | bytes 196612
  10.2 30.4 %copy-start.8 = (f32[8,16,128]{2,1,0:T(8,128)S(1)}, f32[8,16,128]{2,1,0:T(8,128)}, u32[]{:S(2)}) copy-start(f32[8,16,128]{2,1,0:T(8,128)} %yield_ref.1) | copy-start | bytes 196612
  11.5 0.7 copy-start.11
  12.2 0.7 copy-start.12
  12.9 0.7 copy-start.13
  17.1 44.3 %all-to-all-start = ((f32[1664,1,128]{2,1,0:T(1,128)}), f32[1664,1,128]{2,1,0:T(1,128)S(1)}, u32[]{:S(2)}, u32[]{:S(2)}) async-start(f32[1664,1,128]{2,1,0:T(1,128)} %place.1), calls=%async_computation | async-start | bytes 1703936 | tf_op jit(solution)/shard_map/all_to_all | solution.py:524
  34.9 5.7 %collective-permute-start.3 = (f32[40,128]{1,0:T(8,128)S(1)}, f32[40,128]{1,0:T(8,128)S(1)}, u32[]{:S(2)}, u32[]{:S(2)}) collective-permute-start(f32[40,128]{1,0:T(8,128)S(1)} %edges.1), channel_id=1, source_target_pairs={{8,0},{16,8},{24,16},{9,1},{17,9},{25,17},{10,2},{18,10},{26,18},{... | collective-permute-start | bytes 61448 | tf_op jit(solution)/shard_map/ppermute | solution.py:458
  42.0 5.1 %collective-permute-start.4 = (f32[6,9,128]{2,1,0:T(8,128)S(1)}, f32[6,9,128]{2,1,0:T(8,128)S(1)}, u32[]{:S(2)}, u32[]{:S(2)}) collective-permute-start(f32[6,9,128]{2,1,0:T(8,128)S(1)} %get-tuple-element.36), channel_id=1, source_target_pairs={{0,8},{8,16},{16,24},{1,9},{9,17},{17,25},{2,10},{10,18},{18,26},{... | collective-permute-start | bytes 82952 | tf_op jit(solution)/shard_map/ppermute | solution.py:458
  47.6 6.8 %collective-permute-start.5 = (f32[6,16,128]{2,1,0:T(8,128)S(1)}, f32[6,16,128]{2,1,0:T(8,128)S(1)}, u32[]{:S(2)}, u32[]{:S(2)}) collective-permute-start(f32[6,16,128]{2,1,0:T(8,128)S(1)} %get-tuple-element.37), channel_id=1, source_target_pairs={{0,32},{32,64},{64,96},{96,128},{128,160},{160,192},{192,224},{224... | collective-permute-start | bytes 147464 | tf_op jit(solution)/shard_map/ppermute | solution.py:458
  48.9 5.5 %collective-permute-start.6 = (f32[1,384]{1,0:T(1,128)S(1)}, f32[1,384]{1,0:T(1,128)S(1)}, u32[]{:S(2)}, u32[]{:S(2)}) collective-permute-start(f32[1,384]{1,0:T(1,128)S(1)} %get-tuple-element.38), channel_id=1, source_target_pairs={{0,1},{1,2},{2,3},{3,4},{4,5},{5,6},{6,7},{8,9},{9,10},{10,11},{11... | collective-permute-start | bytes 4616 | tf_op jit(solution)/shard_map/ppermute | solution.py:458
  50.2 0.8 %collective-permute-start.7 = (f32[1,128]{1,0:T(1,128)S(1)}, f32[1,128]{1,0:T(1,128)S(1)}, u32[]{:S(2)}, u32[]{:S(2)}) collective-permute-start(f32[1,128]{1,0:T(1,128)S(1)} %get-tuple-element.39), channel_id=1, source_target_pairs={{0,33},{1,34},{2,35},{3,36},{4,37},{5,38},{6,39},{32,65},{33,66},{... | collective-permute-start | bytes 1544 | tf_op jit(solution)/shard_map/ppermute | solution.py:469
  51.0 29.7 %copy-start.6 = (s32[1,1,1,8,4,128]{5,4,3,2,1,0:T(4,128)S(1)}, s32[1,1,1,8,4,128]{5,4,3,2,1,0:T(4,128)}, u32[]{:S(2)}) copy-start(s32[1,1,1,8,4,128]{5,4,3,2,1,0:T(4,128)} %param.18) | copy-start | bytes 49156
  80.7 1.7 %copy-start.3 = (f32[3,8,16,128]{3,2,1,0:T(8,128)S(1)}, f32[3,8,16,128]{3,2,1,0:T(8,128)}, u32[]{:S(2)}) copy-start(f32[3,8,16,128]{3,2,1,0:T(8,128)} %disp_ref.1) | copy-start | bytes 589828
  80.8 1.7 %copy-start.9 = (f32[8,16,128]{2,1,0:T(8,128)S(1)}, f32[8,16,128]{2,1,0:T(8,128)}, u32[]{:S(2)}) copy-start(f32[8,16,128]{2,1,0:T(8,128)} %mass_ref.1) | copy-start | bytes 196612

commit v4 on v3

--- a/solution.py
+++ b/solution.py
@@ -49,21 +49,34 @@
     return [row[:, c * 128 : (c + 1) * 128] for c in range(row.shape[1] // 128)]
 
 
-def faces_kernel(velocity_ref, low_z_ref, low_x_ref, low_y_ref):
+def edges_kernel(low_y_ref, face_x_ref, face_z_ref, face_xz_ref, out_ref):
+    rows = [face_x_ref[c * 16 : c * 16 + 1, :] for c in range(3)]
+    rows = rows + rows_of(face_z_ref[...]) + rows_of(face_xz_ref[...])
+    out_ref[...] = jnp.concatenate([low_y_ref[...]] + rows + [jnp.zeros((7, 128), jnp.float32)], axis=0)
+
+
+def begin_kernel(
+    velocity_ref, disp_ref, anchor_ref, nodes_ref, source_hbm, dest_hbm, target_hbm,
+    low_z_ref, low_x_ref, low_y_ref, cent_ref, send_ref, source_ref, dest_ref, target_ref, count, slot_target, sems,
+):
+    peers = send_ref.shape[0] // ROWS
+    pairs = source_ref.shape[0]
+    copies = [
+        pltpu.make_async_copy(source_hbm, source_ref, sems.at[0]),
+        pltpu.make_async_copy(dest_hbm, dest_ref, sems.at[1]),
+        pltpu.make_async_copy(target_hbm, target_ref, sems.at[2]),
+    ]
+    for copy in copies:
+        copy.start()
+    for peer in range(peers):
+        count[peer] = 0
+    for slot in range(peers * SLOTS):
+        slot_target[slot] = -1
     for c in range(3):
         planes = [velocity_ref[c, x] for x in range(velocity_ref.shape[1])]
         low_z_ref[:, c * 128 : (c + 1) * 128] = lane_pick(jnp.concatenate(planes, axis=0), 0)
         low_x_ref[c * 16 : (c + 1) * 16, :] = planes[0]
         low_y_ref[c * 8 : (c + 1) * 8, :] = jnp.concatenate([plane[0:1] for plane in planes], axis=0)
-
-
-def edges_kernel(low_y_ref, face_x_ref, face_z_ref, face_xz_ref, out_ref):
-    rows = [face_x_ref[c * 16 : c * 16 + 1, :] for c in range(3)]
-    rows = rows + rows_of(face_z_ref[...]) + rows_of(face_xz_ref[...])
-    out_ref[...] = jnp.concatenate([low_y_ref[...]] + rows + [jnp.zeros((7, 128), jnp.float32)], axis=0)
-
-
-def gather_kernel(disp_ref, anchor_ref, nodes_ref, cent_ref):
     high, rest = split_2(disp_ref[...])
     table = jnp.concatenate([high, rest], axis=1)
     iota = lax.broadcasted_iota(jnp.int32, (128, 4 * FACETS), 0)
@@ -78,27 +91,6 @@
             total = kept[:, :128] + kept[:, 128:256] + kept[:, 256:384] + kept[:, 384:]
             total = jnp.sum(total, axis=0, keepdims=True)
             cent_ref[block * 3 + c] = anchor_ref[c * blocks + block : c * blocks + block + 1, :] + 0.25 * total
-
-
-def place_kernel(
-    cent_ref, source_hbm, dest_hbm, target_hbm, send_ref, source_ref, dest_ref, target_ref, count, slot_target, sems
-):
-    peers = send_ref.shape[0] // ROWS
-    pairs = source_ref.shape[0]
-    copies = [
-        pltpu.make_async_copy(source_hbm, source_ref, sems.at[0]),
-        pltpu.make_async_copy(dest_hbm, dest_ref, sems.at[1]),
-        pltpu.make_async_copy(target_hbm, target_ref, sems.at[2]),
-    ]
-    for copy in copies:
-        copy.start()
-    def clear(peer, carry):
-        count[peer] = 0
-        for k in range(SLOTS):
-            slot_target[peer * SLOTS + k] = -1
-        return carry
-
-    lax.fori_loop(0, peers, clear, 0, unroll=4)
     for copy in copies:
         copy.wait()
 
@@ -120,7 +112,7 @@
         send_ref[peer * ROWS + ROWS - 1] = row.astype(jnp.float32)
         return carry
 
-    lax.fori_loop(0, peers, write_targets, 0, unroll=4)
+    lax.fori_loop(0, peers, write_targets, 0, unroll=8)
 
 
 def split_3(value):
@@ -259,7 +251,7 @@
 
 
 def pair_kernel(
-    got_ref, got_rows_ref, own_ref, sums, targets, target_vec, slots, group_block, counts, features, middle_rows,
+    got_ref, got_rows_ref, own_ref, cent_ref, nodes_ref, contact_ref, sums, targets, target_vec, slots, group_block, counts, features, middle_rows,
     even, odd, semaphore,
 ):
     blocks = own_ref.shape[0]
@@ -377,6 +369,7 @@
         return carry
 
     lax.fori_loop(0, (place // GROUP + 3) // 4, two, 0)
+    scatter(sums, cent_ref, nodes_ref, contact_ref)
 
 
 def unused_from(blocks, peers):
@@ -385,6 +378,7 @@
 
 def pair_scratch(blocks, peers):
     return [
+        pltpu.VMEM((blocks * 4, FACETS, FACETS), jnp.float32),
         pltpu.SMEM((8, 128), jnp.int32),
         pltpu.VMEM((8, 128), jnp.int32),
         pltpu.SMEM((unused_from(blocks, peers) + SLOTS * peers,), jnp.int32),
@@ -398,7 +392,7 @@
     ]
 
 
-def scatter_kernel(sums_ref, cent_ref, nodes_ref, contact_ref):
+def scatter(sums_ref, cent_ref, nodes_ref, contact_ref):
     blocks = cent_ref.shape[0] // 3
     high_iota = lax.broadcasted_iota(jnp.int32, (64, FACETS), 0)
     low_iota = lax.broadcasted_iota(jnp.int32, (256, FACETS), 0)
@@ -495,20 +489,16 @@
     anchors = facet_anchor.reshape(blocks, 3, FACETS).transpose(1, 0, 2).reshape(3 * blocks, FACETS)
     barrier = lax.optimization_barrier
 
-    low_z, low_x, low_y = pl.pallas_call(
-        faces_kernel, out_shape=(f32(1, 384), f32(48, size_z), f32(24, size_z)), compiler_params=params(8), name="faces"
-    )(velocity)
-    face_z = shifted(low_z, "gz", -1)
-    face_x = shifted(low_x, "gx", -1)
-    face_xz = shifted_xz(low_z, -1)
-    centroids = pl.pallas_call(
-        gather_kernel, out_shape=f32(blocks * 3, 1, FACETS), compiler_params=params(16), name="gather"
-    )(flat_disp, anchors, nodes)
-    send = pl.pallas_call(
-        place_kernel,
-        out_shape=f32(peers * ROWS, 1, FACETS),
-        in_specs=[VMEM, HBM, HBM, HBM],
-        out_specs=VMEM,
+    low_z, low_x, low_y, centroids, send = pl.pallas_call(
+        begin_kernel,
+        out_shape=(
+            f32(1, 384),
+            f32(48, size_z),
+            f32(24, size_z),
+            f32(blocks * 3, 1, FACETS),
+            f32(peers * ROWS, 1, FACETS),
+        ),
+        in_specs=[VMEM, VMEM, VMEM, VMEM, HBM, HBM, HBM],
         scratch_shapes=[
             pltpu.SMEM((pairs,), jnp.int32),
             pltpu.SMEM((pairs,), jnp.int32),
@@ -517,9 +507,20 @@
             pltpu.SMEM((peers * SLOTS,), jnp.int32),
             pltpu.SemaphoreType.DMA((3,)),
         ],
-        compiler_params=params(16),
-        name="place",
-    )(centroids, pair_source.reshape(pairs), pair_dest.reshape(pairs), pair_target.reshape(pairs))
+        compiler_params=pltpu.CompilerParams(vmem_limit_bytes=64 * 1024 * 1024 - 128 * 1024),
+        name="begin",
+    )(
+        velocity,
+        flat_disp,
+        anchors,
+        nodes,
+        pair_source.reshape(pairs),
+        pair_dest.reshape(pairs),
+        pair_target.reshape(pairs),
+    )
+    face_z = shifted(low_z, "gz", -1)
+    face_x = shifted(low_x, "gx", -1)
+    face_xz = shifted_xz(low_z, -1)
     send, face_x, face_z, face_xz = barrier((send, face_x, face_z, face_xz))
     got = lax.all_to_all(send, ("gx", "gz"), split_axis=0, concat_axis=0, tiled=True)
     edges = pl.pallas_call(edges_kernel, out_shape=f32(40, size_z), compiler_params=params(8), name="edges")(
@@ -555,17 +556,14 @@
     from_x = shifted(to_x, "gx", 1)
     from_z = shifted(to_z, "gz", 1)
     from_xz = shifted_xz(to_xz, 1)
-    got, own, from_x, from_z, from_xz = barrier((got, own, from_x, from_z, from_xz))
-    sums = pl.pallas_call(
+    got, own, to_x, to_z, to_xz = barrier((got, own, to_x, to_z, to_xz))
+    contact = pl.pallas_call(
         pair_kernel,
-        out_shape=f32(blocks * 4, FACETS, FACETS),
+        out_shape=f32(384, 128),
         scratch_shapes=pair_scratch(blocks, peers),
         compiler_params=params(24),
         name="pairs",
-    )(got, got.reshape(peers * ROWS, FACETS), own)
-    contact = pl.pallas_call(
-        scatter_kernel, out_shape=f32(384, 128), compiler_params=params(16), name="scatter"
-    )(sums, centroids, nodes)
+    )(got, got.reshape(peers * ROWS, FACETS), own, centroids, nodes)
     velocity_new, displacement_new = pl.pallas_call(
         update_kernel,
         out_shape=(f32(*velocity.shape), f32(*velocity.shape)),

time: 84.1 us -> 80 us (0.951)
  the two profiles are of different devices: /device:TPU:56 before, /device:TPU:192 now
where the time goes in v4:
time: 80 us; the launch traced here: 79.5 us
  starting transfers between devices  36.3 us (45%)
  Pallas kernels  30.3 us (38%)
  waiting for transfers between devices  12.1 us (15%)
  between operations  0.85 us (1%)
    pallas_call x1, Pallas kernels, on_device(): pl.pallas_call(pair_kernel, out_shape=f32(384, 128), scratch_shapes=pair_...  21.7 us
    all_to_all x1, starting transfers between devices, on_device(): lax.all_to_all(send, ('gx', 'gz'), split_axis=0, concat_axis=0, tiled=True)  16.2 us
    ppermute x6, starting transfers between devices, shifted(): lax.ppermute(value, axis, [(i, i + step) for i in range(count) if 0 <= i...  13.2 us
    ppermute x6, waiting for transfers between devices, shifted(): lax.ppermute(value, axis, [(i, i + step) for i in range(count) if 0 <= i...  8.18 us
    ppermute x2, starting transfers between devices, shifted_xz(): return lax.ppermute(value, ('gx', 'gz'), pairs)  6.88 us
    pallas_call x1, Pallas kernels, on_device(): pl.pallas_call(begin_kernel, out_shape=(f32(1, 384), f32(48, size_z), f32...  5.44 us
    ppermute x2, waiting for transfers between devices, shifted_xz(): return lax.ppermute(value, ('gx', 'gz'), pairs)  2.3 us
  transfers between devices with their start and end apart: 9, of which 5 were waited for; matrix products, arithmetic and copies ran while one was open for 0% of the time, Pallas kernels for 30%

profile of v4, /device:TPU:192, one launch (start us, length us, event | category | flops | bytes accessed | tf_op | source)
XLA Modules:
  0.0 79.5 jit_solution(6933650654643161800)
XLA Ops:
  0.6 5.4 %begin.1 = (f32[1,384]{1,0:T(1,128)}, f32[48,128]{1,0:T(8,128)}, f32[24,128]{1,0:T(8,128)}, f32[24,1,128]{2,1,0:T(1,128)}, f32[1664,1,128]{2,1,0:T(1,128)}) custom-call(f32[3,8,16,128]{3,2,1,0:T(8,128)} %velocity_ref.5, f32[384,128]{1,0:T(8,128)} %bitcast.12, f32[24,128]{1,0:T(8,128)} %bitcast.15, s32[32,128]{1,0:T(8,128)} %bitcast.13, s32[256]{0:T(256)} %bitcast.16, ...), custom_call_target="tpu_custom_call" | custom-call | tf_op jit(solution)/shard_map/begin/pallas_call | solution.py:492
  6.1 0.0 copy-start.9
  6.1 1.9 %collective-permute-start = (f32[48,128]{1,0:T(8,128)}, f32[48,128]{1,0:T(8,128)S(1)}, u32[]{:S(2)}, u32[]{:S(2)}) collective-permute-start(f32[48,128]{1,0:T(8,128)} %get-tuple-element.27), channel_id=1, source_target_pairs={{32,0},{64,32},{96,64},{128,96},{160,128},{192,160},{224,192},{256... | collective-permute-start | bytes 73736 | tf_op jit(solution)/shard_map/ppermute | solution.py:452
  8.0 1.3 %collective-permute-start.2 = (f32[1,384]{1,0:T(1,128)S(1)}, f32[1,384]{1,0:T(1,128)S(1)}, u32[]{:S(2)}, u32[]{:S(2)}) collective-permute-start(f32[1,384]{1,0:T(1,128)S(1)} %copy-done.9), channel_id=1, source_target_pairs={{33,0},{34,1},{35,2},{36,3},{37,4},{38,5},{39,6},{65,32},{66,33},{... | collective-permute-start | bytes 4616 | tf_op jit(solution)/shard_map/ppermute | solution.py:463
  9.3 1.3 %collective-permute-start.1 = (f32[1,384]{1,0:T(1,128)S(1)}, f32[1,384]{1,0:T(1,128)S(1)}, u32[]{:S(2)}, u32[]{:S(2)}) collective-permute-start(f32[1,384]{1,0:T(1,128)S(1)} %copy-done.9), channel_id=1, source_target_pairs={{1,0},{2,1},{3,2},{4,3},{5,4},{6,5},{7,6},{9,8},{10,9},{11,10},{12... | collective-permute-start | bytes 4616 | tf_op jit(solution)/shard_map/ppermute | solution.py:452
  10.6 2.3 %collective-permute-done.2.face_xz_ref = f32[1,384]{1,0:T(1,128)S(1)} collective-permute-done((f32[1,384]{1,0:T(1,128)S(1)}, f32[1,384]{1,0:T(1,128)S(1)}, u32[]{:S(2)}, u32[]{:S(2)}) %collective-permute-start.2) | collective-permute-done | bytes 1568 | tf_op jit(solution)/shard_map/ppermute | solution.py:463
  12.9 2.1 %collective-permute-done.1.face_z_ref = f32[1,384]{1,0:T(1,128)S(1)} collective-permute-done((f32[1,384]{1,0:T(1,128)S(1)}, f32[1,384]{1,0:T(1,128)S(1)}, u32[]{:S(2)}, u32[]{:S(2)}) %collective-permute-start.1) | collective-permute-done | bytes 1568 | tf_op jit(solution)/shard_map/ppermute | solution.py:452
  15.0 0.0 copy-start.4
  15.0 0.0 copy-start.5
  15.0 16.2 %all-to-all-start = ((f32[1664,1,128]{2,1,0:T(1,128)}), f32[1664,1,128]{2,1,0:T(1,128)S(1)}, u32[]{:S(2)}, u32[]{:S(2)}) async-start(f32[1664,1,128]{2,1,0:T(1,128)} %get-tuple-element.29), calls=%async_computation | async-start | bytes 1703936 | tf_op jit(solution)/shard_map/all_to_all | solution.py:525
  31.3 1.3 %collective-permute-start.3 = (f32[40,128]{1,0:T(8,128)S(1)}, f32[40,128]{1,0:T(8,128)S(1)}, u32[]{:S(2)}, u32[]{:S(2)}) collective-permute-start(f32[40,128]{1,0:T(8,128)S(1)} %edges.1), channel_id=1, source_target_pairs={{8,0},{16,8},{24,16},{9,1},{17,9},{25,17},{10,2},{18,10},{26,18},{... | collective-permute-start | bytes 61448 | tf_op jit(solution)/shard_map/ppermute | solution.py:452
  32.6 4.4 %collective-permute-done.3.face_y_ref = f32[40,128]{1,0:T(8,128)S(1)} collective-permute-done((f32[40,128]{1,0:T(8,128)S(1)}, f32[40,128]{1,0:T(8,128)S(1)}, u32[]{:S(2)}, u32[]{:S(2)}) %collective-permute-start.3) | collective-permute-done | bytes 20512 | tf_op jit(solution)/shard_map/ppermute | solution.py:452
  37.0 1.4 %stress.1 = (f32[6,8,16,128]{3,2,1,0:T(8,128)}, f32[8,16,128]{2,1,0:T(8,128)}, f32[3,8,16,128]{3,2,1,0:T(8,128)S(1)}, f32[3,8,16,128]{3,2,1,0:T(8,128)S(1)}, f32...) custom-call(f32[3,8,16,128]{3,2,1,0:T(8,128)S(1)} %copy-done, f32[1,384]{1,0:T(1,128)S(1)} %collective-permute-done.1.face_z_ref, ...), custom_call_target="tpu_custom_call" | custom-call | tf_op jit(solution)/shard_map/stress/pallas_call | solution.py:536
  38.4 3.4 %collective-permute-start.4 = (f32[6,9,128]{2,1,0:T(8,128)S(1)}, f32[6,9,128]{2,1,0:T(8,128)S(1)}, u32[]{:S(2)}, u32[]{:S(2)}) collective-permute-start(f32[6,9,128]{2,1,0:T(8,128)S(1)} %get-tuple-element.37), channel_id=1, source_target_pairs={{0,8},{8,16},{16,24},{1,9},{9,17},{17,25},{2,10},{10,18},{18,26},{... | collective-permute-start | bytes 82952 | tf_op jit(solution)/shard_map/ppermute | solution.py:452
  41.8 1.7 %collective-permute-done.4.from_y_ref = f32[6,9,128]{2,1,0:T(8,128)S(1)} collective-permute-done((f32[6,9,128]{2,1,0:T(8,128)S(1)}, f32[6,9,128]{2,1,0:T(8,128)S(1)}, u32[]{:S(2)}, u32[]{:S(2)}) %collective-permute-start.4) | collective-permute-done | bytes 27680 | tf_op jit(solution)/shard_map/ppermute | solution.py:452
  43.5 0.4 force.1
  44.0 1.9 %collective-permute-start.5 = (f32[6,16,128]{2,1,0:T(8,128)S(1)}, f32[6,16,128]{2,1,0:T(8,128)S(1)}, u32[]{:S(2)}, u32[]{:S(2)}) collective-permute-start(f32[6,16,128]{2,1,0:T(8,128)S(1)} %get-tuple-element.38), channel_id=1, source_target_pairs={{0,32},{32,64},{64,96},{96,128},{128,160},{160,192},{192,224},{224... | collective-permute-start | bytes 147464 | tf_op jit(solution)/shard_map/ppermute | solution.py:452
  45.9 3.4 %collective-permute-start.6 = (f32[1,384]{1,0:T(1,128)S(1)}, f32[1,384]{1,0:T(1,128)S(1)}, u32[]{:S(2)}, u32[]{:S(2)}) collective-permute-start(f32[1,384]{1,0:T(1,128)S(1)} %get-tuple-element.39), channel_id=1, source_target_pairs={{0,1},{1,2},{2,3},{3,4},{4,5},{5,6},{6,7},{8,9},{9,10},{10,11},{11... | collective-permute-start | bytes 4616 | tf_op jit(solution)/shard_map/ppermute | solution.py:452
  49.3 5.6 %collective-permute-start.7 = (f32[1,128]{1,0:T(1,128)S(1)}, f32[1,128]{1,0:T(1,128)S(1)}, u32[]{:S(2)}, u32[]{:S(2)}) collective-permute-start(f32[1,128]{1,0:T(1,128)S(1)} %get-tuple-element.40), channel_id=1, source_target_pairs={{0,33},{1,34},{2,35},{3,36},{4,37},{5,38},{6,39},{32,65},{33,66},{... | collective-permute-start | bytes 1544 | tf_op jit(solution)/shard_map/ppermute | solution.py:463
  54.9 0.0 copy-start.3
  54.9 0.1 own.1.own_ref
  55.0 1.6 %all-to-all-done.got_ref = f32[1664,1,128]{2,1,0:T(1,128)S(1)} async-done(((f32[1664,1,128]{2,1,0:T(1,128)}), f32[1664,1,128]{2,1,0:T(1,128)S(1)}, u32[]{:S(2)}, u32[]{:S(2)}) %all-to-all-start) | async-done | bytes 852000 | tf_op jit(solution)/shard_map/all_to_all | solution.py:525
  56.6 21.7 %pairs.1.contact_ref = f32[384,128]{1,0:T(8,128)S(1)} custom-call(f32[1664,1,128]{2,1,0:T(1,128)S(1)} %all-to-all-done.got_ref, f32[1664,128]{1,0:T(8,128)S(1)} %bitcast.11, bf16[8,128,128]{2,1,0:T(8,128)(2,1)S(1)} %own.1.own_ref, f32[24,1,128]{2,1,0:T(1,128)S(1)} %copy-done.7, s32[32,128]{1,0:T(8,128)S(1)} %bitcast.14), custom_call_target="tpu_custom_call" | custom-call | tf_op jit(solution)/shard_map/pairs/pallas_call | solution.py:560
  78.4 1.0 %update.1 = (f32[3,8,16,128]{3,2,1,0:T(8,128)}, f32[3,8,16,128]{3,2,1,0:T(8,128)}) custom-call(f32[384,128]{1,0:T(8,128)S(1)} %pairs.1.contact_ref, f32[3,8,16,128]{3,2,1,0:T(8,128)S(1)} %get-tuple-element.35.upper_ref, f32[3,8,16,128]{3,2,1,0:T(8,128)S(1)} %get-tuple-element.43.lower_ref, f32[6,9,128]{2,1,0:T(8,128)S(1)} %collective-permute-done.4.from_y_ref, ...), custom_call_target="tpu_custom_call" | custom-call | tf_op jit(solution)/shard_map/update/pallas_call | solution.py:567
  (21 shorter events, 0.0 us)
Async XLA Ops:
  6.1 1.9 %copy-start.9 = (f32[1,384]{1,0:T(1,128)S(1)}, f32[1,384]{1,0:T(1,128)}, u32[]{:S(2)}) copy-start(f32[1,384]{1,0:T(1,128)} %get-tuple-element.28) | copy-start | bytes 4612
  6.1 8.9 %collective-permute-start = (f32[48,128]{1,0:T(8,128)}, f32[48,128]{1,0:T(8,128)S(1)}, u32[]{:S(2)}, u32[]{:S(2)}) collective-permute-start(f32[48,128]{1,0:T(8,128)} %get-tuple-element.27), channel_id=1, source_target_pairs={{32,0},{64,32},{96,64},{128,96},{160,128},{192,160},{224,192},{256... | collective-permute-start | bytes 73736 | tf_op jit(solution)/shard_map/ppermute | solution.py:452
  8.0 4.9 %collective-permute-start.2 = (f32[1,384]{1,0:T(1,128)S(1)}, f32[1,384]{1,0:T(1,128)S(1)}, u32[]{:S(2)}, u32[]{:S(2)}) collective-permute-start(f32[1,384]{1,0:T(1,128)S(1)} %copy-done.9), channel_id=1, source_target_pairs={{33,0},{34,1},{35,2},{36,3},{37,4},{38,5},{39,6},{65,32},{66,33},{... | collective-permute-start | bytes 4616 | tf_op jit(solution)/shard_map/ppermute | solution.py:463
  9.3 5.7 %collective-permute-start.1 = (f32[1,384]{1,0:T(1,128)S(1)}, f32[1,384]{1,0:T(1,128)S(1)}, u32[]{:S(2)}, u32[]{:S(2)}) collective-permute-start(f32[1,384]{1,0:T(1,128)S(1)} %copy-done.9), channel_id=1, source_target_pairs={{1,0},{2,1},{3,2},{4,3},{5,4},{6,5},{7,6},{9,8},{10,9},{11,10},{12... | collective-permute-start | bytes 4616 | tf_op jit(solution)/shard_map/ppermute | solution.py:452
  15.0 16.2 %copy-start.8 = (f32[24,128]{1,0:T(8,128)S(1)}, f32[24,128]{1,0:T(8,128)}, u32[]{:S(2)}) copy-start(f32[24,128]{1,0:T(8,128)} %get-tuple-element.34.low_y_ref) | copy-start | bytes 36868
  15.0 21.9 %copy-start = (f32[3,8,16,128]{3,2,1,0:T(8,128)S(1)}, f32[3,8,16,128]{3,2,1,0:T(8,128)}, u32[]{:S(2)}) copy-start(f32[3,8,16,128]{3,2,1,0:T(8,128)} %velocity_ref.5) | copy-start | bytes 589828
  15.0 21.9 %copy-start.2 = (f32[6,8,16,128]{3,2,1,0:T(8,128)S(1)}, f32[6,8,16,128]{3,2,1,0:T(8,128)}, u32[]{:S(2)}) copy-start(f32[6,8,16,128]{3,2,1,0:T(8,128)} %stress_ref.1) | copy-start | bytes 1179652
  15.0 21.9 %copy-start.4 = (f32[8,16,128]{2,1,0:T(8,128)S(1)}, f32[8,16,128]{2,1,0:T(8,128)}, u32[]{:S(2)}) copy-start(f32[8,16,128]{2,1,0:T(8,128)} %plastic_ref.1) | copy-start | bytes 196612
  15.0 21.9 %copy-start.5 = (f32[8,16,128]{2,1,0:T(8,128)S(1)}, f32[8,16,128]{2,1,0:T(8,128)}, u32[]{:S(2)}) copy-start(f32[8,16,128]{2,1,0:T(8,128)} %yield_ref.1) | copy-start | bytes 196612
  15.0 41.6 %all-to-all-start = ((f32[1664,1,128]{2,1,0:T(1,128)}), f32[1664,1,128]{2,1,0:T(1,128)S(1)}, u32[]{:S(2)}, u32[]{:S(2)}) async-start(f32[1664,1,128]{2,1,0:T(1,128)} %get-tuple-element.29), calls=%async_computation | async-start | bytes 1703936 | tf_op jit(solution)/shard_map/all_to_all | solution.py:525
  31.3 5.7 %collective-permute-start.3 = (f32[40,128]{1,0:T(8,128)S(1)}, f32[40,128]{1,0:T(8,128)S(1)}, u32[]{:S(2)}, u32[]{:S(2)}) collective-permute-start(f32[40,128]{1,0:T(8,128)S(1)} %edges.1), channel_id=1, source_target_pairs={{8,0},{16,8},{24,16},{9,1},{17,9},{25,17},{10,2},{18,10},{26,18},{... | collective-permute-start | bytes 61448 | tf_op jit(solution)/shard_map/ppermute | solution.py:452
  38.4 5.1 %collective-permute-start.4 = (f32[6,9,128]{2,1,0:T(8,128)S(1)}, f32[6,9,128]{2,1,0:T(8,128)S(1)}, u32[]{:S(2)}, u32[]{:S(2)}) collective-permute-start(f32[6,9,128]{2,1,0:T(8,128)S(1)} %get-tuple-element.37), channel_id=1, source_target_pairs={{0,8},{8,16},{16,24},{1,9},{9,17},{17,25},{2,10},{10,18},{18,26},{... | collective-permute-start | bytes 82952 | tf_op jit(solution)/shard_map/ppermute | solution.py:452
  43.5 11.4 %copy-start.7 = (f32[24,1,128]{2,1,0:T(1,128)S(1)}, f32[24,1,128]{2,1,0:T(1,128)}, u32[]{:S(2)}) copy-start(f32[24,1,128]{2,1,0:T(1,128)} %get-tuple-element.30.cent_ref) | copy-start | bytes 36868
  44.0 34.4 %collective-permute-start.5 = (f32[6,16,128]{2,1,0:T(8,128)S(1)}, f32[6,16,128]{2,1,0:T(8,128)S(1)}, u32[]{:S(2)}, u32[]{:S(2)}) collective-permute-start(f32[6,16,128]{2,1,0:T(8,128)S(1)} %get-tuple-element.38), channel_id=1, source_target_pairs={{0,32},{32,64},{64,96},{96,128},{128,160},{160,192},{192,224},{224... | collective-permute-start | bytes 147464 | tf_op jit(solution)/shard_map/ppermute | solution.py:452
  45.9 32.5 %collective-permute-start.6 = (f32[1,384]{1,0:T(1,128)S(1)}, f32[1,384]{1,0:T(1,128)S(1)}, u32[]{:S(2)}, u32[]{:S(2)}) collective-permute-start(f32[1,384]{1,0:T(1,128)S(1)} %get-tuple-element.39), channel_id=1, source_target_pairs={{0,1},{1,2},{2,3},{3,4},{4,5},{5,6},{6,7},{8,9},{9,10},{10,11},{11... | collective-permute-start | bytes 4616 | tf_op jit(solution)/shard_map/ppermute | solution.py:452
  49.3 29.1 %collective-permute-start.7 = (f32[1,128]{1,0:T(1,128)S(1)}, f32[1,128]{1,0:T(1,128)S(1)}, u32[]{:S(2)}, u32[]{:S(2)}) collective-permute-start(f32[1,128]{1,0:T(1,128)S(1)} %get-tuple-element.40), channel_id=1, source_target_pairs={{0,33},{1,34},{2,35},{3,36},{4,37},{5,38},{6,39},{32,65},{33,66},{... | collective-permute-start | bytes 1544 | tf_op jit(solution)/shard_map/ppermute | solution.py:463
  54.9 1.7 %copy-start.3 = (s32[1,1,1,8,4,128]{5,4,3,2,1,0:T(4,128)S(1)}, s32[1,1,1,8,4,128]{5,4,3,2,1,0:T(4,128)}, u32[]{:S(2)}) copy-start(s32[1,1,1,8,4,128]{5,4,3,2,1,0:T(4,128)} %param.18) | copy-start | bytes 49156
  56.6 21.8 %copy-start.1 = (f32[3,8,16,128]{3,2,1,0:T(8,128)S(1)}, f32[3,8,16,128]{3,2,1,0:T(8,128)}, u32[]{:S(2)}) copy-start(f32[3,8,16,128]{3,2,1,0:T(8,128)} %disp_ref.1) | copy-start | bytes 589828
  56.6 21.8 %copy-start.6 = (f32[8,16,128]{2,1,0:T(8,128)S(1)}, f32[8,16,128]{2,1,0:T(8,128)}, u32[]{:S(2)}) copy-start(f32[8,16,128]{2,1,0:T(8,128)} %mass_ref.1) | copy-start | bytes 196612

commit v5 on v4

--- a/solution.py
+++ b/solution.py
@@ -9,6 +9,7 @@
 SLOTS = 4
 CENTER = 2.0
 GROUP = 8
+AHEAD = 4
 ROWS = 13
 TIME_STEP = 0.25
 SHEAR_MODULUS = 1.0
@@ -55,9 +56,17 @@
     out_ref[...] = jnp.concatenate([low_y_ref[...]] + rows + [jnp.zeros((7, 128), jnp.float32)], axis=0)
 
 
+def faces_kernel(velocity_ref, low_z_ref, low_x_ref, low_y_ref):
+    for c in range(3):
+        planes = [velocity_ref[c, x] for x in range(velocity_ref.shape[1])]
+        low_z_ref[:, c * 128 : (c + 1) * 128] = lane_pick(jnp.concatenate(planes, axis=0), 0)
+        low_x_ref[c * 16 : (c + 1) * 16, :] = planes[0]
+        low_y_ref[c * 8 : (c + 1) * 8, :] = jnp.concatenate([plane[0:1] for plane in planes], axis=0)
+
+
 def begin_kernel(
-    velocity_ref, disp_ref, anchor_ref, nodes_ref, source_hbm, dest_hbm, target_hbm,
-    low_z_ref, low_x_ref, low_y_ref, cent_ref, send_ref, source_ref, dest_ref, target_ref, count, slot_target, sems,
+    disp_ref, anchor_ref, nodes_ref, source_hbm, dest_hbm, target_hbm,
+    cent_ref, send_ref, source_ref, dest_ref, target_ref, count, slot_target, sems,
 ):
     peers = send_ref.shape[0] // ROWS
     pairs = source_ref.shape[0]
@@ -72,11 +81,6 @@
         count[peer] = 0
     for slot in range(peers * SLOTS):
         slot_target[slot] = -1
-    for c in range(3):
-        planes = [velocity_ref[c, x] for x in range(velocity_ref.shape[1])]
-        low_z_ref[:, c * 128 : (c + 1) * 128] = lane_pick(jnp.concatenate(planes, axis=0), 0)
-        low_x_ref[c * 16 : (c + 1) * 16, :] = planes[0]
-        low_y_ref[c * 8 : (c + 1) * 8, :] = jnp.concatenate([plane[0:1] for plane in planes], axis=0)
     high, rest = split_2(disp_ref[...])
     table = jnp.concatenate([high, rest], axis=1)
     iota = lax.broadcasted_iota(jnp.int32, (128, 4 * FACETS), 0)
@@ -252,7 +256,7 @@
 
 def pair_kernel(
     got_ref, got_rows_ref, own_ref, cent_ref, nodes_ref, contact_ref, sums, targets, target_vec, slots, group_block, counts, features, middle_rows,
-    even, odd, semaphore,
+    near, semaphore,
 ):
     blocks = own_ref.shape[0]
     peers = got_ref.shape[0] // ROWS
@@ -260,25 +264,52 @@
     target_rows = got_rows_ref[pl.ds(ROWS - 1, peers, stride=ROWS), :]
     if peers < 128:
         target_rows = jnp.concatenate([target_rows, jnp.full((128 - peers, 128), -1.0)], axis=0)
-    target_vec[...] = target_rows.T[0:8, :].astype(jnp.int32)
+    target_rows = target_rows.T[0:8, :].astype(jnp.int32)
+    lane = lax.broadcasted_iota(jnp.int32, (8, 128), 1)
+    tally = jnp.zeros((8, 128), jnp.float32)
+    for block in range(blocks):
+        number = jnp.sum(jnp.where(target_rows == block, 1.0, 0.0), axis=1, keepdims=True)
+        tally = jnp.where(lane == block, number, tally)
+    target_vec[0:8, :] = target_rows
+    target_vec[8:16, :] = tally.astype(jnp.int32)
     copy = pltpu.make_async_copy(target_vec, targets, semaphore)
     copy.start()
     sums[...] = jnp.zeros(sums.shape, jnp.float32)
     sub = lax.broadcasted_iota(jnp.int32, (8, FACETS), 0)
     far = jnp.where(sub == 3, -1.0e6, 0.0)
     features[total_slots] = jnp.concatenate([far, jnp.zeros((40, FACETS), jnp.float32)], axis=0).astype(jnp.bfloat16)
-    for k in range(SLOTS):
-        for block in range(blocks + 1):
-            counts[k][block] = 0
     for c in range(3):
         middle_rows[3 * total_slots + c] = jnp.zeros((1, FACETS), jnp.float32)
     copy.wait()
+    place = 0
+    for block in range(blocks):
+        first = place
+        for k in range(SLOTS):
+            counts[k][block] = place
+            place = place + targets[8 + k, block]
+        for k in range(GROUP):
+            slots[place + k] = total_slots
+        place = (place + (GROUP - 1)) & ~(GROUP - 1)
+
+        def name_groups(group, carry):
+            group_block[group] = block
+            return carry
+
+        lax.fori_loop(first // GROUP, place // GROUP, name_groups, 0)
+    for k in range(2 * AHEAD * GROUP):
+        slots[place + k] = total_slots
+    for k in range(2 * AHEAD):
+        group_block[place // GROUP + k] = 0
+    for k in range(SLOTS):
+        counts[k][blocks] = unused_from(blocks, peers) + k * peers
 
     def prepare(peer, carry):
         for k in range(SLOTS):
             target = targets[k, peer]
             block = jnp.where(target < 0, blocks, target)
-            counts[k][block] = counts[k][block] + 1
+            spot = counts[k][block]
+            counts[k][block] = spot + 1
+            slots[spot] = peer * SLOTS + k
             x, y, z = [
                 jnp.broadcast_to(got_ref[peer * ROWS + 3 * k + c], (8, FACETS)) - CENTER for c in range(3)
             ]
@@ -295,99 +326,55 @@
         return carry
 
     lax.fori_loop(0, peers, prepare, 0, unroll=2)
-    place = 0
-    for block in range(blocks):
-        first = place
-        for k in range(SLOTS):
-            number = counts[k][block]
-            counts[k][block] = place
-            place = place + number
-        for k in range(GROUP):
-            slots[place + k] = total_slots
-        place = (place + (GROUP - 1)) & ~(GROUP - 1)
-
-        def name_groups(group, carry):
-            group_block[group] = block
-            return carry
-
-        lax.fori_loop(first // GROUP, place // GROUP, name_groups, 0)
-    for k in range(6 * GROUP):
-        slots[place + k] = total_slots
-    for k in range(6):
-        group_block[place // GROUP + k] = 0
-    unused = unused_from(blocks, peers)
-    for k in range(SLOTS):
-        number = counts[k][blocks]
-        counts[k][blocks] = unused
-        unused = unused + number
-
-    def sort_peer(peer, carry):
-        for k in range(SLOTS):
-            target = targets[k, peer]
-            block = jnp.where(target < 0, blocks, target)
-            spot = counts[k][block]
-            counts[k][block] = spot + 1
-            slots[spot] = peer * SLOTS + k
+
+    def reach(group, out):
+        columns = [features[slots[group * GROUP + k]] for k in range(GROUP)]
+        out[...] = jnp.dot(
+            own_ref[group_block[group]][:, :48], jnp.concatenate(columns, axis=1), preferred_element_type=jnp.float32
+        )
+
+    def add(group, near):
+        block = group_block[group]
+        bases = [3 * slots[group * GROUP + k] for k in range(GROUP)]
+        for start in range(0, FACETS, 32):
+            part = slice(start, start + 32)
+            total = [sums[block * 4 + q, part, :] for q in range(4)]
+            for k in range(GROUP):
+                weight = jnp.maximum(near[part, k * FACETS : (k + 1) * FACETS], 0.0)
+                total[3] = total[3] + weight
+                for c in range(3):
+                    total[c] = total[c] + weight * middle_rows[bases[k] + c]
+            for q in range(4):
+                sums[block * 4 + q, part, :] = total[q]
+
+    for i in range(AHEAD):
+        reach(i, near[i])
+
+    def some(step, carry):
+        for i in range(AHEAD):
+            add(step * AHEAD + i, near[i])
+            reach((step + 1) * AHEAD + i, near[i])
         return carry
 
-    lax.fori_loop(0, peers, sort_peer, 0, unroll=2)
-
-    def reach(step, out):
-        for half in range(2):
-            group = 2 * step + half
-            columns = [features[slots[group * GROUP + k]] for k in range(GROUP)]
-            out[:, half * GROUP * FACETS : (half + 1) * GROUP * FACETS] = jnp.dot(
-                own_ref[group_block[group]][:, :48],
-                jnp.concatenate(columns, axis=1),
-                preferred_element_type=jnp.float32,
-            )
-
-    def add(step, near):
-        for half in range(2):
-            group = 2 * step + half
-            block = group_block[group]
-            bases = [3 * slots[group * GROUP + k] for k in range(GROUP)]
-            for start in range(0, FACETS, 32):
-                part = slice(start, start + 32)
-                total = [sums[block * 4 + q, part, :] for q in range(4)]
-                for k in range(GROUP):
-                    column = (half * GROUP + k) * FACETS
-                    weight = jnp.maximum(near[part, column : column + FACETS], 0.0)
-                    total[3] = total[3] + weight
-                    for c in range(3):
-                        total[c] = total[c] + weight * middle_rows[bases[k] + c]
-                for q in range(4):
-                    sums[block * 4 + q, part, :] = total[q]
-
-    reach(0, even)
-
-    def two(step, carry):
-        reach(2 * step + 1, odd)
-        add(2 * step, even)
-        reach(2 * step + 2, even)
-        add(2 * step + 1, odd)
-        return carry
-
-    lax.fori_loop(0, (place // GROUP + 3) // 4, two, 0)
+    lax.fori_loop(0, (place // GROUP + (AHEAD - 1)) // AHEAD, some, 0)
     scatter(sums, cent_ref, nodes_ref, contact_ref)
 
 
 def unused_from(blocks, peers):
-    return SLOTS * peers + (blocks + 6) * GROUP
+    return SLOTS * peers + (blocks + 2 * AHEAD) * GROUP
 
 
 def pair_scratch(blocks, peers):
     return [
         pltpu.VMEM((blocks * 4, FACETS, FACETS), jnp.float32),
-        pltpu.SMEM((8, 128), jnp.int32),
-        pltpu.VMEM((8, 128), jnp.int32),
+        pltpu.SMEM((16, 128), jnp.int32),
+        pltpu.VMEM((16, 128), jnp.int32),
         pltpu.SMEM((unused_from(blocks, peers) + SLOTS * peers,), jnp.int32),
-        pltpu.SMEM((SLOTS * peers // GROUP + blocks + 8,), jnp.int32),
+        pltpu.SMEM((SLOTS * peers // GROUP + blocks + 2 * AHEAD,), jnp.int32),
         [pltpu.SMEM((blocks + 1,), jnp.int32) for _ in range(SLOTS)],
         pltpu.VMEM((peers * SLOTS + 1, 48, FACETS), jnp.bfloat16),
         pltpu.VMEM((3 * peers * SLOTS + 3, 1, FACETS), jnp.float32),
-        pltpu.VMEM((FACETS, 2 * GROUP * FACETS), jnp.float32),
-        pltpu.VMEM((FACETS, 2 * GROUP * FACETS), jnp.float32),
+        [pltpu.VMEM((FACETS, GROUP * FACETS), jnp.float32) for _ in range(AHEAD)],
         pltpu.SemaphoreType.DMA,
     ]
 
@@ -489,16 +476,16 @@
     anchors = facet_anchor.reshape(blocks, 3, FACETS).transpose(1, 0, 2).reshape(3 * blocks, FACETS)
     barrier = lax.optimization_barrier
 
-    low_z, low_x, low_y, centroids, send = pl.pallas_call(
+    low_z, low_x, low_y = pl.pallas_call(
+        faces_kernel, out_shape=(f32(1, 384), f32(48, size_z), f32(24, size_z)), compiler_params=params(8), name="faces"
+    )(velocity)
+    centroids, send = pl.pallas_call(
         begin_kernel,
         out_shape=(
-            f32(1, 384),
-            f32(48, size_z),
-            f32(24, size_z),
             f32(blocks * 3, 1, FACETS),
             f32(peers * ROWS, 1, FACETS),
         ),
-        in_specs=[VMEM, VMEM, VMEM, VMEM, HBM, HBM, HBM],
+        in_specs=[VMEM, VMEM, VMEM, HBM, HBM, HBM],
         scratch_shapes=[
             pltpu.SMEM((pairs,), jnp.int32),
             pltpu.SMEM((pairs,), jnp.int32),
@@ -510,7 +497,6 @@
         compiler_params=pltpu.CompilerParams(vmem_limit_bytes=64 * 1024 * 1024 - 128 * 1024),
         name="begin",
     )(
-        velocity,
         flat_disp,
         anchors,
         nodes,

time: 80 us -> 76.1 us (0.951)
  the two profiles are of different devices: /device:TPU:192 before, /device:TPU:128 now
where the time goes in v5:
time: 76.1 us; the launch traced here: 75.6 us
  starting transfers between devices  37.2 us (49%)
  Pallas kernels  26.7 us (35%)
  waiting for transfers between devices  9.82 us (13%)
  local copies, waits for them, and re-layouts  0.96 us (1%)
  between operations  0.87 us (1%)
    all_to_all x1, starting transfers between devices, on_device(): lax.all_to_all(send, ('gx', 'gz'), split_axis=0, concat_axis=0, tiled=True)  18.3 us
    pallas_call x1, Pallas kernels, on_device(): pl.pallas_call(pair_kernel, out_shape=f32(384, 128), scratch_shapes=pair_...  18 us
    ppermute x6, starting transfers between devices, shifted(): lax.ppermute(value, axis, [(i, i + step) for i in range(count) if 0 <= i...  13.2 us
    ppermute x6, waiting for transfers between devices, shifted(): lax.ppermute(value, axis, [(i, i + step) for i in range(count) if 0 <= i...  6.12 us
    ppermute x2, starting transfers between devices, shifted_xz(): return lax.ppermute(value, ('gx', 'gz'), pairs)  5.67 us
    pallas_call x1, Pallas kernels, on_device(): pl.pallas_call(begin_kernel, out_shape=(f32(blocks * 3, 1, FACETS), f32(p...  5.07 us
    all_to_all x1, waiting for transfers between devices, on_device(): lax.all_to_all(send, ('gx', 'gz'), split_axis=0, concat_axis=0, tiled=True)  3.69 us
  transfers between devices with their start and end apart: 9, of which 3 were waited for; matrix products, arithmetic and copies ran while one was open for 0% of the time, Pallas kernels for 33%

profile of v5, /device:TPU:128, one launch (start us, length us, event | category | flops | bytes accessed | tf_op | source)
XLA Modules:
  0.0 75.6 jit_solution(3869882449875312936)
XLA Ops:
  0.6 0.0 copy-start
  0.6 0.9 %copy-done = f32[3,8,16,128]{3,2,1,0:T(8,128)S(1)} copy-done((f32[3,8,16,128]{3,2,1,0:T(8,128)S(1)}, f32[3,8,16,128]{3,2,1,0:T(8,128)}, u32[]{:S(2)}) %copy-start) | copy-done | bytes 196632
  1.6 0.6 faces.1
  2.2 1.9 %collective-permute-start = (f32[48,128]{1,0:T(8,128)}, f32[48,128]{1,0:T(8,128)S(1)}, u32[]{:S(2)}, u32[]{:S(2)}) collective-permute-start(f32[48,128]{1,0:T(8,128)} %get-tuple-element.27), channel_id=1, source_target_pairs={{32,0},{64,32},{96,64},{128,96},{160,128},{192,160},{224,192},{256... | collective-permute-start | bytes 73736 | tf_op jit(solution)/shard_map/ppermute | solution.py:439
  4.1 1.3 %collective-permute-start.2 = (f32[1,384]{1,0:T(1,128)S(1)}, f32[1,384]{1,0:T(1,128)S(1)}, u32[]{:S(2)}, u32[]{:S(2)}) collective-permute-start(f32[1,384]{1,0:T(1,128)S(1)} %get-tuple-element.28), channel_id=1, source_target_pairs={{33,0},{34,1},{35,2},{36,3},{37,4},{38,5},{39,6},{65,32},{66,33},{... | collective-permute-start | bytes 4616 | tf_op jit(solution)/shard_map/ppermute | solution.py:450
  5.4 1.3 %collective-permute-start.1 = (f32[1,384]{1,0:T(1,128)S(1)}, f32[1,384]{1,0:T(1,128)S(1)}, u32[]{:S(2)}, u32[]{:S(2)}) collective-permute-start(f32[1,384]{1,0:T(1,128)S(1)} %get-tuple-element.28), channel_id=1, source_target_pairs={{1,0},{2,1},{3,2},{4,3},{5,4},{6,5},{7,6},{9,8},{10,9},{11,10},{12... | collective-permute-start | bytes 4616 | tf_op jit(solution)/shard_map/ppermute | solution.py:439
  6.7 5.1 %begin.1 = (f32[24,1,128]{2,1,0:T(1,128)}, f32[1664,1,128]{2,1,0:T(1,128)}) custom-call(f32[384,128]{1,0:T(8,128)} %bitcast.12, f32[24,128]{1,0:T(8,128)} %bitcast.15, s32[32,128]{1,0:T(8,128)} %bitcast.13, s32[256]{0:T(256)} %bitcast.16, s32[256]{0:T(256)} %bitcast.17, s32[256]{0:T(256)} %bitcast.18), custom_call_target="tpu_custom_call" | custom-call | tf_op jit(solution)/shard_map/begin/pallas_call | solution.py:482
  11.8 0.0 copy-start.1
  11.8 0.0 copy-start.3
  11.9 18.3 %all-to-all-start = ((f32[1664,1,128]{2,1,0:T(1,128)}), f32[1664,1,128]{2,1,0:T(1,128)S(1)}, u32[]{:S(2)}, u32[]{:S(2)}) async-start(f32[1664,1,128]{2,1,0:T(1,128)} %get-tuple-element.29), calls=%async_computation | async-start | bytes 1703936 | tf_op jit(solution)/shard_map/all_to_all | solution.py:511
  30.2 1.3 %collective-permute-start.3 = (f32[40,128]{1,0:T(8,128)S(1)}, f32[40,128]{1,0:T(8,128)S(1)}, u32[]{:S(2)}, u32[]{:S(2)}) collective-permute-start(f32[40,128]{1,0:T(8,128)S(1)} %edges.1), channel_id=1, source_target_pairs={{8,0},{16,8},{24,16},{9,1},{17,9},{25,17},{10,2},{18,10},{26,18},{... | collective-permute-start | bytes 61448 | tf_op jit(solution)/shard_map/ppermute | solution.py:439
  31.5 4.4 %collective-permute-done.3.face_y_ref = f32[40,128]{1,0:T(8,128)S(1)} collective-permute-done((f32[40,128]{1,0:T(8,128)S(1)}, f32[40,128]{1,0:T(8,128)S(1)}, u32[]{:S(2)}, u32[]{:S(2)}) %collective-permute-start.3) | collective-permute-done | bytes 20512 | tf_op jit(solution)/shard_map/ppermute | solution.py:439
  35.9 1.4 %stress.1 = (f32[6,8,16,128]{3,2,1,0:T(8,128)}, f32[8,16,128]{2,1,0:T(8,128)}, f32[3,8,16,128]{3,2,1,0:T(8,128)S(1)}, f32[3,8,16,128]{3,2,1,0:T(8,128)S(1)}, f32...) custom-call(f32[3,8,16,128]{3,2,1,0:T(8,128)S(1)} %copy-done.1, f32[1,384]{1,0:T(1,128)S(1)} %collective-permute-done.1.face_z_ref, ...), custom_call_target="tpu_custom_call" | custom-call | tf_op jit(solution)/shard_map/stress/pallas_call | solution.py:522
  37.4 3.4 %collective-permute-start.4 = (f32[6,9,128]{2,1,0:T(8,128)S(1)}, f32[6,9,128]{2,1,0:T(8,128)S(1)}, u32[]{:S(2)}, u32[]{:S(2)}) collective-permute-start(f32[6,9,128]{2,1,0:T(8,128)S(1)} %get-tuple-element.37), channel_id=1, source_target_pairs={{0,8},{8,16},{16,24},{1,9},{9,17},{17,25},{2,10},{10,18},{18,26},{... | collective-permute-start | bytes 82952 | tf_op jit(solution)/shard_map/ppermute | solution.py:439
  40.8 1.7 %collective-permute-done.4.from_y_ref = f32[6,9,128]{2,1,0:T(8,128)S(1)} collective-permute-done((f32[6,9,128]{2,1,0:T(8,128)S(1)}, f32[6,9,128]{2,1,0:T(8,128)S(1)}, u32[]{:S(2)}, u32[]{:S(2)}) %collective-permute-start.4) | collective-permute-done | bytes 27680 | tf_op jit(solution)/shard_map/ppermute | solution.py:439
  42.5 0.4 force.1
  42.9 1.9 %collective-permute-start.5 = (f32[6,16,128]{2,1,0:T(8,128)S(1)}, f32[6,16,128]{2,1,0:T(8,128)S(1)}, u32[]{:S(2)}, u32[]{:S(2)}) collective-permute-start(f32[6,16,128]{2,1,0:T(8,128)S(1)} %get-tuple-element.38), channel_id=1, source_target_pairs={{0,32},{32,64},{64,96},{96,128},{128,160},{160,192},{192,224},{224... | collective-permute-start | bytes 147464 | tf_op jit(solution)/shard_map/ppermute | solution.py:439
  44.9 3.4 %collective-permute-start.6 = (f32[1,384]{1,0:T(1,128)S(1)}, f32[1,384]{1,0:T(1,128)S(1)}, u32[]{:S(2)}, u32[]{:S(2)}) collective-permute-start(f32[1,384]{1,0:T(1,128)S(1)} %get-tuple-element.39), channel_id=1, source_target_pairs={{0,1},{1,2},{2,3},{3,4},{4,5},{5,6},{6,7},{8,9},{9,10},{10,11},{11... | collective-permute-start | bytes 4616 | tf_op jit(solution)/shard_map/ppermute | solution.py:439
  48.2 4.4 %collective-permute-start.7 = (f32[1,128]{1,0:T(1,128)S(1)}, f32[1,128]{1,0:T(1,128)S(1)}, u32[]{:S(2)}, u32[]{:S(2)}) collective-permute-start(f32[1,128]{1,0:T(1,128)S(1)} %get-tuple-element.40), channel_id=1, source_target_pairs={{0,33},{1,34},{2,35},{3,36},{4,37},{5,38},{6,39},{32,65},{33,66},{... | collective-permute-start | bytes 1544 | tf_op jit(solution)/shard_map/ppermute | solution.py:450
  52.6 0.0 copy-start.4
  52.7 0.1 own.1.own_ref
  52.8 3.7 %all-to-all-done.got_ref = f32[1664,1,128]{2,1,0:T(1,128)S(1)} async-done(((f32[1664,1,128]{2,1,0:T(1,128)}), f32[1664,1,128]{2,1,0:T(1,128)S(1)}, u32[]{:S(2)}, u32[]{:S(2)}) %all-to-all-start) | async-done | bytes 852000 | tf_op jit(solution)/shard_map/all_to_all | solution.py:511
  56.5 18.0 %pairs.1.contact_ref = f32[384,128]{1,0:T(8,128)S(1)} custom-call(f32[1664,1,128]{2,1,0:T(1,128)S(1)} %all-to-all-done.got_ref, f32[1664,128]{1,0:T(8,128)S(1)} %bitcast.11, bf16[8,128,128]{2,1,0:T(8,128)(2,1)S(1)} %own.1.own_ref, f32[24,1,128]{2,1,0:T(1,128)S(1)} %copy-done.8, s32[32,128]{1,0:T(8,128)S(1)} %bitcast.14), custom_call_target="tpu_custom_call" | custom-call | tf_op jit(solution)/shard_map/pairs/pallas_call | solution.py:546
  74.6 1.0 %update.1 = (f32[3,8,16,128]{3,2,1,0:T(8,128)}, f32[3,8,16,128]{3,2,1,0:T(8,128)}) custom-call(f32[384,128]{1,0:T(8,128)S(1)} %pairs.1.contact_ref, f32[3,8,16,128]{3,2,1,0:T(8,128)S(1)} %get-tuple-element.35.upper_ref, f32[3,8,16,128]{3,2,1,0:T(8,128)S(1)} %get-tuple-element.43.lower_ref, f32[6,9,128]{2,1,0:T(8,128)S(1)} %collective-permute-done.4.from_y_ref, ...), custom_call_target="tpu_custom_call" | custom-call | tf_op jit(solution)/shard_map/update/pallas_call | solution.py:553
  (20 shorter events, 0.1 us)
Async XLA Ops:
  0.6 0.9 %copy-start = (f32[3,8,16,128]{3,2,1,0:T(8,128)S(1)}, f32[3,8,16,128]{3,2,1,0:T(8,128)}, u32[]{:S(2)}) copy-start(f32[3,8,16,128]{3,2,1,0:T(8,128)} %velocity_ref.5) | copy-start | bytes 589828
  2.2 9.6 %collective-permute-start = (f32[48,128]{1,0:T(8,128)}, f32[48,128]{1,0:T(8,128)S(1)}, u32[]{:S(2)}, u32[]{:S(2)}) collective-permute-start(f32[48,128]{1,0:T(8,128)} %get-tuple-element.27), channel_id=1, source_target_pairs={{32,0},{64,32},{96,64},{128,96},{160,128},{192,160},{224,192},{256... | collective-permute-start | bytes 73736 | tf_op jit(solution)/shard_map/ppermute | solution.py:439
  4.1 7.7 %collective-permute-start.2 = (f32[1,384]{1,0:T(1,128)S(1)}, f32[1,384]{1,0:T(1,128)S(1)}, u32[]{:S(2)}, u32[]{:S(2)}) collective-permute-start(f32[1,384]{1,0:T(1,128)S(1)} %get-tuple-element.28), channel_id=1, source_target_pairs={{33,0},{34,1},{35,2},{36,3},{37,4},{38,5},{39,6},{65,32},{66,33},{... | collective-permute-start | bytes 4616 | tf_op jit(solution)/shard_map/ppermute | solution.py:450
  5.4 6.4 %collective-permute-start.1 = (f32[1,384]{1,0:T(1,128)S(1)}, f32[1,384]{1,0:T(1,128)S(1)}, u32[]{:S(2)}, u32[]{:S(2)}) collective-permute-start(f32[1,384]{1,0:T(1,128)S(1)} %get-tuple-element.28), channel_id=1, source_target_pairs={{1,0},{2,1},{3,2},{4,3},{5,4},{6,5},{7,6},{9,8},{10,9},{11,10},{12... | collective-permute-start | bytes 4616 | tf_op jit(solution)/shard_map/ppermute | solution.py:439
  11.8 24.1 %copy-start.1 = (f32[3,8,16,128]{3,2,1,0:T(8,128)S(1)}, f32[3,8,16,128]{3,2,1,0:T(8,128)}, u32[]{:S(2)}) copy-start(f32[3,8,16,128]{3,2,1,0:T(8,128)} %velocity_ref.5) | copy-start | bytes 589828
  11.8 24.1 %copy-start.3 = (f32[6,8,16,128]{3,2,1,0:T(8,128)S(1)}, f32[6,8,16,128]{3,2,1,0:T(8,128)}, u32[]{:S(2)}) copy-start(f32[6,8,16,128]{3,2,1,0:T(8,128)} %stress_ref.1) | copy-start | bytes 1179652
  11.8 24.1 %copy-start.5 = (f32[8,16,128]{2,1,0:T(8,128)S(1)}, f32[8,16,128]{2,1,0:T(8,128)}, u32[]{:S(2)}) copy-start(f32[8,16,128]{2,1,0:T(8,128)} %plastic_ref.1) | copy-start | bytes 196612
  11.8 24.1 %copy-start.6 = (f32[8,16,128]{2,1,0:T(8,128)S(1)}, f32[8,16,128]{2,1,0:T(8,128)}, u32[]{:S(2)}) copy-start(f32[8,16,128]{2,1,0:T(8,128)} %yield_ref.1) | copy-start | bytes 196612
  11.9 44.7 %all-to-all-start = ((f32[1664,1,128]{2,1,0:T(1,128)}), f32[1664,1,128]{2,1,0:T(1,128)S(1)}, u32[]{:S(2)}, u32[]{:S(2)}) async-start(f32[1664,1,128]{2,1,0:T(1,128)} %get-tuple-element.29), calls=%async_computation | async-start | bytes 1703936 | tf_op jit(solution)/shard_map/all_to_all | solution.py:511
  30.2 5.7 %collective-permute-start.3 = (f32[40,128]{1,0:T(8,128)S(1)}, f32[40,128]{1,0:T(8,128)S(1)}, u32[]{:S(2)}, u32[]{:S(2)}) collective-permute-start(f32[40,128]{1,0:T(8,128)S(1)} %edges.1), channel_id=1, source_target_pairs={{8,0},{16,8},{24,16},{9,1},{17,9},{25,17},{10,2},{18,10},{26,18},{... | collective-permute-start | bytes 61448 | tf_op jit(solution)/shard_map/ppermute | solution.py:439
  37.4 5.1 %collective-permute-start.4 = (f32[6,9,128]{2,1,0:T(8,128)S(1)}, f32[6,9,128]{2,1,0:T(8,128)S(1)}, u32[]{:S(2)}, u32[]{:S(2)}) collective-permute-start(f32[6,9,128]{2,1,0:T(8,128)S(1)} %get-tuple-element.37), channel_id=1, source_target_pairs={{0,8},{8,16},{16,24},{1,9},{9,17},{17,25},{2,10},{10,18},{18,26},{... | collective-permute-start | bytes 82952 | tf_op jit(solution)/shard_map/ppermute | solution.py:439
  42.5 10.2 %copy-start.8 = (f32[24,1,128]{2,1,0:T(1,128)S(1)}, f32[24,1,128]{2,1,0:T(1,128)}, u32[]{:S(2)}) copy-start(f32[24,1,128]{2,1,0:T(1,128)} %get-tuple-element.30.cent_ref) | copy-start | bytes 36868
  42.9 31.6 %collective-permute-start.5 = (f32[6,16,128]{2,1,0:T(8,128)S(1)}, f32[6,16,128]{2,1,0:T(8,128)S(1)}, u32[]{:S(2)}, u32[]{:S(2)}) collective-permute-start(f32[6,16,128]{2,1,0:T(8,128)S(1)} %get-tuple-element.38), channel_id=1, source_target_pairs={{0,32},{32,64},{64,96},{96,128},{128,160},{160,192},{192,224},{224... | collective-permute-start | bytes 147464 | tf_op jit(solution)/shard_map/ppermute | solution.py:439
  44.9 29.7 %collective-permute-start.6 = (f32[1,384]{1,0:T(1,128)S(1)}, f32[1,384]{1,0:T(1,128)S(1)}, u32[]{:S(2)}, u32[]{:S(2)}) collective-permute-start(f32[1,384]{1,0:T(1,128)S(1)} %get-tuple-element.39), channel_id=1, source_target_pairs={{0,1},{1,2},{2,3},{3,4},{4,5},{5,6},{6,7},{8,9},{9,10},{10,11},{11... | collective-permute-start | bytes 4616 | tf_op jit(solution)/shard_map/ppermute | solution.py:439
  48.2 26.3 %collective-permute-start.7 = (f32[1,128]{1,0:T(1,128)S(1)}, f32[1,128]{1,0:T(1,128)S(1)}, u32[]{:S(2)}, u32[]{:S(2)}) collective-permute-start(f32[1,128]{1,0:T(1,128)S(1)} %get-tuple-element.40), channel_id=1, source_target_pairs={{0,33},{1,34},{2,35},{3,36},{4,37},{5,38},{6,39},{32,65},{33,66},{... | collective-permute-start | bytes 1544 | tf_op jit(solution)/shard_map/ppermute | solution.py:450
  52.6 3.9 %copy-start.4 = (s32[1,1,1,8,4,128]{5,4,3,2,1,0:T(4,128)S(1)}, s32[1,1,1,8,4,128]{5,4,3,2,1,0:T(4,128)}, u32[]{:S(2)}) copy-start(s32[1,1,1,8,4,128]{5,4,3,2,1,0:T(4,128)} %param.18) | copy-start | bytes 49156
  56.5 18.0 %copy-start.2 = (f32[3,8,16,128]{3,2,1,0:T(8,128)S(1)}, f32[3,8,16,128]{3,2,1,0:T(8,128)}, u32[]{:S(2)}) copy-start(f32[3,8,16,128]{3,2,1,0:T(8,128)} %disp_ref.1) | copy-start | bytes 589828
  56.5 18.0 %copy-start.7 = (f32[8,16,128]{2,1,0:T(8,128)S(1)}, f32[8,16,128]{2,1,0:T(8,128)}, u32[]{:S(2)}) copy-start(f32[8,16,128]{2,1,0:T(8,128)} %mass_ref.1) | copy-start | bytes 196612
